TPU v7x, 32 devices: a whole 2x2x4 slice. The times are simulated.
32 devices in a mesh: wide: 8 (over y, x, core), narrow: 4 (over z).
Axes of the slice: x: 2, y: 2, z: 4, core: 2. Of those that a mesh axis runs over, the one named last changes fastest.
Arguments:
- tokens: bfloat16 [16384, 1024], P(('wide', 'narrow')), may hold values from -6 to 6
- patch_keep: int32 [32, 196], P(('wide', 'narrow')), may hold values 0 or 1
- text_len: int32 [32], P(('wide', 'narrow')), may hold values from 64 to 316, as said below
- buckets: int32 [16384, 512], P(('wide', 'narrow')), may hold values from 0 to 31
- mask_embed: bfloat16 [1024], P(('wide', 'narrow')), may hold values from -6 to 6
- norm_attn: bfloat16 [1024], P(('wide', 'narrow')), may hold values from 0.099609375 to 1.8984375
- w_query: bfloat16 [1024, 1024], P(('wide', 'narrow')), may hold values from -0.046875 to 0.046875
- w_key: bfloat16 [1024, 1024], P(('wide', 'narrow')), may hold values from -0.1875 to 0.1875
- w_value: bfloat16 [1024, 1024], P(('wide', 'narrow')), may hold values from -0.1875 to 0.1875
- w_out: bfloat16 [1024, 1024], P(('wide', 'narrow')), may hold values from -0.5 to 0.5
- bias_table: bfloat16 [512], P(('wide', 'narrow')), may hold values from -5 to 5
- norm_ffn: bfloat16 [1024], P(('wide', 'narrow')), may hold values from 0.099609375 to 1.8984375
- w_gate: bfloat16 [1024, 2816], P(('wide', 'narrow')), may hold values from -0.1875 to 0.1875
- w_up: bfloat16 [1024, 2816], P(('wide', 'narrow')), may hold values from -0.1875 to 0.1875
- w_down: bfloat16 [2816, 1024], P(('wide', 'narrow')), may hold values from -0.109375 to 0.109375
- cotangent: bfloat16 [16384, 1024], P(('wide', 'narrow')), may hold values from -6 to 6
Outputs:
- layer_out: bfloat16 [16384, 1024], P(('wide', 'narrow'))
- input_grad: float32 [16384, 1024], P(('wide', 'narrow'))
- embed_grad: float32 [1024], P(('wide', 'narrow'))
- norm_attn_grad: float32 [1024], P(('wide', 'narrow'))
- query_grad: float32 [1024, 1024], P(('wide', 'narrow'))
- key_grad: float32 [1024, 1024], P(('wide', 'narrow'))
- value_grad: float32 [1024, 1024], P(('wide', 'narrow'))
- out_proj_grad: float32 [1024, 1024], P(('wide', 'narrow'))
- table_grad: float32 [512], P(('wide', 'narrow'))
- norm_ffn_grad: float32 [1024], P(('wide', 'narrow'))
- gate_grad: float32 [1024, 2816], P(('wide', 'narrow'))
- up_grad: float32 [1024, 2816], P(('wide', 'narrow'))
- down_grad: float32 [2816, 1024], P(('wide', 'narrow'))
Inputs may be any that keep to these rules, and one draw needn't show every extreme that they name: `text_len`: live text tokens of a page; some page has all 316.
All inputs are finite; a program needn't handle non-finite values. No bound on the sum of `patch_keep` on one device may be relied on, other than what follows from the above.
Results may differ from a plain program's by a relative error of at most 0.014.
The roundings to bfloat16 on the way count: a program that leaves them out, or rounds other values in their place, can miss the bound.
Values may be sent and summed in bfloat16 or wider, within the bound.
A program may use at most 256 MiB of HBM per device.

v0:
```python
import jax
import jax.numpy as jnp
from jax import lax
from jax.sharding import PartitionSpec as P

HEADS = 16
HEAD = 64
BUCKETS = 32


EPSILON = 1e-06
NEG_FILL = -1000000000.0
CONTRACT_LAST = (((1,), (1,)), ((), ()))
CONTRACT_FIRST = (((0,), (0,)), ((), ()))


def norm_rows(inputs, scale_gain):
    return (
        inputs * lax.rsqrt(jnp.mean(inputs * inputs, axis=-1, keepdims=True) + EPSILON) * scale_gain
    )


def gelu_tanh(inputs):
    return jax.nn.gelu(inputs, approximate=True)


def matmul(left, right):
    return jnp.dot(left, right, preferred_element_type=jnp.float32)


def times_trans(left, right):
    return lax.dot_general(left, right, CONTRACT_LAST, preferred_element_type=jnp.float32)


def trans_times(left, right):
    return lax.dot_general(left, right, CONTRACT_FIRST, preferred_element_type=jnp.float32)


def bucket_table(bucket):
    return (bucket[:, :, None] == jnp.arange(BUCKETS, dtype=jnp.int32)[None, None, :]).astype(
        jnp.bfloat16
    )


def page_scores(query_page, key_page, one_hot, live_keys, table_rows):
    position_bias = jnp.einsum(
        "qkb,bh->hqk", one_hot, table_rows, preferred_element_type=jnp.float32
    )
    scores = (
        jnp.einsum("qhd,khd->hqk", query_page, key_page, preferred_element_type=jnp.float32)
        + position_bias
    )
    return jnp.where(live_keys[None, None, :], scores, NEG_FILL)


def per_device(
    tokens,
    patch_keep,
    text_len,
    buckets,
    mask_embed,
    norm_attn,
    w_query,
    w_key,
    w_value,
    w_out,
    bias_table,
    norm_ffn,
    w_gate,
    w_up,
    w_down,
    cotangent,
):
    page_count, patches = patch_keep.shape
    row_count = tokens.shape[0]
    page_rows = row_count // page_count
    keep_rows = (
        jnp.concatenate(
            [patch_keep, jnp.ones((page_count, page_rows - patches), jnp.int32)], axis=1
        ).reshape(row_count, 1)
        == 1
    )
    live_keys = jnp.arange(page_rows, dtype=jnp.int32)[None, :] < (patches + text_len)[:, None]
    bucket_pages = buckets.reshape(page_count, page_rows, page_rows)

    def shaped(tensor):
        return tensor.reshape(page_count, page_rows, HEADS, HEAD)

    attn_set = (
        lax.all_gather(mask_embed, ("wide", "narrow"), axis=0, tiled=True),
        lax.all_gather(norm_attn, ("wide", "narrow"), axis=0, tiled=True),
        lax.all_gather(w_query, ("wide", "narrow"), axis=0, tiled=True),
        lax.all_gather(w_key, ("wide", "narrow"), axis=0, tiled=True),
        lax.all_gather(w_value, ("wide", "narrow"), axis=0, tiled=True),
        lax.all_gather(w_out, ("wide", "narrow"), axis=0, tiled=True),
        lax.all_gather(bias_table, ("wide", "narrow"), axis=0, tiled=True),
    )
    ffn_set = (
        lax.all_gather(norm_ffn, ("wide", "narrow"), axis=0, tiled=True),
        lax.all_gather(w_gate, ("wide", "narrow"), axis=0, tiled=True),
        lax.all_gather(w_up, ("wide", "narrow"), axis=0, tiled=True),
        lax.all_gather(w_down, ("wide", "narrow"), axis=0, tiled=True),
    )
    embed_all, gain_attn, query_all, key_all, value_all, out_all, table_all = attn_set
    gain_ffn, gate_all, up_all, down_all = ffn_set
    start_rows = jnp.where(
        keep_rows, tokens.astype(jnp.float32), embed_all.astype(jnp.float32)[None, :]
    )
    gain_one = gain_attn.astype(jnp.float32)
    normed = norm_rows(start_rows, gain_one).astype(jnp.bfloat16)
    queries = matmul(normed, query_all).astype(jnp.bfloat16)
    keys_local = matmul(normed, key_all).astype(jnp.bfloat16)
    values = matmul(normed, value_all).astype(jnp.bfloat16)
    table_rows = table_all.reshape(BUCKETS, HEADS)

    def attend_forward(page_items):
        query_page, key_page, value_page, bucket, live_page = page_items
        scores = page_scores(query_page, key_page, bucket_table(bucket), live_page, table_rows)
        row_max = jnp.max(scores, axis=-1, keepdims=True)
        exponent = jnp.exp(scores - row_max)
        row_total = jnp.sum(exponent, axis=-1, keepdims=True)
        attn_prob = (exponent / row_total).astype(jnp.bfloat16)
        mixed_page = jnp.einsum(
            "hqk,khd->qhd", attn_prob, value_page, preferred_element_type=jnp.float32
        )
        return (mixed_page, row_max + jnp.log(row_total))

    mixed_all, log_total = lax.map(
        attend_forward,
        (shaped(queries), shaped(keys_local), shaped(values), bucket_pages, live_keys),
    )
    attended = mixed_all.reshape(row_count, -1).astype(jnp.bfloat16)
    mid_rows = start_rows + matmul(attended, out_all)
    gain_two = gain_ffn.astype(jnp.float32)
    normed_two = norm_rows(mid_rows, gain_two).astype(jnp.bfloat16)
    gate_pre = matmul(normed_two, gate_all)
    up_pre = matmul(normed_two, up_all)
    gelu_val, gelu_back = jax.vjp(gelu_tanh, gate_pre)
    hidden_act = (gelu_val * up_pre).astype(jnp.bfloat16)
    result = (mid_rows + matmul(hidden_act, down_all)).astype(jnp.bfloat16)
    gain_ffn, gate_all, up_all, down_all = (
        lax.all_gather(norm_ffn, ("wide", "narrow"), axis=0, tiled=True),
        lax.all_gather(w_gate, ("wide", "narrow"), axis=0, tiled=True),
        lax.all_gather(w_up, ("wide", "narrow"), axis=0, tiled=True),
        lax.all_gather(w_down, ("wide", "narrow"), axis=0, tiled=True),
    )
    gain_two = gain_ffn.astype(jnp.float32)
    grad_down = trans_times(hidden_act, cotangent)
    grad_act = times_trans(cotangent, down_all)
    grad_gate = gelu_back(grad_act * up_pre)[0].astype(jnp.bfloat16)
    grad_up = (grad_act * gelu_val).astype(jnp.bfloat16)
    grad_gate_w = trans_times(normed_two, grad_gate)
    grad_up_w = trans_times(normed_two, grad_up)
    grad_normed_two = times_trans(grad_gate, gate_all) + times_trans(grad_up, up_all)
    grad_mid_norm, grad_gain_two = jax.vjp(norm_rows, mid_rows, gain_two)[1](grad_normed_two)
    grad_mid = cotangent.astype(jnp.float32) + grad_mid_norm
    wide_count = lax.axis_size("wide")
    narrow_count = lax.axis_size("narrow")

    def split_two(gradient):
        return gradient.reshape(
            (wide_count, narrow_count, gradient.shape[0] // (wide_count * narrow_count))
            + gradient.shape[1:]
        )

    def join_two(gradient):
        return gradient.reshape(gradient.shape[2:])

    sectioned = (
        lax.psum_scatter(split_two(grad_gain_two), "narrow", scatter_dimension=1, tiled=True),
        lax.psum_scatter(split_two(grad_gate_w), "narrow", scatter_dimension=1, tiled=True),
        lax.psum_scatter(split_two(grad_up_w), "narrow", scatter_dimension=1, tiled=True),
        lax.psum_scatter(split_two(grad_down), "narrow", scatter_dimension=1, tiled=True),
    )
    sectioned = (
        lax.psum_scatter(sectioned[0], "wide", scatter_dimension=0, tiled=True),
        lax.psum_scatter(sectioned[1], "wide", scatter_dimension=0, tiled=True),
        lax.psum_scatter(sectioned[2], "wide", scatter_dimension=0, tiled=True),
        lax.psum_scatter(sectioned[3], "wide", scatter_dimension=0, tiled=True),
    )
    ffn_parts = tuple((join_two(member) for member in sectioned))
    embed_all, gain_attn, query_all, key_all, value_all, out_all, table_all = (
        lax.all_gather(mask_embed, ("wide", "narrow"), axis=0, tiled=True),
        lax.all_gather(norm_attn, ("wide", "narrow"), axis=0, tiled=True),
        lax.all_gather(w_query, ("wide", "narrow"), axis=0, tiled=True),
        lax.all_gather(w_key, ("wide", "narrow"), axis=0, tiled=True),
        lax.all_gather(w_value, ("wide", "narrow"), axis=0, tiled=True),
        lax.all_gather(w_out, ("wide", "narrow"), axis=0, tiled=True),
        lax.all_gather(bias_table, ("wide", "narrow"), axis=0, tiled=True),
    )
    gain_one = gain_attn.astype(jnp.float32)
    table_rows = table_all.reshape(BUCKETS, HEADS)
    grad_attn = grad_mid.astype(jnp.bfloat16)
    grad_out_w = trans_times(attended, grad_attn)
    grad_attended = times_trans(grad_attn, out_all).astype(jnp.bfloat16)

    def attend_back(page_items):
        query_page, key_page, value_page, bucket, live_page, total_page, grad_page = page_items
        one_hot = bucket_table(bucket)
        scores = page_scores(query_page, key_page, one_hot, live_page, table_rows)
        attn_prob = jnp.exp(scores - total_page)
        grad_prob = jnp.einsum(
            "qhd,khd->hqk", grad_page, value_page, preferred_element_type=jnp.float32
        )
        row_delta = jnp.sum(grad_prob * attn_prob, axis=-1, keepdims=True)
        grad_scores = (attn_prob * (grad_prob - row_delta)).astype(jnp.bfloat16)
        grad_query = jnp.einsum(
            "hqk,khd->qhd", grad_scores, key_page, preferred_element_type=jnp.float32
        ).astype(jnp.bfloat16)
        grad_key = jnp.einsum(
            "hqk,qhd->khd", grad_scores, query_page, preferred_element_type=jnp.float32
        ).astype(jnp.bfloat16)
        grad_value = jnp.einsum(
            "hqk,qhd->khd",
            attn_prob.astype(jnp.bfloat16),
            grad_page,
            preferred_element_type=jnp.float32,
        ).astype(jnp.bfloat16)
        grad_bias = jnp.einsum(
            "qkb,hqk->bh", one_hot, grad_scores, preferred_element_type=jnp.float32
        )
        return (grad_query, grad_key, grad_value, grad_bias)

    grad_q, grad_k, grad_v, grad_bias = lax.map(
        attend_back,
        (
            shaped(queries),
            shaped(keys_local),
            shaped(values),
            bucket_pages,
            live_keys,
            log_total,
            shaped(grad_attended),
        ),
    )
    grad_q = grad_q.reshape(row_count, -1)
    grad_k = grad_k.reshape(row_count, -1)
    grad_v = grad_v.reshape(row_count, -1)
    grad_table = jnp.sum(grad_bias, axis=0).reshape(-1)
    grad_query_w = trans_times(normed, grad_q)
    grad_key_w = trans_times(normed, grad_k)
    grad_value_w = trans_times(normed, grad_v)
    grad_normed = (
        times_trans(grad_q, query_all)
        + times_trans(grad_k, key_all)
        + times_trans(grad_v, value_all)
    )
    grad_start_norm, grad_gain_one = jax.vjp(norm_rows, start_rows, gain_one)[1](grad_normed)
    grad_start = grad_mid + grad_start_norm
    input_grad = jnp.where(keep_rows, grad_start, 0.0)
    grad_embed = jnp.sum(jnp.where(keep_rows, 0.0, grad_start), axis=0)
    sectioned_attn = (
        lax.psum_scatter(split_two(grad_embed), "narrow", scatter_dimension=1, tiled=True),
        lax.psum_scatter(split_two(grad_gain_one), "narrow", scatter_dimension=1, tiled=True),
        lax.psum_scatter(split_two(grad_query_w), "narrow", scatter_dimension=1, tiled=True),
        lax.psum_scatter(split_two(grad_key_w), "narrow", scatter_dimension=1, tiled=True),
        lax.psum_scatter(split_two(grad_value_w), "narrow", scatter_dimension=1, tiled=True),
        lax.psum_scatter(split_two(grad_out_w), "narrow", scatter_dimension=1, tiled=True),
        lax.psum_scatter(split_two(grad_table), "narrow", scatter_dimension=1, tiled=True),
    )
    sectioned_attn = (
        lax.psum_scatter(sectioned_attn[0], "wide", scatter_dimension=0, tiled=True),
        lax.psum_scatter(sectioned_attn[1], "wide", scatter_dimension=0, tiled=True),
        lax.psum_scatter(sectioned_attn[2], "wide", scatter_dimension=0, tiled=True),
        lax.psum_scatter(sectioned_attn[3], "wide", scatter_dimension=0, tiled=True),
        lax.psum_scatter(sectioned_attn[4], "wide", scatter_dimension=0, tiled=True),
        lax.psum_scatter(sectioned_attn[5], "wide", scatter_dimension=0, tiled=True),
        lax.psum_scatter(sectioned_attn[6], "wide", scatter_dimension=0, tiled=True),
    )
    attn_parts = tuple((join_two(member) for member in sectioned_attn))
    return (
        result,
        input_grad,
        attn_parts[0],
        attn_parts[1],
        attn_parts[2],
        attn_parts[3],
        attn_parts[4],
        attn_parts[5],
        attn_parts[6],
        ffn_parts[0],
        ffn_parts[1],
        ffn_parts[2],
        ffn_parts[3],
    )


def solution(mesh):
    return jax.shard_map(
        per_device,
        mesh=mesh,
        in_specs=(
            P(("wide", "narrow"), None),
            P(("wide", "narrow"), None),
            P(("wide", "narrow")),
            P(("wide", "narrow"), None),
            P(("wide", "narrow")),
            P(("wide", "narrow")),
            P(("wide", "narrow"), None),
            P(("wide", "narrow"), None),
            P(("wide", "narrow"), None),
            P(("wide", "narrow"), None),
            P(("wide", "narrow")),
            P(("wide", "narrow")),
            P(("wide", "narrow"), None),
            P(("wide", "narrow"), None),
            P(("wide", "narrow"), None),
            P(("wide", "narrow"), None),
        ),
        out_specs=(
            P(("wide", "narrow"), None),
            P(("wide", "narrow"), None),
            P(("wide", "narrow")),
            P(("wide", "narrow")),
            P(("wide", "narrow"), None),
            P(("wide", "narrow"), None),
            P(("wide", "narrow"), None),
            P(("wide", "narrow"), None),
            P(("wide", "narrow")),
            P(("wide", "narrow")),
            P(("wide", "narrow"), None),
            P(("wide", "narrow"), None),
            P(("wide", "narrow"), None),
        ),
        check_vma=False,
    )
```

profile of v0, /device:TPU:0, one launch (start us, length us, event | category | flops | bytes accessed | tf_op | source)
XLA Modules:
  0.0 2568.6 jit_solution(6185511055658960123)
XLA Ops:
  16.0 42.2 %all-reduce.23 = (bf16[1024]{0:T(1024)(128)(2,1)S(1)}, bf16[1024]{0:T(1024)(128)(2,1)S(1)}, bf16[512]{0:T(512)(128)(2,1)S(1)}, bf16[1024]{0:T(1024)(128)(2,1)S(1)}) all-reduce(bf16[1024]{0:T(1024)(128)(2,1)S(1)} %dynamic-update-slice.1, bf16[1024]{0:T(1024)(128)(2,1)S(1)} %dynamic-update-slice, ...), channel_id=1, replica_groups=mesh['wide'=8,'narrow'=4] {'wide','narrow'}, use_global_device_ids=true, to_apply=%add.2 | all-reduce | flops 3584 | bytes 14336
  58.3 1.6 copy.96
  59.8 8.7 iota_compare_fusion
  68.5 45.7 %copy.98 = pred[512,512,32]{1,2,0:T(32,128)(4,1)S(1)} copy(pred[512,512,32]{0,2,1:T(32,128)(4,1)} %iota_compare_fusion) | data formatting | bytes 16777216 | tf_op jit(solution)/shard_map/while/body/eval_jaxpr/eq | solution.py:40
  114.3 7.9 fusion.27
  122.2 19.4 copy.99
  142.7 2.9 convolution_convert_fusion.3
  146.1 3.9 convolution_convert_fusion.4
  150.0 1.5 copy.94
  151.5 35.4 %all-gather.8.cloned.1.call-done = bf16[1024,1024]{1,0:T(8,128)(2,1)} async-done(((bf16[32,1024]{1,0:T(8,128)(2,1)}), bf16[1024,1024]{1,0:T(8,128)(2,1)}) %all-gather.8.cloned.1.call-update) | async-done | bytes 2097168 | tf_op jit(solution)/shard_map/all_gather | solution.py:94
  186.9 3.9 convolution_convert_fusion.5
  190.7 1.5 copy.93
  192.3 11.6 fusion.37
  203.8 8.3 fusion
  212.1 8.9 fusion.19
  221.1 24.0 all-gather.14.cloned.1.call-done
  245.0 3.6 multiply_reduce_fusion.5
  248.7 1.4 multiply_convert_fusion.3
  250.1 63.9 %all-gather.18.cloned.1.call-done = bf16[1024,2816]{1,0:T(8,128)(2,1)} async-done(((bf16[32,2816]{1,0:T(8,128)(2,1)}), bf16[1024,2816]{1,0:T(8,128)(2,1)}) %all-gather.18.cloned.1.call-update) | async-done | bytes 5767184 | tf_op jit(solution)/shard_map/all_gather | solution.py:101
  313.9 8.6 fusion.39
  322.5 60.4 %all-gather.16.cloned.1.call-done = bf16[1024,2816]{1,0:T(8,128)(2,1)} async-done(((bf16[32,2816]{1,0:T(8,128)(2,1)}), bf16[1024,2816]{1,0:T(8,128)(2,1)}) %all-gather.16.cloned.1.call-update) | async-done | bytes 5767184 | tf_op jit(solution)/shard_map/all_gather | solution.py:100
  382.9 8.6 fusion.38
  391.5 60.6 %all-gather.20.cloned.1.call-done = bf16[2816,1024]{1,0:T(8,128)(2,1)} async-done(((bf16[88,1024]{1,0:T(8,128)(2,1)}), bf16[2816,1024]{1,0:T(8,128)(2,1)}) %all-gather.20.cloned.1.call-update) | async-done | bytes 5767184 | tf_op jit(solution)/shard_map/all_gather | solution.py:102
  452.1 13.4 multiply_convert_fusion.1
  465.5 6.2 fusion.47
  471.6 6.0 fusion.46
  477.6 3.2 fusion.40
  480.8 4.0 multiply_reduce_fusion.1
  485.5 1.3 copy-done.3
  486.8 1.3 convolution_convert_fusion.2
  489.6 9.7 fusion.20
  499.3 14.8 multiply_reduce_fusion
  514.1 10.5 multiply_convert_fusion
  524.6 6.5 convolution_convert_fusion
  531.2 1.5 convolution_convert_fusion.1
  533.4 3.3 fusion.23
  536.7 6.2 fusion.48
  542.9 1.3 fusion.41
  544.5 1.3 fusion.42
  546.7 2.0 multiply_reduce_fusion.2
  548.8 2.3 select_reduce_fusion
  551.6 4.6 fusion.45
  556.1 3.2 fusion.44
  559.4 3.4 fusion.43
  564.0 1690.7 %all-reduce.26.cloned.1.call-done = (f32[8,4,32,1024]{3,2,1,0:T(8,128)}, f32[8,4,32,1024]{3,2,1,0:T(8,128)}, f32[8,4,32,1024]{3,2,1,0:T(8,128)}, f32[8,4,32,1024...) async-done(((f32[8,4,32,1024]{3,2,1,0:T(8,128)}, f32[8,4,32,1024]{3,2,1,0:T(8,128)}, ...) | async-done | bytes 51380240
  2254.7 3.0 constant_dynamic-slice_fusion.10
  2257.7 3.0 constant_dynamic-slice_fusion.9
  2260.8 3.0 constant_dynamic-slice_fusion.8
  2263.8 3.0 constant_dynamic-slice_fusion.7
  2266.9 4.4 constant_dynamic-slice_fusion.2
  2271.4 4.4 constant_dynamic-slice_fusion
  2275.8 4.3 constant_dynamic-slice_fusion.1
  2281.5 9.3 fusion.4
  2290.9 18.3 all-reduce.21
  2311.2 22.6 all-reduce.20
  2333.8 1.2 fusion.31
  2336.1 1.2 fusion.33
  2338.4 3.1 broadcast_select_fusion
  2341.5 7.7 add_convert_fusion
  2349.3 25.2 reduce-scatter.31.cloned.1.call-done
  2374.5 40.0 %reduce-scatter.33.cloned.1.call-done = f32[1,1,32,1024]{3,2,1,0:T(8,128)} async-done(((f32[8,1,32,1024]{3,2,1,0:T(8,128)}), f32[1,1,32,1024]{3,2,1,0:T(8,128)}) %reduce-scatter.33.cloned.1.call-update) | async-done | bytes 131088 | tf_op jit(solution)/shard_map/reduce_scatter | solution.py:267
  2414.5 49.3 %reduce-scatter.35.cloned.1.call-done = f32[1,1,32,2816]{3,2,1,0:T(8,128)} async-done(((f32[8,1,32,2816]{3,2,1,0:T(8,128)}), f32[1,1,32,2816]{3,2,1,0:T(8,128)}) %reduce-scatter.35.cloned.1.call-update) | async-done | bytes 360464 | tf_op jit(solution)/shard_map/reduce_scatter | solution.py:177
  2463.7 48.7 %reduce-scatter.39.cloned.1.call-done = f32[1,1,88,1024]{3,2,1,0:T(8,128)} async-done(((f32[8,1,88,1024]{3,2,1,0:T(8,128)}), f32[1,1,88,1024]{3,2,1,0:T(8,128)}) %reduce-scatter.39.cloned.1.call-update) | async-done | bytes 360464 | tf_op jit(solution)/shard_map/reduce_scatter | solution.py:179
  2512.5 49.1 %reduce-scatter.37.cloned.1.call-done = f32[1,1,32,2816]{3,2,1,0:T(8,128)} async-done(((f32[8,1,32,2816]{3,2,1,0:T(8,128)}), f32[1,1,32,2816]{3,2,1,0:T(8,128)}) %reduce-scatter.37.cloned.1.call-update) | async-done | bytes 360464 | tf_op jit(solution)/shard_map/reduce_scatter | solution.py:178
  (156 shorter events, 21.8 us)
Async XLA Ops:
  7.2 135.5 %all-gather.12.cloned.1.call-start = ((), (), s32[]{:S(2)}) async-start(), calls=%async_computation.9 | async-start | bytes 2162688 | tf_op jit(solution)/shard_map/all_gather | solution.py:93
  7.9 138.2 %all-gather.10.cloned.1.call-start = ((), (), s32[]{:S(2)}) async-start(), calls=%async_computation.8 | async-start | bytes 2162688 | tf_op jit(solution)/shard_map/all_gather | solution.py:92
  8.7 178.2 %all-gather.8.cloned.1.call-start = ((), (), s32[]{:S(2)}) async-start(), calls=%async_computation.7 | async-start | bytes 2162688 | tf_op jit(solution)/shard_map/all_gather | solution.py:94
  9.4 235.6 %all-gather.14.cloned.1.call-start = ((), (), s32[]{:S(2)}) async-start(), calls=%async_computation.10 | async-start | bytes 2162688 | tf_op jit(solution)/shard_map/all_gather | solution.py:95
  10.0 303.9 %all-gather.18.cloned.1.call-start = ((), (), s32[]{:S(2)}) async-start(), calls=%async_computation.12 | async-start | bytes 5947392 | tf_op jit(solution)/shard_map/all_gather | solution.py:101
  10.6 372.4 %all-gather.16.cloned.1.call-start = ((), (), s32[]{:S(2)}) async-start(), calls=%async_computation.11 | async-start | bytes 5947392 | tf_op jit(solution)/shard_map/all_gather | solution.py:100
  11.1 441.0 %all-gather.20.cloned.1.call-start = ((), (), s32[]{:S(2)}) async-start(), calls=%async_computation.13 | async-start | bytes 5947392 | tf_op jit(solution)/shard_map/all_gather | solution.py:102
  11.9 2242.8 %all-reduce.26.cloned.1.call-start = ((), (), s32[]{:S(2)}) async-start(), calls=%async_computation.21 | async-start | bytes 102760448
  59.8 8.7 copy-start.10
  122.2 19.4 copy-start.29
  122.2 19.5 copy-start.5
  142.1 0.6 copy-start.21
  142.7 44.2 %copy-start.23 = (f32[512]{0:T(512)}, f32[512]{0:T(512)S(1)}, u32[]{:S(2)}) copy-start(f32[512]{0:T(512)S(1)} %fusion.29) | copy-start | bytes 6148
  151.5 40.7 %copy-start.7 = (bf16[512,1024]{0,1:T(8,128)(2,1)}, bf16[512,1024]{0,1:T(8,128)(2,1)S(1)}, u32[]{:S(2)}) copy-start(bf16[512,1024]{0,1:T(8,128)(2,1)S(1)} %copy.94) | copy-start | bytes 3145732
  192.2 19.9 copy-start.12
  248.6 236.2 %copy-start.1 = (f32[512,1024]{1,0:T(8,128)}, f32[512,1024]{1,0:T(8,128)S(1)}, u32[]{:S(2)}) copy-start(f32[512,1024]{1,0:T(8,128)S(1)} %get-tuple-element.111) | copy-start | bytes 6291460
  248.6 240.0 %copy-start.20 = (f32[16,512]{1,0:T(8,128)}, f32[16,512]{1,0:T(8,128)S(1)}, u32[]{:S(2)}) copy-start(f32[16,512]{1,0:T(8,128)S(1)} %log_add_fusion) | copy-start | bytes 98308
  452.1 13.4 copy-start.17
  465.5 12.1 slice-start.6
  471.6 6.0 slice-start.7
  471.6 9.1 slice-start.4
  477.6 3.2 slice-start.5
  480.8 4.1 copy-start.18
  484.9 1.9 copy-start.16
  485.5 1.3 copy-start.3
  488.6 1.0 copy-start.8
  489.6 24.5 slice-start
  489.6 24.5 slice-start.1
  499.3 14.8 slice-start.2
  499.3 14.8 slice-start.3
  524.6 6.5 copy-start
  531.1 13.1 copy-start.14
  531.1 2.0 copy-start.4
  531.1 2.2 copy-start.9
  533.4 3.3 copy-start.19
  533.4 3.3 copy-start.32
  536.7 6.2 copy-start.27
  542.9 1.6 copy-start.26
  544.5 1.3 copy-start.6
  544.5 1.5 copy-start.13
  544.5 1.5 copy-start.24
  544.5 2.2 copy-start.28
  546.7 2.0 copy-start.22
  551.6 4.6 copy-start.15
  562.7 0.7 copy-start.31
  562.7 1786.5 %reduce-scatter.27.cloned.1.call-start = ((), (), s32[]{:S(2)}) async-start(), calls=%async_computation.14 | async-start | bytes 1179648 | tf_op jit(solution)/shard_map/reduce_scatter | solution.py:264
  2257.7 91.6 %reduce-scatter.29.cloned.1.call-start = ((), (), s32[]{:S(2)}) async-start(), calls=%async_computation.15 | async-start | bytes 1179648 | tf_op jit(solution)/shard_map/reduce_scatter | solution.py:265
  2260.7 113.7 %reduce-scatter.31.cloned.1.call-start = ((), (), s32[]{:S(2)}) async-start(), calls=%async_computation.16 | async-start | bytes 1179648 | tf_op jit(solution)/shard_map/reduce_scatter | solution.py:266
  2263.8 150.7 %reduce-scatter.33.cloned.1.call-start = ((), (), s32[]{:S(2)}) async-start(), calls=%async_computation.17 | async-start | bytes 1179648 | tf_op jit(solution)/shard_map/reduce_scatter | solution.py:267
  2266.9 196.9 %reduce-scatter.35.cloned.1.call-start = ((), (), s32[]{:S(2)}) async-start(), calls=%async_computation.18 | async-start | bytes 3244032 | tf_op jit(solution)/shard_map/reduce_scatter | solution.py:177
  2271.3 241.2 %reduce-scatter.39.cloned.1.call-start = ((), (), s32[]{:S(2)}) async-start(), calls=%async_computation.20 | async-start | bytes 3244032 | tf_op jit(solution)/shard_map/reduce_scatter | solution.py:179
  2275.8 285.8 %reduce-scatter.37.cloned.1.call-start = ((), (), s32[]{:S(2)}) async-start(), calls=%async_computation.19 | async-start | bytes 3244032 | tf_op jit(solution)/shard_map/reduce_scatter | solution.py:178
  2280.1 0.7 copy-start.30
  2280.1 1.2 copy-start.25
  2280.1 1.3 copy-start.11
  2290.7 50.8 %copy-start.2 = (f32[512,1024]{1,0:T(8,128)S(1)}, f32[512,1024]{1,0:T(8,128)}, u32[]{:S(2)}) copy-start(f32[512,1024]{1,0:T(8,128)} %copy-done.1) | copy-start | bytes 6291460
Sparse Core Ops, SparseCore 0:
  10.9 59.2 all-gather.11
  73.1 55.4 all-gather.9
  131.5 55.3 all-gather.7
  189.7 55.3 all-gather.13
  247.7 66.1 all-gather.17
  316.6 66.2 all-gather.15
  385.8 66.2 all-gather.19
  562.9 1691.7 all-reduce.25
  2258.8 35.4 reduce-scatter.26
  2298.2 36.1 reduce-scatter.28
  2338.4 36.0 reduce-scatter.30
  2378.4 36.0 reduce-scatter.32
  2418.8 44.8 reduce-scatter.34
  2467.5 44.8 reduce-scatter.38
  2516.7 44.8 reduce-scatter.36
where the time goes:
time: 2580 us; the launch traced here: 2570 us
  waiting for transfers between devices  2150 us (83%)
  matrix products  168 us (7%)
  local copies, waits for them, and re-layouts  114 us (4%)
  blocking collectives  83.1 us (3%)
  other arithmetic  35.4 us (1%)
    unnamed x16, waiting for transfers between devices  1700 us
    unnamed x3, blocking collectives  83.1 us
    all_gather x1, waiting for transfers between devices, per_device(): lax.all_gather(w_up, ('wide', 'narrow'), axis=0, tiled=True)  63.9 us
    all_gather x1, waiting for transfers between devices, per_device(): lax.all_gather(w_down, ('wide', 'narrow'), axis=0, tiled=True)  60.6 us
    all_gather x1, waiting for transfers between devices, per_device(): lax.all_gather(w_gate, ('wide', 'narrow'), axis=0, tiled=True)  60.4 us
  transfers between devices with their start and end apart: 15, of which 11 were waited for; matrix products, arithmetic and copies ran while one was open for 8% of the time, Pallas kernels for 0%

commit v1 on v0

v1 whole, which is shorter than its diff:
```python
import functools

import jax
import jax.numpy as jnp
from jax import lax
from jax.experimental import pallas as pl
from jax.experimental.pallas import tpu as pltpu
from jax.sharding import PartitionSpec as P

MESH = pl.DeviceIdType.MESH
VMEM_LIMIT = 60 << 20


def round_up(value, unit):
    return -(-value // unit) * unit


class Plan:
    def __init__(self, wide, narrow):
        self.wide, self.narrow = wide, narrow
        self.bits = [2 << i for i in range(wide.bit_length() - 2)]
        assert wide == 2 * 2 ** len(self.bits)

    def orders(self, parts):
        return [self.bits, self.bits[::-1]][:parts]


def span(bits):
    out = [0]
    for bit in bits:
        out = out + [member ^ bit for member in out]
    return out


def column_parts(columns):
    if columns < 512:
        return [(0, columns)]
    half = round_up(columns // 2, 128)
    return [(0, half), (half, columns - half)]


def enter(plan):
    w, n = lax.axis_index("wide"), lax.axis_index("narrow")
    barrier = pltpu.get_barrier_semaphore()
    partners = [(w ^ bit, n) for bit in [1] + plan.bits]
    partners += [(w, lax.rem(n + d, plan.narrow)) for d in range(1, plan.narrow)]
    for partner in partners:
        pl.semaphore_signal(barrier, inc=1, device_id=partner, device_id_type=MESH)
    pl.semaphore_wait(barrier, len(partners))
    return w, n


class Gather:
    def __init__(self, plan, shape):
        self.plan = plan
        self.rows, self.columns = shape
        self.padded = round_up(self.rows, 16)
        self.aligned = self.padded == self.rows
        self.group = plan.narrow * self.rows
        self.parts = column_parts(self.columns)
        self.orders = plan.orders(len(self.parts))
        self.chunks = 1 << len(plan.bits)

    def out_shape(self):
        return jax.ShapeDtypeStruct((self.plan.wide, self.group, self.columns), jnp.bfloat16)

    def scratch(self):
        sem = pltpu.SemaphoreType.DMA
        count, parts = self.plan.narrow, len(self.parts)
        base = [sem((2, count)), sem((2, parts, self.chunks)), sem((2, parts, self.chunks)), sem((2,))]
        if not self.aligned:
            base += [
                pltpu.VMEM((count, self.padded, self.columns), jnp.bfloat16),
                pltpu.VMEM((self.group, self.columns), jnp.bfloat16),
            ]
        return base

    def bind(self, place, shard, out, scratch):
        self.w, self.n = place
        self.shard, self.out = shard, out
        self.zsem, self.bsem, self.csem, self.lsem = scratch[:4]
        if not self.aligned:
            self.stage, self.compact = scratch[4:]

    def own_slot(self):
        if self.aligned:
            return self.out.at[self.w, pl.ds(pl.multiple_of(self.n * self.rows, self.rows), self.rows), :]
        return self.stage.at[self.n]

    def z_copy(self, d):
        return pltpu.make_async_remote_copy(
            src_ref=self.shard,
            dst_ref=self.own_slot(),
            send_sem=self.zsem.at[0, d],
            recv_sem=self.zsem.at[1, d],
            device_id=(self.w, lax.rem(self.n + d, self.plan.narrow)),
            device_id_type=MESH,
        )

    def place_copy(self):
        return pltpu.make_async_copy(self.shard, self.own_slot(), self.lsem.at[0])

    def group_copy(self):
        return pltpu.make_async_copy(self.compact, self.out.at[self.w], self.lsem.at[1])

    def start(self):
        for d in range(1, self.plan.narrow):
            self.z_copy(d).start()
        self.place_copy().start()

    def piece(self, ref, part):
        start, size = self.parts[part]
        return ref if size == self.columns else ref.at[:, pl.ds(start, size)]

    def hop(self, sems, part, mask, bit, slot):
        chunk = self.out.at[self.w ^ mask]
        source = self.compact if mask == 0 and not self.aligned else chunk
        return pltpu.make_async_remote_copy(
            src_ref=self.piece(source, part),
            dst_ref=self.piece(chunk, part),
            send_sem=sems.at[0, part, slot],
            recv_sem=sems.at[1, part, slot],
            device_id=(self.w ^ bit, self.n),
            device_id_type=MESH,
        )

    def hops(self, part, stage):
        order = self.orders[part]
        masks = span(order[:stage])
        return [self.hop(self.bsem, part, mask, order[stage], len(masks) + i - 1) for i, mask in enumerate(masks)]

    def core_hops(self, part, stage):
        masks = span(self.orders[part])
        low, high = (0, 1) if stage == 0 else (1 << (stage - 1), 1 << stage)
        return [self.hop(self.csem, part, masks[i], 1, i) for i in range(low, high)]

    def stages(self):
        return len(self.plan.bits) + 2

    def step(self, stage):
        bits, parts = len(self.plan.bits), range(len(self.parts))
        if stage == 0:
            for d in range(1, self.plan.narrow):
                self.z_copy(d).wait_recv()
            self.place_copy().wait()
            if not self.aligned:
                size, wide = self.group, self.plan.narrow * self.padded
                row = lax.broadcasted_iota(jnp.int32, (size, wide), 0)
                column = lax.broadcasted_iota(jnp.int32, (size, wide), 1)
                pick = column == (row // self.rows) * self.padded + row % self.rows
                self.compact[...] = jnp.dot(
                    pick.astype(jnp.bfloat16),
                    self.stage[...].reshape(wide, self.columns),
                    preferred_element_type=jnp.float32,
                ).astype(jnp.bfloat16)
                self.group_copy().start()
        elif stage <= bits:
            for part in parts:
                for copy in self.hops(part, stage - 1):
                    copy.wait_recv()
        else:
            for part in parts:
                for s in range(bits + 1):
                    for copy in self.core_hops(part, s):
                        copy.wait_recv()
            if not self.aligned:
                self.group_copy().wait()
        if stage < bits:
            for part in parts:
                for copy in self.hops(part, stage):
                    copy.start()
        if stage <= bits:
            for part in parts:
                for copy in self.core_hops(part, stage):
                    copy.start()

    def finish(self):
        for d in range(1, self.plan.narrow):
            self.z_copy(d).wait_send()
        for part in range(len(self.parts)):
            for s in range(len(self.plan.bits)):
                for copy in self.hops(part, s):
                    copy.wait_send()
            for s in range(len(self.plan.bits) + 1):
                for copy in self.core_hops(part, s):
                    copy.wait_send()


def split(flat, sizes):
    out, at = [], 0
    for size in sizes:
        out.append(flat[at : at + size])
        at += size
    return out


def gather_kernel(plan, items, *refs):
    count = len(items)
    shards, outs = refs[:count], refs[count : 2 * count]
    scratch = split(refs[2 * count :], [len(item.scratch()) for item in items])
    place = enter(plan)
    for item, shard, out, own in zip(items, shards, outs, scratch):
        item.bind(place, shard, out, own)
    stages = items[0].stages()
    for item in items[:3]:
        item.start()
    for tick in range(count + stages - 1):
        for stage in range(stages):
            k = tick - stage
            if 0 <= k < count:
                items[k].step(stage)
        if tick + 3 < count:
            items[tick + 3].start()
    for item in items:
        item.finish()


def gather_all(plan, shards):
    items = [Gather(plan, shard.shape) for shard in shards]
    padded = [
        shard if item.aligned else jnp.pad(shard, ((0, item.padded - item.rows), (0, 0)))
        for item, shard in zip(items, shards)
    ]
    return pl.pallas_call(
        functools.partial(gather_kernel, plan, items),
        out_shape=[item.out_shape() for item in items],
        in_specs=[pl.BlockSpec(memory_space=pl.ANY)] * len(items),
        out_specs=[pl.BlockSpec(memory_space=pl.ANY)] * len(items),
        scratch_shapes=[piece for item in items for piece in item.scratch()],
        compiler_params=pltpu.CompilerParams(
            collective_id=0, has_side_effects=True, vmem_limit_bytes=VMEM_LIMIT
        ),
    )(*padded)


class Reduce:
    def __init__(self, plan, rows, columns):
        self.plan = plan
        self.rows, self.columns = rows, columns
        self.padded = round_up(rows, 16)
        self.aligned = self.padded == rows
        self.group = plan.narrow * rows
        self.parts = column_parts(columns)
        self.orders = plan.orders(len(self.parts))
        self.chunks = 1 << len(plan.bits)

    def grad_shape(self):
        return jax.ShapeDtypeStruct((self.plan.wide, self.group, self.columns), jnp.bfloat16)

    def out_shape(self):
        return jax.ShapeDtypeStruct((self.rows, self.columns), jnp.float32)

    def scratch(self):
        sem = pltpu.SemaphoreType.DMA
        count, parts = self.plan.narrow, len(self.parts)
        base = [
            sem((2, self.chunks)),
            sem((2, parts, self.chunks)),
            sem((2, count)),
            sem((self.chunks,)),
            pltpu.VMEM((self.chunks, self.group, self.columns), jnp.bfloat16),
            pltpu.VMEM((self.chunks, self.group, self.columns), jnp.bfloat16),
            pltpu.VMEM((self.chunks - 1, self.group, self.columns), jnp.bfloat16),
            pltpu.VMEM((count - 1, self.padded, self.columns), jnp.bfloat16),
        ]
        if not self.aligned:
            base.append(pltpu.VMEM((count, self.padded, self.columns), jnp.bfloat16))
        return base

    def bind(self, place, grad, out, scratch):
        self.w, self.n = place
        self.grad, self.out = grad, out
        self.csem, self.bsem, self.zsem, self.lsem = scratch[:4]
        self.acc, self.crecv, self.brecv, self.zrecv = scratch[4:8]
        if not self.aligned:
            self.stage = scratch[8]

    def core_copy(self, slot):
        return pltpu.make_async_remote_copy(
            src_ref=self.grad.at[self.w ^ 1 ^ (2 * slot)],
            dst_ref=self.crecv.at[slot],
            send_sem=self.csem.at[0, slot],
            recv_sem=self.csem.at[1, slot],
            device_id=(self.w ^ 1, self.n),
            device_id_type=MESH,
        )

    def load_copy(self, slot):
        return pltpu.make_async_copy(self.grad.at[self.w ^ (2 * slot)], self.acc.at[slot], self.lsem.at[slot])

    def piece(self, ref, part):
        start, size = self.parts[part]
        return ref if size == self.columns else ref.at[:, pl.ds(start, size)]

    def hops(self, part, stage):
        order = self.orders[part]
        bit, masks = order[stage], span(order[stage + 1 :])
        base = self.chunks - 2 * len(masks)
        return [
            (
                mask >> 1,
                base + i,
                pltpu.make_async_remote_copy(
                    src_ref=self.piece(self.acc.at[(bit ^ mask) >> 1], part),
                    dst_ref=self.piece(self.brecv.at[base + i], part),
                    send_sem=self.bsem.at[0, part, base + i],
                    recv_sem=self.bsem.at[1, part, base + i],
                    device_id=(self.w ^ bit, self.n),
                    device_id_type=MESH,
                ),
            )
            for i, mask in enumerate(masks)
        ]

    def z_copy(self, d):
        peer = lax.rem(self.n + d, self.plan.narrow)
        if self.aligned:
            source = self.acc.at[0, pl.ds(pl.multiple_of(peer * self.rows, self.rows), self.rows), :]
        else:
            source = self.stage.at[peer]
        return pltpu.make_async_remote_copy(
            src_ref=source,
            dst_ref=self.zrecv.at[d - 1],
            send_sem=self.zsem.at[0, d],
            recv_sem=self.zsem.at[1, d],
            device_id=(self.w, peer),
            device_id_type=MESH,
        )

    def start(self):
        for slot in range(self.chunks):
            self.core_copy(slot).start()
        for slot in range(self.chunks):
            self.load_copy(slot).start()

    def add(self, slot, received, start, size):
        def body(i, carry):
            rows = pl.ds(pl.multiple_of(i * 16, 16), 16)
            self.acc[slot, rows, pl.ds(start, size)] += received[rows, pl.ds(start, size)]
            return carry

        lax.fori_loop(0, self.group // 16, body, 0)

    def stages(self):
        return len(self.plan.bits) + 2

    def step(self, stage):
        bits, parts = len(self.plan.bits), range(len(self.parts))
        if stage == 0:
            for slot in range(self.chunks):
                self.load_copy(slot).wait()
                self.core_copy(slot).wait_recv()
                self.add(slot, self.crecv.at[slot], 0, self.columns)
        elif stage <= bits:
            for part in parts:
                for slot, at, copy in self.hops(part, stage - 1):
                    copy.wait_recv()
                    self.add(slot, self.brecv.at[at], *self.parts[part])
        if stage < bits:
            for part in parts:
                for _, _, copy in self.hops(part, stage):
                    copy.start()
        elif stage == bits:
            if not self.aligned:
                size, wide = self.group, self.plan.narrow * self.padded
                row = lax.broadcasted_iota(jnp.int32, (wide, size), 0)
                column = lax.broadcasted_iota(jnp.int32, (wide, size), 1)
                pick = row == (column // self.rows) * self.padded + column % self.rows
                self.stage[...] = (
                    jnp.dot(pick.astype(jnp.bfloat16), self.acc[0], preferred_element_type=jnp.float32)
                    .astype(jnp.bfloat16)
                    .reshape(self.stage.shape)
                )
            for d in range(1, self.plan.narrow):
                self.z_copy(d).start()
        else:
            if self.aligned:
                total = self.acc[0, pl.ds(pl.multiple_of(self.n * self.rows, self.rows), self.rows), :]
            else:
                total = self.stage[self.n]
            total = total.astype(jnp.float32)
            for d in range(1, self.plan.narrow):
                self.z_copy(d).wait_recv()
                total = total + self.zrecv[d - 1].astype(jnp.float32)
            self.out[...] = total[: self.rows]

    def finish(self):
        for slot in range(self.chunks):
            self.core_copy(slot).wait_send()
        for part in range(len(self.parts)):
            for s in range(len(self.plan.bits)):
                for _, _, copy in self.hops(part, s):
                    copy.wait_send()
        for d in range(1, self.plan.narrow):
            self.z_copy(d).wait_send()


class SumAll:
    def __init__(self, plan, shape):
        self.plan, self.shape = plan, shape
        self.rounds = [(bit, 0) for bit in [1] + plan.bits]
        self.rounds += [(0, 1 << i) for i in range(plan.narrow.bit_length() - 1)]

    def scratch(self):
        sem, count = pltpu.SemaphoreType.DMA, len(self.rounds)
        return [sem((2, count)), pltpu.VMEM((count, *self.shape), jnp.float32), pltpu.VMEM((count, *self.shape), jnp.float32)]

    def bind(self, place, out, scratch):
        self.w, self.n = place
        self.out = out
        self.sem, self.held, self.received = scratch

    def copy(self, turn):
        bit, other = self.rounds[turn]
        return pltpu.make_async_remote_copy(
            src_ref=self.held.at[turn],
            dst_ref=self.received.at[turn],
            send_sem=self.sem.at[0, turn],
            recv_sem=self.sem.at[1, turn],
            device_id=(self.w ^ bit, self.n ^ other),
            device_id_type=MESH,
        )

    def start(self, value):
        self.held[0] = value
        self.copy(0).start()

    def step(self, turn):
        self.copy(turn).wait_recv()
        total = self.held[turn] + self.received[turn]
        if turn + 1 < len(self.rounds):
            self.held[turn + 1] = total
            self.copy(turn + 1).start()
        else:
            self.out[...] = total

    def finish(self):
        for turn in range(len(self.rounds)):
            self.copy(turn).wait_send()


def reduce_kernel(plan, items, small, *refs):
    count = len(items)
    grads, small_in = refs[:count], refs[count]
    outs, small_out = refs[count + 1 : 2 * count + 1], refs[2 * count + 1]
    pieces = split(refs[2 * count + 2 :], [len(item.scratch()) for item in items] + [len(small.scratch())])
    place = enter(plan)
    for item, grad, out, own in zip(items, grads, outs, pieces):
        item.bind(place, grad, out, own)
    small.bind(place, small_out, pieces[-1])
    stages = items[0].stages()
    items[0].start()
    items[1].start()
    small.start(small_in[...])
    for tick in range(count + stages - 1):
        if tick < len(small.rounds):
            small.step(tick)
        for stage in range(stages):
            k = tick - stage
            if 0 <= k < count:
                items[k].step(stage)
        if tick + 2 < count:
            items[tick + 2].start()
    for item in items:
        item.finish()
    small.finish()


def reduce_all(plan, grads, rows, small_value):
    items = [Reduce(plan, r, grad.shape[-1]) for grad, r in zip(grads, rows)]
    small = SumAll(plan, small_value.shape)
    return pl.pallas_call(
        functools.partial(reduce_kernel, plan, items, small),
        out_shape=[item.out_shape() for item in items] + [jax.ShapeDtypeStruct(small_value.shape, jnp.float32)],
        in_specs=[pl.BlockSpec(memory_space=pl.ANY)] * len(items) + [pl.BlockSpec(memory_space=pltpu.VMEM)],
        out_specs=[pl.BlockSpec(memory_space=pltpu.VMEM)] * (len(items) + 1),
        scratch_shapes=[piece for item in items + [small] for piece in item.scratch()],
        compiler_params=pltpu.CompilerParams(
            collective_id=1, has_side_effects=True, vmem_limit_bytes=VMEM_LIMIT
        ),
    )(*[grad.reshape(item.grad_shape().shape) for grad, item in zip(grads, items)], small_value)


HEADS = 16
HEAD = 64
BUCKETS = 32
EPSILON = 1e-06
NEG_FILL = -1000000000.0
LANES = 128


def norm_rows(inputs, scale_gain):
    return (
        inputs * lax.rsqrt(jnp.mean(inputs * inputs, axis=-1, keepdims=True) + EPSILON) * scale_gain
    )


def gelu_tanh(inputs):
    return jax.nn.gelu(inputs, approximate=True)


def matmul(left, right):
    return jnp.dot(left, right, preferred_element_type=jnp.float32)


def times_trans(left, right):
    return lax.dot_general(left, right, (((1,), (1,)), ((), ())), preferred_element_type=jnp.float32)


def trans_times(left, right):
    return lax.dot_general(left, right, (((0,), (0,)), ((), ())), preferred_element_type=jnp.float32)


def bucket_table(bucket):
    return (bucket[:, :, None] == jnp.arange(BUCKETS, dtype=jnp.int32)[None, None, :]).astype(jnp.bfloat16)


def page_scores(query_page, key_page, one_hot, live_keys, table_rows):
    position_bias = jnp.einsum("qkb,bh->hqk", one_hot, table_rows, preferred_element_type=jnp.float32)
    scores = (
        jnp.einsum("qhd,khd->hqk", query_page, key_page, preferred_element_type=jnp.float32)
        + position_bias
    )
    return jnp.where(live_keys[None, None, :], scores, NEG_FILL)


def pack_small(vectors, device):
    rows = []
    for vector in vectors:
        size = vector.shape[0]
        rows.append(
            lax.dynamic_update_slice(
                jnp.zeros((LANES,), vector.dtype), vector, (lax.rem(device * size, LANES),)
            )
        )
    rows += [jnp.zeros((LANES,), vectors[0].dtype)] * (16 - len(rows))
    return jnp.stack(rows)


def unpack_small(gathered, sizes):
    out = []
    for i, size in enumerate(sizes):
        blocks = gathered[:, i, :].astype(jnp.float32).reshape(-1, LANES // size, LANES)
        out.append(jnp.sum(blocks, axis=1).reshape(-1))
    return out


def per_device(
    plan,
    tokens,
    patch_keep,
    text_len,
    buckets,
    mask_embed,
    norm_attn,
    w_query,
    w_key,
    w_value,
    w_out,
    bias_table,
    norm_ffn,
    w_gate,
    w_up,
    w_down,
    cotangent,
):
    page_count, patches = patch_keep.shape
    row_count = tokens.shape[0]
    page_rows = row_count // page_count
    device = lax.axis_index("wide") * plan.narrow + lax.axis_index("narrow")
    keep_rows = (
        jnp.concatenate(
            [patch_keep, jnp.ones((page_count, page_rows - patches), jnp.int32)], axis=1
        ).reshape(row_count, 1)
        == 1
    )
    live_keys = jnp.arange(page_rows, dtype=jnp.int32)[None, :] < (patches + text_len)[:, None]
    bucket_pages = buckets.reshape(page_count, page_rows, page_rows)

    def shaped(tensor):
        return tensor.reshape(page_count, page_rows, HEADS, HEAD)

    small_set = (mask_embed, norm_attn, norm_ffn, bias_table)
    gathered = gather_all(
        plan, (pack_small(small_set, device), w_query, w_key, w_value, w_out, w_gate, w_up, w_down)
    )
    embed_all, gain_one, gain_two, table_all = unpack_small(
        gathered[0].reshape(-1, 16, LANES), [member.shape[0] for member in small_set]
    )
    query_all, key_all, value_all, out_all, gate_all, up_all, down_all = (
        member.reshape(-1, member.shape[-1]) for member in gathered[1:]
    )
    start_rows = jnp.where(keep_rows, tokens.astype(jnp.float32), embed_all[None, :])
    normed = norm_rows(start_rows, gain_one).astype(jnp.bfloat16)
    queries = matmul(normed, query_all).astype(jnp.bfloat16)
    keys_local = matmul(normed, key_all).astype(jnp.bfloat16)
    values = matmul(normed, value_all).astype(jnp.bfloat16)
    table_rows = table_all.astype(jnp.bfloat16).reshape(BUCKETS, HEADS)

    def attend_forward(page_items):
        query_page, key_page, value_page, bucket, live_page = page_items
        scores = page_scores(query_page, key_page, bucket_table(bucket), live_page, table_rows)
        row_max = jnp.max(scores, axis=-1, keepdims=True)
        exponent = jnp.exp(scores - row_max)
        row_total = jnp.sum(exponent, axis=-1, keepdims=True)
        attn_prob = (exponent / row_total).astype(jnp.bfloat16)
        mixed_page = jnp.einsum(
            "hqk,khd->qhd", attn_prob, value_page, preferred_element_type=jnp.float32
        )
        return (mixed_page, row_max + jnp.log(row_total))

    mixed_all, log_total = lax.map(
        attend_forward,
        (shaped(queries), shaped(keys_local), shaped(values), bucket_pages, live_keys),
    )
    attended = mixed_all.reshape(row_count, -1).astype(jnp.bfloat16)
    mid_rows = start_rows + matmul(attended, out_all)
    normed_two = norm_rows(mid_rows, gain_two).astype(jnp.bfloat16)
    gate_pre = matmul(normed_two, gate_all)
    up_pre = matmul(normed_two, up_all)
    gelu_val, gelu_back = jax.vjp(gelu_tanh, gate_pre)
    hidden_act = (gelu_val * up_pre).astype(jnp.bfloat16)
    result = (mid_rows + matmul(hidden_act, down_all)).astype(jnp.bfloat16)
    grad_down = trans_times(hidden_act, cotangent).astype(jnp.bfloat16)
    grad_act = times_trans(cotangent, down_all)
    grad_gate = gelu_back(grad_act * up_pre)[0].astype(jnp.bfloat16)
    grad_up = (grad_act * gelu_val).astype(jnp.bfloat16)
    grad_gate_w = trans_times(normed_two, grad_gate).astype(jnp.bfloat16)
    grad_up_w = trans_times(normed_two, grad_up).astype(jnp.bfloat16)
    grad_normed_two = times_trans(grad_gate, gate_all) + times_trans(grad_up, up_all)
    grad_mid_norm, grad_gain_two = jax.vjp(norm_rows, mid_rows, gain_two)[1](grad_normed_two)
    grad_mid = cotangent.astype(jnp.float32) + grad_mid_norm
    grad_attn = grad_mid.astype(jnp.bfloat16)
    grad_out_w = trans_times(attended, grad_attn).astype(jnp.bfloat16)
    grad_attended = times_trans(grad_attn, out_all).astype(jnp.bfloat16)

    def attend_back(page_items):
        query_page, key_page, value_page, bucket, live_page, total_page, grad_page = page_items
        one_hot = bucket_table(bucket)
        scores = page_scores(query_page, key_page, one_hot, live_page, table_rows)
        attn_prob = jnp.exp(scores - total_page)
        grad_prob = jnp.einsum(
            "qhd,khd->hqk", grad_page, value_page, preferred_element_type=jnp.float32
        )
        row_delta = jnp.sum(grad_prob * attn_prob, axis=-1, keepdims=True)
        grad_scores = (attn_prob * (grad_prob - row_delta)).astype(jnp.bfloat16)
        grad_query = jnp.einsum(
            "hqk,khd->qhd", grad_scores, key_page, preferred_element_type=jnp.float32
        ).astype(jnp.bfloat16)
        grad_key = jnp.einsum(
            "hqk,qhd->khd", grad_scores, query_page, preferred_element_type=jnp.float32
        ).astype(jnp.bfloat16)
        grad_value = jnp.einsum(
            "hqk,qhd->khd",
            attn_prob.astype(jnp.bfloat16),
            grad_page,
            preferred_element_type=jnp.float32,
        ).astype(jnp.bfloat16)
        grad_bias = jnp.einsum(
            "qkb,hqk->bh", one_hot, grad_scores, preferred_element_type=jnp.float32
        )
        return (grad_query, grad_key, grad_value, grad_bias)

    grad_q, grad_k, grad_v, grad_bias = lax.map(
        attend_back,
        (
            shaped(queries),
            shaped(keys_local),
            shaped(values),
            bucket_pages,
            live_keys,
            log_total,
            shaped(grad_attended),
        ),
    )
    grad_q = grad_q.reshape(row_count, -1)
    grad_k = grad_k.reshape(row_count, -1)
    grad_v = grad_v.reshape(row_count, -1)
    grad_table = jnp.sum(grad_bias, axis=0).reshape(-1)
    grad_query_w = trans_times(normed, grad_q).astype(jnp.bfloat16)
    grad_key_w = trans_times(normed, grad_k).astype(jnp.bfloat16)
    grad_value_w = trans_times(normed, grad_v).astype(jnp.bfloat16)
    grad_normed = (
        times_trans(grad_q, query_all)
        + times_trans(grad_k, key_all)
        + times_trans(grad_v, value_all)
    )
    grad_start_norm, grad_gain_one = jax.vjp(norm_rows, start_rows, gain_one)[1](grad_normed)
    grad_start = grad_mid + grad_start_norm
    input_grad = jnp.where(keep_rows, grad_start, 0.0)
    grad_embed = jnp.sum(jnp.where(keep_rows, 0.0, grad_start), axis=0)
    width = grad_embed.shape[0]
    small_grads = jnp.stack(
        [grad_embed, grad_gain_one, grad_gain_two, jnp.pad(grad_table, (0, width - grad_table.shape[0]))]
        + [jnp.zeros((width,), jnp.float32)] * 4
    )
    weight_rows = [w.shape[0] for w in (w_down, w_gate, w_up, w_out, w_query, w_key, w_value)]
    down_part, gate_part, up_part, out_part, query_part, key_part, value_part, small_sums = reduce_all(
        plan,
        (grad_down, grad_gate_w, grad_up_w, grad_out_w, grad_query_w, grad_key_w, grad_value_w),
        weight_rows,
        small_grads,
    )

    def own(row, size):
        return lax.dynamic_slice(small_sums[row], (device * size,), (size,))

    return (
        result,
        input_grad,
        own(0, mask_embed.shape[0]),
        own(1, norm_attn.shape[0]),
        query_part,
        key_part,
        value_part,
        out_part,
        own(3, bias_table.shape[0]),
        own(2, norm_ffn.shape[0]),
        gate_part,
        up_part,
        down_part,
    )


def solution(mesh):
    rows, flat = P(("wide", "narrow"), None), P(("wide", "narrow"))
    plan = Plan(mesh.shape["wide"], mesh.shape["narrow"])
    return jax.shard_map(
        functools.partial(per_device, plan),
        mesh=mesh,
        in_specs=(rows, rows, flat, rows, flat, flat, rows, rows, rows, rows, flat, flat, rows, rows, rows, rows),
        out_specs=(rows, rows, flat, flat, rows, rows, rows, rows, flat, flat, rows, rows, rows),
        check_vma=False,
    )
```

time: 2580 us -> 567 us (0.22)
  waiting for transfers between devices: 2150 us -> 0 us
  Pallas kernels: 0 us -> 275 us
  blocking collectives: 83.1 us -> 0 us
    unnamed x16 -> x0, waiting for transfers between devices: 1700 us -> none
    pallas_call x0 -> x2, Pallas kernels: none -> 275 us  [the longest x1 140 us: reduce_all(): pl.pallas_call(functools.partial(reduce_kernel, plan, items, small), out_...]
    all_gather x7 -> x0, waiting for transfers between devices: 244 us -> none  [the longest x1 63.9 us: per_device(): lax.all_gather(w_up, ('wide', 'narrow'), axis=0, tiled=True)]
    reduce_scatter x7 -> x0, waiting for transfers between devices: 212 us -> none  [the longest x1 49.3 us: per_device(): lax.psum_scatter(sectioned[1], 'wide', scatter_dimension=0, tiled=True)]
    unnamed x3 -> x0, blocking collectives: 83.1 us -> none
  transfers between devices with their start and end apart: 15 -> 0, of which waited for: 11 -> 0; matrix products, arithmetic and copies ran while one was open for 8% -> 0% of each run, Pallas kernels for 0% -> 0%
where the time goes in v1:
time: 567 us; the launch traced here: 558 us
  Pallas kernels  275 us (49%)
  matrix products  151 us (27%)
  local copies, waits for them, and re-layouts  98.3 us (17%)
  other arithmetic  31.1 us (5%)
    pallas_call x1, Pallas kernels, reduce_all(): pl.pallas_call(functools.partial(reduce_kernel, plan, items, small), out_...  140 us
    pallas_call x1, Pallas kernels, gather_all(): pl.pallas_call(functools.partial(gather_kernel, plan, items), out_shape=[...  135 us
    eq x1, local copies, waits for them, and re-layouts, bucket_table(): bucket[:, :, None] == jnp.arange(BUCKETS, dtype=jnp.int32)[None, None, :]  46.2 us
    dot_general x7, matrix products, matmul(): return jnp.dot(left, right, preferred_element_type=jnp.float32)  31.5 us
    dot_general x7, matrix products, trans_times(): lax.dot_general(left, right, (((0,), (0,)), ((), ())), preferred_element_...  26.6 us
    dot_general x7, matrix products, times_trans(): lax.dot_general(left, right, (((1,), (1,)), ((), ())), preferred_element_...  25.2 us
    dot_general x1, local copies, waits for them, and re-layouts, page_scores(): jnp.einsum('qkb,bh->hqk', one_hot, table_rows, preferred_element_type=jnp...  19.4 us
    unnamed x106, local copies, waits for them, and re-layouts  19 us

profile of v1, /device:TPU:0, one launch (start us, length us, event | category | flops | bytes accessed | tf_op | source)
XLA Modules:
  0.0 557.8 jit_solution(10179977615558475922)
XLA Ops:
  0.7 0.8 dynamic_update_slice.32
  1.5 0.8 dynamic_update_slice.33
  2.3 0.8 dynamic_update_slice.34
  3.1 0.8 dynamic_update_slice.35
  3.9 1.2 stack.44.refs_0_
  5.1 1.6 pad.9.refs_7_
  6.7 135.4 %shard_map.255 = (bf16[8,64,128]{2,1,0:T(8,128)(2,1)}, bf16[8,128,1024]{2,1,0:T(8,128)(2,1)}, bf16[8,128,1024]{2,1,0:T(8,128)(2,1)}, bf16[8,128,1024]{2,1,0:T(8,...) custom-call(bf16[16,128]{1,0:T(8,128)(2,1)} %stack.44.refs_0_, ...), custom_call_target="tpu_custom_call" | custom-call | tf_op jit(solution)/shard_map/pallas_call | solution.py:224
  142.1 1.7 slice_convert_fusion
  143.8 0.7 compare_reduce_fusion
  145.0 2.9 convolution_convert_fusion.12
  148.0 1.3 copy.46
  149.7 8.7 %iota_compare_fusion = pred[512,512,32]{0,2,1:T(32,128)(4,1)} fusion(s32[512,512]{0,1:T(8,128)S(1)} %copy.50), kind=kLoop, calls=%fused_computation | loop fusion | flops 8388608 | bytes 9437184 | tf_op jit(solution)/shard_map/while/body/eval_jaxpr/eq | solution.py:515
  158.3 46.2 %copy.52 = pred[512,512,32]{1,2,0:T(32,128)(4,1)} copy(pred[512,512,32]{0,2,1:T(32,128)(4,1)} %iota_compare_fusion) | data formatting | bytes 16777216 | tf_op jit(solution)/shard_map/while/body/eval_jaxpr/eq | solution.py:515
  204.6 10.1 %fusion.30 = f32[16,512,512]{2,0,1:T(8,128)} fusion(pred[512,512,32]{1,2,0:T(32,128)(4,1)} %copy.52, bf16[32,16]{1,0:T(8,128)(2,1)S(1)} %convert_element_type.175), kind=kOutput, calls=%fused_computation.72 | convolution fusion | flops 268435456 | bytes 25166848 | tf_op jit(solution)/shard_map/while/body/eval_jaxpr/qkb,bh->hqk/dot_general | solution.py:519
  214.7 19.4 %copy.53 = f32[16,512,512]{1,2,0:T(8,128)} copy(f32[16,512,512]{2,0,1:T(8,128)} %fusion.30) | data formatting | bytes 33554432 | tf_op jit(solution)/shard_map/while/body/eval_jaxpr/qkb,bh->hqk/dot_general | solution.py:519
  234.1 2.9 convolution_convert_fusion.11
  237.6 4.2 convolution_convert_fusion.10
  241.8 1.5 copy.48
  244.0 11.6 %fusion.40 = (f32[16,512]{1,0:T(8,128)S(1)}, f32[16,512,512]{1,2,0:T(8,128)}) fusion(f32[16,512,512]{1,2,0:T(8,128)} %copy.53, bf16[512,16,64]{0,2,1:T(8,128)(2,1)S(1)} %bitcast.119, bf16[512,16,64]{0,2,1:T(8,128)(2,1)S(1)} %bitcast.117, pred[512]{0:T(512)(128)(4,1)S(1)} %iota_compare_fusion.1), kind=kOutput, calls=%fused_computation.91 | convolution fusion | flops 549445632 | bytes 35684864 | tf_op jit(solution)/shard_map/while/body/eval_jaxpr/qhd,khd->hqk/dot_general | solution.py:521
  255.6 8.4 %fusion = f32[16,512]{1,0:T(8,128)S(1)} fusion(f32[16,512,512]{1,2,0:T(8,128)} %get-tuple-element.129, f32[16,512]{1,0:T(8,128)S(1)} %get-tuple-element.128), kind=kLoop, calls=%fused_computation.7 | loop fusion | flops 8380416 | bytes 16842752 | tf_op jit(solution)/shard_map/while/body/eval_jaxpr/reduce_sum | solution.py:605
  264.0 7.7 %fusion.20 = bf16[16,64,512]{2,1,0:T(8,128)(2,1)S(1)} fusion(bf16[512,16,64]{0,2,1:T(8,128)(2,1)S(1)} %bitcast.127, f32[16,512,512]{1,2,0:T(8,128)} %get-tuple-element.129, f32[16,512]{1,0:T(8,128)S(1)} %fusion, f32[16,512]{1,0:T(8,128)S(1)} %get-tuple-element.128), kind=kOutput, calls=%fused_computation.54 | convolution fusion | flops 549978112 | bytes 18939904 | tf_op jit(solution)/shard_map/while/body/eval_jaxpr/hqk,khd->qhd/dot_general | solution.py:607
  271.7 1.4 multiply_reduce_fusion.5
  273.5 8.1 %fusion.41 = f32[512,2816]{1,0:T(8,128)} fusion(bf16[512,1024]{1,0:T(8,128)(2,1)S(1)} %multiply_convert_fusion.2, bf16[1024,2816]{1,0:T(8,128)(2,1)} %bitcast.179), kind=kOutput, calls=%fused_computation.92 | convolution fusion | flops 2952790016 | bytes 12582912 | tf_op jit(solution)/shard_map/dot_general | solution.py:503
  281.7 5.0 fusion.42
  286.7 12.0 %fusion.15 = (bf16[512,2816]{1,0:T(8,128)(2,1)S(1)}, bf16[512,2816]{1,0:T(8,128)(2,1)}, bf16[512,2816]{1,0:T(8,128)(2,1)}) fusion(f32[512,2816]{1,0:T(8,128)} %fusion.41, f32[512,2816]{1,0:T(8,128)} %fusion.42, bf16[2816,1024]{1,0:T(8,128)(2,1)S(1)} %bitcast.185, bf16[512,1024]{1,0:T(8,128)(2,1)S(1)} %copy-done.21), kind=kOutput, calls=%fused_computation.25 | convolution fusion | flops 2990276608 | bytes 27000832 | tf_op jit(solution)/shard_map/dot_general | solution.py:507
  298.7 7.0 %add_convert_fusion = bf16[512,1024]{1,0:T(8,128)(2,1)} fusion(f32[512,1024]{1,0:T(8,128)S(1)} %get-tuple-element.131, bf16[512,2816]{1,0:T(8,128)(2,1)} %get-tuple-element.119, bf16[2816,1024]{1,0:T(8,128)(2,1)S(1)} %bitcast.186), kind=kOutput, calls=%fused_computation.41 | convolution fusion | flops 2953838592 | bytes 11796480 | tf_op jit(solution)/shard_map/dot_general | solution.py:503
  305.7 3.2 fusion.43
  308.9 3.9 multiply_reduce_fusion.1
  313.5 1.3 copy-done.8
  314.8 1.3 convolution_convert_fusion.9
  316.1 0.9 copy.56
  317.1 9.8 %fusion.21 = bf16[16,64,512]{2,1,0:T(8,128)(2,1)} fusion(bf16[512,16,64]{0,2,1:T(8,128)(2,1)S(1)} %bitcast.121, f32[16,512,512]{1,2,0:T(8,128)} %get-tuple-element.129, f32[16,512]{1,0:T(8,128)S(1)} %log_add_fusion), kind=kOutput, calls=%fused_computation.61 | convolution fusion | flops 545783808 | bytes 18907136 | tf_op jit(solution)/shard_map/while/body/eval_jaxpr/hqk,qhd->khd/dot_general | solution.py:653
  326.9 16.6 %multiply_reduce_fusion = (f32[16,512]{1,0:T(8,128)}, f32[16,512,512]{1,2,0:T(8,128)}) fusion(f32[16,512,512]{1,2,0:T(8,128)} %get-tuple-element.129, f32[16,512]{1,0:T(8,128)} %copy-done.23, bf16[512,16,64]{0,2,1:T(8,128)(2,1)} %bitcast.122, bf16[512,16,64]{0,2,1:T(8,128)(2,1)} %bitcast.126), kind=kOutput, calls=%fused_computation.2 | convolution fusion | flops 549445632 | bytes 35717120 | tf_op jit(solution)/shard_map/while/body/eval_jaxpr/qhd,khd->hqk/dot_general | solution.py:642
  343.5 8.0 %multiply_convert_fusion = bf16[16,512,512]{1,2,0:T(8,128)(2,1)S(1)} fusion(f32[16,512,512]{1,2,0:T(8,128)} %get-tuple-element.134, f32[16,512,512]{1,2,0:T(8,128)S(1)} %bitcast.116, f32[16,512]{1,0:T(8,128)} %get-tuple-element.133, f32[16,512]{1,0:T(8,128)} %copy-done.23), kind=kLoop, calls=%fused_computation.1 | loop fusion | flops 16777216 | bytes 42008576 | tf_op jit(solution)/shard_map/while/body/eval_jaxpr/convert_element_type | solution.py:646
  351.5 1.5 convolution_convert_fusion.8
  353.0 2.1 copy-done
  355.0 1.3 fusion.44
  356.3 2.1 copy-done.1
  358.6 2.6 convolution_convert_fusion.7
  361.3 1.3 fusion.45
  362.8 0.7 copy-done.31
  363.5 2.1 multiply_reduce_fusion.2
  365.7 0.8 select_reduce_fusion
  366.5 1.5 broadcast_select_fusion
  368.0 1.3 copy-done.36
  369.4 5.0 convolution_convert_fusion.2
  374.4 5.0 convolution_convert_fusion.1
  379.5 5.2 convolution_convert_fusion
  384.6 2.6 convolution_convert_fusion.6
  387.3 2.9 convolution_convert_fusion.5
  390.2 2.9 convolution_convert_fusion.4
  393.1 2.9 convolution_convert_fusion.3
  396.0 7.6 %fusion.24 = f32[32,16]{1,0:T(8,128)S(1)} fusion(bf16[16,512,512]{1,2,0:T(8,128)(2,1)S(1)} %copy-done.1, s32[512,512]{0,1:T(8,128)S(1)} %copy-done.11), kind=kOutput, calls=%fused_computation.62 | convolution fusion | flops 276824064 | bytes 9439232 | tf_op jit(solution)/shard_map/while/body/eval_jaxpr/qkb,hqk->bh/dot_general | solution.py:659
  403.7 0.7 stack.48.refs_7_
  404.3 140.0 %shard_map.256 = (f32[88,1024]{1,0:T(8,128)}, f32[32,2816]{1,0:T(8,128)}, f32[32,2816]{1,0:T(8,128)}, f32[32,1024]{1,0:T(8,128)}, f32[32,1024]{1,0:T(8,128)}, /*...) custom-call(bf16[8,352,1024]{2,1,0:T(8,128)(2,1)} %bitcast.123, bf16[8,128,2816]{2,1,0:T(8,128)(2,1)} %bitcast.124, ...), custom_call_target="tpu_custom_call" | custom-call | tf_op jit(solution)/shard_map/pallas_call | solution.py:472
  544.4 0.9 fusion.39
  545.3 0.6 fusion.34
  547.1 1.6 copy.94
  548.7 1.6 copy.95
  550.2 1.6 copy.96
  551.8 1.6 copy.97
  553.4 1.7 copy.98
  555.1 1.7 copy.99
  556.9 0.7 copy.100
  (124 shorter events, 4.2 us)
Async XLA Ops:
  0.6 143.9 %copy-start.5 = (bf16[512,1024]{1,0:T(8,128)(2,1)S(1)}, bf16[512,1024]{1,0:T(8,128)(2,1)}, u32[]{:S(2)}) copy-start(bf16[512,1024]{1,0:T(8,128)(2,1)} %param.16) | copy-start | bytes 3145732
  145.0 2.9 copy-start.26
  145.0 92.5 %copy-start.28 = (f32[512]{0:T(512)}, f32[512]{0:T(512)S(1)}, u32[]{:S(2)}) copy-start(f32[512]{0:T(512)S(1)} %fusion.32) | copy-start | bytes 6148
  147.9 1.4 copy-start.18
  149.6 8.7 %copy-start.10 = (s32[512,512]{0,1:T(8,128)}, s32[512,512]{0,1:T(8,128)S(1)}, u32[]{:S(2)}) copy-start(s32[512,512]{0,1:T(8,128)S(1)} %copy.50) | copy-start | bytes 3145732
  237.6 6.4 %copy-start.2 = (bf16[512,1024]{0,1:T(8,128)(2,1)}, bf16[512,1024]{0,1:T(8,128)(2,1)S(1)}, u32[]{:S(2)}) copy-start(bf16[512,1024]{0,1:T(8,128)(2,1)S(1)} %copy.47) | copy-start | bytes 3145732
  255.6 8.4 %copy-start.12 = (bf16[512,1024]{0,1:T(8,128)(2,1)S(1)}, bf16[512,1024]{0,1:T(8,128)(2,1)}, u32[]{:S(2)}) copy-start(bf16[512,1024]{0,1:T(8,128)(2,1)} %copy.46) | copy-start | bytes 3145732
  264.0 7.7 %copy-start.6 = (bf16[512,1024]{1,0:T(8,128)(2,1)S(1)}, bf16[512,1024]{1,0:T(8,128)(2,1)}, u32[]{:S(2)}) copy-start(bf16[512,1024]{1,0:T(8,128)(2,1)} %param.16) | copy-start | bytes 3145732
  264.0 7.7 %copy-start.13 = (bf16[8,128,1024]{2,1,0:T(8,128)(2,1)S(1)}, bf16[8,128,1024]{2,1,0:T(8,128)(2,1)}, u32[]{:S(2)}) copy-start(bf16[8,128,1024]{2,1,0:T(8,128)(2,1)} %get-tuple-element.99) | copy-start | bytes 6291460
  271.7 1.5 copy-start.15
  271.7 1.4 copy-start.25
  273.2 8.4 %slice-start.4 = ((s8[5767168]{0:T(1024)(128)(4,1)}), s8[4194304]{0:T(1024)(128)(4,1)S(1)}, s32[]{:S(2)}) async-start(s8[5767168]{0:T(1024)(128)(4,1)} %bitcast.175), calls=%async_computation.4 | async-start | bytes 8388608
  273.4 8.2 %copy-start.19 = (bf16[512,1024]{1,0:T(8,128)(2,1)}, bf16[512,1024]{1,0:T(8,128)(2,1)S(1)}, u32[]{:S(2)}) copy-start(bf16[512,1024]{1,0:T(8,128)(2,1)S(1)} %multiply_convert_fusion.2) | copy-start | bytes 3145732
  273.4 8.2 %slice-start.5 = ((s8[5767168]{0:T(1024)(128)(4,1)}), s8[1572864]{0:T(1024)(128)(4,1)S(1)}, s32[]{:S(2)}) async-start(s8[5767168]{0:T(1024)(128)(4,1)} %bitcast.175), calls=%async_computation.5 | async-start | bytes 3145728
  273.5 13.2 %slice-start.8 = ((s8[5767168]{0:T(1024)(128)(4,1)}), s8[4194304]{0:T(1024)(128)(4,1)S(1)}, s32[]{:S(2)}) async-start(s8[5767168]{0:T(1024)(128)(4,1)} %bitcast.183), calls=%async_computation.8 | async-start | bytes 8388608
  281.6 5.0 copy-start.21
  281.7 5.0 slice-start.9
  281.7 24.1 %slice-start.6 = ((s8[5767168]{0:T(1024)(128)(4,1)}), s8[4194304]{0:T(1024)(128)(4,1)S(1)}, s32[]{:S(2)}) async-start(s8[5767168]{0:T(1024)(128)(4,1)} %bitcast.180), calls=%async_computation.6 | async-start | bytes 8388608
  286.6 19.1 %slice-start.7 = ((s8[5767168]{0:T(1024)(128)(4,1)}), s8[1572864]{0:T(1024)(128)(4,1)S(1)}, s32[]{:S(2)}) async-start(s8[5767168]{0:T(1024)(128)(4,1)} %bitcast.180), calls=%async_computation.7 | async-start | bytes 3145728
  298.7 10.2 %copy-start.34 = (bf16[512,2816]{1,0:T(8,128)(2,1)}, bf16[512,2816]{1,0:T(8,128)(2,1)S(1)}, u32[]{:S(2)}) copy-start(bf16[512,2816]{1,0:T(8,128)(2,1)S(1)} %get-tuple-element.117) | copy-start | bytes 8650756
  298.7 7.0 %copy-start.37 = (bf16[512,2816]{1,0:T(8,128)(2,1)S(1)}, bf16[512,2816]{1,0:T(8,128)(2,1)}, u32[]{:S(2)}) copy-start(bf16[512,2816]{1,0:T(8,128)(2,1)} %get-tuple-element.118) | copy-start | bytes 8650756
  312.9 1.9 copy-start.14
  313.4 1.3 copy-start.8
  317.0 9.8 %copy-start.4 = (bf16[512,1024]{0,1:T(8,128)(2,1)}, bf16[512,1024]{0,1:T(8,128)(2,1)S(1)}, u32[]{:S(2)}) copy-start(bf16[512,1024]{0,1:T(8,128)(2,1)S(1)} %copy.56) | copy-start | bytes 3145732
  317.1 9.8 %copy-start.23 = (f32[16,512]{1,0:T(8,128)}, f32[16,512]{1,0:T(8,128)S(1)}, u32[]{:S(2)}) copy-start(f32[16,512]{1,0:T(8,128)S(1)} %log_add_fusion) | copy-start | bytes 98308
  326.9 16.6 %slice-start = ((s8[16777216]{0:T(1024)(128)(4,1)}), s8[4194304]{0:T(1024)(128)(4,1)S(1)}, s32[]{:S(2)}) async-start(s8[16777216]{0:T(1024)(128)(4,1)} %bitcast.115), calls=%async_computation | async-start | bytes 8388608
  326.9 16.6 %slice-start.1 = ((s8[16777216]{0:T(1024)(128)(4,1)}), s8[4194304]{0:T(1024)(128)(4,1)S(1)}, s32[]{:S(2)}) async-start(s8[16777216]{0:T(1024)(128)(4,1)} %bitcast.115), calls=%async_computation.1 | async-start | bytes 8388608
  326.9 16.6 %slice-start.2 = ((s8[16777216]{0:T(1024)(128)(4,1)}), s8[4194304]{0:T(1024)(128)(4,1)S(1)}, s32[]{:S(2)}) async-start(s8[16777216]{0:T(1024)(128)(4,1)} %bitcast.115), calls=%async_computation.2 | async-start | bytes 8388608
  326.9 16.6 %slice-start.3 = ((s8[16777216]{0:T(1024)(128)(4,1)}), s8[4194304]{0:T(1024)(128)(4,1)S(1)}, s32[]{:S(2)}) async-start(s8[16777216]{0:T(1024)(128)(4,1)} %bitcast.115), calls=%async_computation.3 | async-start | bytes 8388608
  351.5 3.5 copy-start
  351.5 3.5 copy-start.33
  355.0 3.4 copy-start.1
  355.0 3.6 copy-start.3
  358.6 2.6 copy-start.32
  361.3 1.3 copy-start.7
  361.3 1.5 copy-start.17
  361.3 1.5 copy-start.29
  361.3 2.2 copy-start.31
  363.5 2.1 copy-start.27
  363.5 2.2 copy-start.9
  366.5 1.6 copy-start.22
  366.5 2.9 copy-start.36
  369.4 5.0 copy-start.20
  369.4 5.0 copy-start.38
  374.4 5.0 copy-start.35
  379.5 5.2 copy-start.16
  393.1 2.9 copy-start.11
  396.0 7.7 %copy-start.30 = (f32[1024]{0:T(1024)S(1)}, f32[1024]{0:T(1024)}, u32[]{:S(2)}) copy-start(f32[1024]{0:T(1024)} %get-tuple-element.111) | copy-start | bytes 12292
  544.4 12.5 %copy-start.24 = (f32[88,1024]{1,0:T(8,128)S(1)}, f32[88,1024]{1,0:T(8,128)}, u32[]{:S(2)}) copy-start(f32[88,1024]{1,0:T(8,128)} %get-tuple-element.163) | copy-start | bytes 1081348

commit v2 on v1

v2 whole, which is shorter than its diff:
```python
import functools
import types

import jax
import jax.numpy as jnp
from jax import lax
from jax.experimental import pallas as pl
from jax.experimental.pallas import tpu as pltpu
from jax.sharding import PartitionSpec as P

MESH = pl.DeviceIdType.MESH
VMEM_LIMIT = 62 << 20
HEADS = 16
HEAD = 64
BUCKETS = 32
EPSILON = 1e-06
NEG_FILL = -1000000000.0
LANES = 128
TILE = 256
CONTRACT_LAST = (((1,), (1,)), ((), ()))
CONTRACT_FIRST = (((0,), (0,)), ((), ()))
BF16, F32, I32 = jnp.bfloat16, jnp.float32, jnp.int32
GELU_SCALE = 0.7978845608028654
GELU_CUBE = 0.044715


def round_up(value, unit):
    return -(-value // unit) * unit


def matmul(left, right):
    return jnp.dot(left, right, preferred_element_type=F32)


def times_trans(left, right):
    return lax.dot_general(left, right, CONTRACT_LAST, preferred_element_type=F32)


def trans_times(left, right):
    return lax.dot_general(left, right, CONTRACT_FIRST, preferred_element_type=F32)


class Plan:
    def __init__(self, wide, narrow):
        self.wide, self.narrow = wide, narrow
        self.bits = [2 << i for i in range(wide.bit_length() - 2)]
        self.chunks = wide // 2
        assert wide == 2 << len(self.bits)


def span(bits):
    out = [0]
    for bit in bits:
        out = out + [member ^ bit for member in out]
    return out


def halves(start, size):
    half = round_up(size // 2, LANES)
    return [(start, half), (start + half, size - half)] if size > 2 * LANES else [(start, size)]


def enter(plan):
    w, n = lax.axis_index("wide"), lax.axis_index("narrow")
    barrier = pltpu.get_barrier_semaphore()
    partners = [(w ^ bit, n) for bit in [1] + plan.bits]
    partners += [(w, lax.rem(n + d, plan.narrow)) for d in range(1, plan.narrow)]
    for partner in partners:
        pl.semaphore_signal(barrier, inc=1, device_id=partner, device_id_type=MESH)
    pl.semaphore_wait(barrier, len(partners))
    return w, n


def loop(low, high, body):
    def step(i, carry):
        body(i)
        return carry

    lax.fori_loop(low, high, step, 0)


def at(index, size):
    return pl.ds(pl.multiple_of(index * size, size), size)


def streamed(low, high, copies, body):
    for copy in copies(lax.rem(low, 2), low):
        copy.start()

    def step(i):
        slot = lax.rem(i, 2)

        @pl.when(i + 1 < high)
        def _():
            for copy in copies(1 - slot, i + 1):
                copy.start()

        for copy in copies(slot, i):
            copy.wait()
        body(i, slot)

    loop(low, high, step)


def run(kernel, inputs, outputs, scratch, in_vmem, out_vmem, collective_id, name):
    sizes = [len(jax.tree.leaves(tree)) for tree in (inputs, outputs, scratch)]
    forms = [jax.tree.structure(tree) for tree in (inputs, outputs, scratch)]

    def flat(*refs):
        first, second = sizes[0], sizes[0] + sizes[1]
        parts = (refs[:first], refs[first:second], refs[second:])
        kernel(*(types.SimpleNamespace(**form.unflatten(part)) for form, part in zip(forms, parts)))

    def specs(tree, resident):
        return jax.tree.leaves(
            {
                key: jax.tree.map(
                    lambda _: pl.BlockSpec(memory_space=pltpu.VMEM if key in resident else pl.ANY), value
                )
                for key, value in tree.items()
            }
        )

    result = pl.pallas_call(
        flat,
        out_shape=jax.tree.leaves(outputs),
        in_specs=specs(inputs, in_vmem),
        out_specs=specs(outputs, out_vmem),
        scratch_shapes=jax.tree.leaves(scratch),
        compiler_params=pltpu.CompilerParams(
            collective_id=collective_id, has_side_effects=True, vmem_limit_bytes=VMEM_LIMIT
        ),
        name=name,
    )(*jax.tree.leaves(inputs))
    return types.SimpleNamespace(**forms[1].unflatten(result))


def sems(*shape):
    return pltpu.SemaphoreType.DMA(shape)


def struct(shape, dtype):
    return jax.ShapeDtypeStruct(shape, dtype)


class Gather:
    def __init__(self, plan, rows, window):
        self.plan, self.rows = plan, rows
        self.start_column, self.columns = window
        self.padded = round_up(self.rows, 16)
        self.aligned = self.padded == self.rows
        self.group = plan.narrow * self.rows
        self.parts = halves(*window)
        self.orders = [plan.bits, plan.bits[::-1]][: len(self.parts)]
        self.chunks = plan.chunks

    def reserve(self):
        count, parts = self.plan.narrow, len(self.parts)
        shapes = [sems(2, count), sems(2, parts, self.chunks), sems(2, parts, self.chunks), sems(2)]
        if not self.aligned:
            shapes.append(pltpu.VMEM((count, self.padded, self.columns), BF16))
            shapes.append(pltpu.VMEM((self.group, self.columns), BF16))
        return shapes

    def bind(self, place, shard, out, refs):
        self.w, self.n = place
        self.shard, self.out = shard, out
        self.zsem, self.bsem, self.csem, self.lsem = refs[:4]
        if not self.aligned:
            self.stage, self.compact = refs[4:]

    def window(self):
        return pl.ds(self.start_column, self.columns)

    def own_slot(self):
        if self.aligned:
            rows = pl.ds(pl.multiple_of(self.n * self.rows, self.rows), self.rows)
            return self.out.at[self.w, rows, self.window()]
        return self.stage.at[self.n]

    def z_copy(self, d):
        return pltpu.make_async_remote_copy(
            src_ref=self.shard.at[:, self.window()],
            dst_ref=self.own_slot(),
            send_sem=self.zsem.at[0, d],
            recv_sem=self.zsem.at[1, d],
            device_id=(self.w, lax.rem(self.n + d, self.plan.narrow)),
            device_id_type=MESH,
        )

    def place_copy(self):
        return pltpu.make_async_copy(self.shard.at[:, self.window()], self.own_slot(), self.lsem.at[0])

    def group_copy(self):
        return pltpu.make_async_copy(self.compact, self.out.at[self.w, :, self.window()], self.lsem.at[1])

    def start(self):
        for d in range(1, self.plan.narrow):
            self.z_copy(d).start()
        self.place_copy().start()

    def hop(self, sems, part, mask, bit, slot):
        start, size = self.parts[part]
        target = self.out.at[self.w ^ mask, :, pl.ds(start, size)]
        source = target
        if mask == 0 and not self.aligned:
            source = self.compact.at[:, pl.ds(start - self.start_column, size)]
        return pltpu.make_async_remote_copy(
            src_ref=source,
            dst_ref=target,
            send_sem=sems.at[0, part, slot],
            recv_sem=sems.at[1, part, slot],
            device_id=(self.w ^ bit, self.n),
            device_id_type=MESH,
        )

    def hops(self, part, stage):
        order = self.orders[part]
        masks = span(order[:stage])
        return [self.hop(self.bsem, part, mask, order[stage], len(masks) + i - 1) for i, mask in enumerate(masks)]

    def core_hops(self, part, stage):
        masks = span(self.orders[part])
        low, high = (0, 1) if stage == 0 else (1 << (stage - 1), 1 << stage)
        return [self.hop(self.csem, part, masks[i], 1, i) for i in range(low, high)]

    def stages(self):
        return len(self.plan.bits) + 2

    def step(self, stage):
        bits, parts = len(self.plan.bits), range(len(self.parts))
        if stage == 0:
            for d in range(1, self.plan.narrow):
                self.z_copy(d).wait_recv()
            self.place_copy().wait()
            if not self.aligned:
                size, wide = self.group, self.plan.narrow * self.padded
                row = lax.broadcasted_iota(I32, (size, wide), 0)
                column = lax.broadcasted_iota(I32, (size, wide), 1)
                pick = column == (row // self.rows) * self.padded + row % self.rows
                self.compact[...] = matmul(
                    pick.astype(F32).astype(BF16), self.stage[...].reshape(wide, self.columns)
                ).astype(BF16)
                self.group_copy().start()
        elif stage <= bits:
            for part in parts:
                for copy in self.hops(part, stage - 1):
                    copy.wait_recv()
        else:
            for part in parts:
                for s in range(bits + 1):
                    for copy in self.core_hops(part, s):
                        copy.wait_recv()
            if not self.aligned:
                self.group_copy().wait()
        if stage < bits:
            for part in parts:
                for copy in self.hops(part, stage):
                    copy.start()
        if stage <= bits:
            for part in parts:
                for copy in self.core_hops(part, stage):
                    copy.start()

    def finish(self):
        for d in range(1, self.plan.narrow):
            self.z_copy(d).wait_send()
        for part in range(len(self.parts)):
            for s in range(len(self.plan.bits)):
                for copy in self.hops(part, s):
                    copy.wait_send()
            for s in range(len(self.plan.bits) + 1):
                for copy in self.core_hops(part, s):
                    copy.wait_send()


class Swap:
    def __init__(self, plan):
        self.plan = plan

    def reserve(self):
        return sems(3, self.plan.chunks)

    def bind(self, place, source, kept, sent, sem):
        self.w, self.n = place
        self.source, self.kept, self.sent, self.sem = source, kept, sent, sem
        self.group = source.shape[0] // self.plan.wide

    def chunk(self, index):
        return self.source.at[pl.ds(pl.multiple_of(index * self.group, self.group), self.group), :]

    def local(self, slot):
        return pltpu.make_async_copy(self.chunk(self.w ^ (2 * slot)), self.kept.at[slot], self.sem.at[2, slot])

    def remote(self, slot):
        return pltpu.make_async_remote_copy(
            src_ref=self.chunk(self.w ^ 1 ^ (2 * slot)),
            dst_ref=self.sent.at[slot],
            send_sem=self.sem.at[0, slot],
            recv_sem=self.sem.at[1, slot],
            device_id=(self.w ^ 1, self.n),
            device_id_type=MESH,
        )

    def start(self):
        for slot in range(self.plan.chunks):
            self.remote(slot).start()
            if self.kept is not None:
                self.local(slot).start()

    def wait_recv(self):
        for slot in range(self.plan.chunks):
            self.remote(slot).wait_recv()

    def finish(self):
        for slot in range(self.plan.chunks):
            self.remote(slot).wait_send()
            if self.kept is not None:
                self.local(slot).wait()


def to_sibling(place, source, target, sem):
    return pltpu.make_async_remote_copy(
        src_ref=source,
        dst_ref=target,
        send_sem=sem.at[0],
        recv_sem=sem.at[1],
        device_id=(place[0] ^ 1, place[1]),
        device_id_type=MESH,
    )


def column_of(row):
    eye = lax.broadcasted_iota(I32, (LANES, LANES), 0) == lax.broadcasted_iota(I32, (LANES, LANES), 1)
    pieces = [
        jnp.sum(jnp.where(eye, row[:, start : start + LANES], 0.0), axis=1, keepdims=True)
        for start in range(0, row.shape[1], LANES)
    ]
    return jnp.concatenate(pieces, axis=0)


def unpack_small(plan, packed, sizes):
    summed = jnp.sum(packed.astype(F32).reshape(plan.wide, plan.narrow, 16, LANES), axis=1)
    rows = []
    for i, size in enumerate(sizes):
        each = LANES // (size * plan.narrow)
        blocks = [
            sum(summed[first + j, i : i + 1, :] for j in range(each))
            for first in range(0, plan.wide, each)
        ]
        rows.append(jnp.concatenate(blocks, axis=1))
    return rows


def same_bucket(width):
    row = lax.broadcasted_iota(I32, (width, width), 0) // HEADS
    column = lax.broadcasted_iota(I32, (width, width), 1) // HEADS
    return (row == column).astype(F32)


def spread_table(table_row):
    width = BUCKETS * HEADS
    lane = lax.broadcasted_iota(I32, (HEADS, width), 1)
    head = lax.broadcasted_iota(I32, (HEADS, width), 0)
    same = lane % HEADS == head
    picked = jnp.where(same, table_row, 0.0).astype(BF16)
    spread = matmul(picked, same_bucket(width).astype(BF16))
    return jnp.concatenate(
        [jnp.where(same, spread[h : h + 1, :], 0.0).astype(BF16) for h in range(HEADS)], axis=0
    )


def bucket_rows(bucket):
    small = bucket.astype(F32).astype(BF16)
    one, zero = jnp.ones_like(small), jnp.zeros_like(small)
    return jnp.concatenate(
        [jnp.where(small == jnp.asarray(j, BF16), one, zero) for j in range(BUCKETS)], axis=0
    )


class Sizes:
    def __init__(self, plan, rows, width, ff, shards):
        self.plan, self.rows, self.width, self.ff = plan, rows, width, ff
        self.shards = shards
        self.group = plan.narrow * shards[0]
        self.down_group = plan.narrow * shards[6]
        self.split = round_up(ff // 2, TILE)
        self.ff_windows = [(0, self.split), (self.split, ff - self.split)]
        self.half_windows = [(0, width // 2), (width // 2, width // 2)]

    def full(self):
        wide = self.plan.wide
        return (
            [(wide, self.group, self.width)] * 4
            + [(wide, self.group, self.ff)] * 2
            + [(wide, self.down_group, self.width)]
        )


QUERY, KEY, VALUE, OUT, GATE, UP, DOWN = range(7)


class Forward:
    def __init__(self, plan, sizes):
        self.plan, self.sizes = plan, sizes
        whole = (0, sizes.width)
        wide = [(weight, window) for window in sizes.ff_windows for weight in (GATE, UP)]
        down = [(DOWN, window) for window in sizes.half_windows]
        self.order = [(weight, whole) for weight in (QUERY, KEY, VALUE, OUT)] + wide + down
        self.small = Gather(plan, 16, (0, LANES))
        self.items = [self.small] + [Gather(plan, sizes.shards[weight], window) for weight, window in self.order]
        self.swaps = [Swap(plan) for _ in range(4)]
        self.extra = self.small.stages() - 4

    def call(self, small, shards, tokens, keep, live, buckets, cotangent):
        plan, s = self.plan, self.sizes
        rows, width, ff, chunks = s.rows, s.width, s.ff, plan.chunks
        turned = struct((2, chunks, s.group, rows), BF16)
        row_block, ff_block = struct((rows, width), BF16), struct((rows, ff), BF16)
        inputs = dict(
            small=small, shards=shards, tokens=tokens, keep=keep, live=live, buckets=buckets, cotangent=cotangent
        )
        outputs = dict(
            small=struct((plan.wide, plan.narrow * 16, LANES), BF16),
            full=[struct(shape, BF16) for shape in s.full()],
            queries=row_block,
            keys=row_block,
            values=row_block,
            prob=struct((HEADS, rows, rows), BF16),
            mid=struct((rows, width), F32),
            hidden=ff_block,
            gate_slope=ff_block,
            up_slope=ff_block,
            turned=[turned] * 3,
            grad_down=struct((chunks, s.down_group, width), BF16),
            rows=struct((8, width), F32),
        )
        square, stream = pltpu.VMEM((rows, width), BF16), pltpu.VMEM((rows, width), F32)
        scratch = dict(
            items=[item.reserve() for item in self.items],
            swaps=[swap.reserve() for swap in self.swaps],
            direct=sems(2),
            held=[pltpu.VMEM(shape, BF16) for shape in s.full()[:3] + s.full()[4:6]],
            load=sems(len(self.items)),
            small=pltpu.VMEM((plan.wide, plan.narrow * 16, LANES), BF16),
            keep=pltpu.VMEM((rows, 1), F32),
            table=pltpu.VMEM((HEADS * 16, BUCKETS * 16), BF16),
            bias=pltpu.VMEM((HEADS, rows, rows), BF16),
            stream=stream,
            normed=square,
            q=square,
            k=square,
            v=square,
            attended=square,
            normed_turned=pltpu.VMEM((width, rows), BF16),
            attended_turned=pltpu.VMEM((width, rows), BF16),
            hidden_turned=pltpu.VMEM((ff, rows), BF16),
            hidden_far=pltpu.VMEM((chunks, s.down_group, rows), BF16),
            cot_far=square,
            prob_stage=pltpu.VMEM((2, 2, rows, rows), BF16),
            prob_sem=sems(2),
            tile_stage=pltpu.VMEM((2, 3, rows, TILE), BF16),
            tile_sem=sems(2, 3),
            down_stage=pltpu.VMEM((2, s.down_group, width), BF16),
            down_sem=sems(2),
            store=sems(4),
        )
        return run(
            self.kernel,
            inputs,
            outputs,
            scratch,
            {"tokens", "keep", "live", "buckets", "cotangent"},
            {"rows"},
            0,
            "gather_forward",
        )

    def kernel(self, i, o, t):
        self.i, self.o, self.t = i, o, t
        self.place = place = enter(self.plan)
        self.small.bind(place, i.small, o.small, t.items[0])
        for item, (weight, _), refs in zip(self.items[1:], self.order, t.items[1:]):
            item.bind(place, i.shards[weight], o.full[weight], refs)
        direct = to_sibling(place, i.cotangent, t.cot_far, t.direct)
        normed, attended, second, hidden = self.swaps
        for swap, source, target, sem in zip(
            self.swaps, (t.normed_turned, t.attended_turned, t.normed_turned), o.turned, t.swaps
        ):
            swap.bind(place, source, target.at[0], target.at[1], sem)
        hidden.bind(place, t.hidden_turned, None, t.hidden_far, t.swaps[3])
        pairs = ((t.q, o.queries), (t.k, o.keys), (t.v, o.values), (t.stream, o.mid))
        store = [pltpu.make_async_copy(*pair, t.store.at[at_]) for at_, pair in enumerate(pairs)]

        for item in self.items[:3]:
            item.start()
        direct.start()
        for turn in range(-self.extra, 4):
            self.tick(turn)
        self.set_up()
        normed.start()
        self.tick(4)
        blocks = self.sizes.rows // 16
        self.bias(0, blocks // 2)
        self.tick(5)
        self.project(QUERY, t.q)
        store[0].start()
        self.bias(blocks // 2, blocks)
        self.tick(6)
        self.project(KEY, t.k)
        store[1].start()
        self.tick(7)
        self.project(VALUE, t.v)
        store[2].start()
        count = HEADS // 2
        self.attend(0, count // 4)
        self.tick(8)
        self.attend(count // 4, 5 * count // 8)
        self.tick(9)
        self.attend(5 * count // 8, count)
        for slot in range(2):
            self.prob_copy(slot, count - 2 + slot).wait()
        self.out_project()
        store[3].start()
        attended.start()
        normed.finish()
        self.norm(2)
        second.start()
        self.tick(10)
        tiles, first = self.sizes.ff // TILE, self.sizes.split // TILE
        self.feed(0, first)
        self.tick(11)
        self.feed(first, tiles)
        for j in (tiles - 2, tiles - 1):
            for copy in self.tile_copies(j % 2, j):
                copy.wait()
        hidden.start()
        self.tick(12)
        direct.wait_recv()
        hidden.wait_recv()
        self.down_gradient()
        self.tick(13)
        for item in self.items:
            item.finish()
        direct.wait_send()
        hidden.finish()
        attended.finish()
        second.finish()
        for swap in (normed, attended, second):
            swap.wait_recv()
        for copy in store:
            copy.wait()

    def held(self, weight):
        return self.t.held[{QUERY: 0, KEY: 1, VALUE: 2, OUT: 0, GATE: 3, UP: 4}[weight]]

    def load(self, k):
        if k == 0:
            return pltpu.make_async_copy(self.o.small, self.t.small, self.t.load.at[0])
        weight, window = self.order[k - 1]
        columns = pl.ds(*window)
        return pltpu.make_async_copy(
            self.o.full[weight].at[:, :, columns], self.held(weight).at[:, :, columns], self.t.load.at[k]
        )

    def tick(self, turn):
        stages, turn = self.small.stages(), turn + self.extra
        for stage in range(stages):
            k = turn - stage
            if 0 <= k < len(self.items):
                self.items[k].step(stage)
                if stage == stages - 1 and (k == 0 or self.order[k - 1][0] != DOWN):
                    self.load(k).start()
        if turn + 3 < len(self.items):
            self.items[turn + 3].start()

    def set_up(self):
        i, o, t = self.i, self.o, self.t
        self.load(0).wait()
        devices = self.plan.wide * self.plan.narrow
        counts = [self.sizes.width // devices] * 3 + [BUCKETS * HEADS // devices]
        embed, gain_one, gain_two, table = unpack_small(self.plan, t.small[...], counts)
        o.rows[...] = jnp.concatenate(
            [embed, gain_one, gain_two, jnp.zeros((5, self.sizes.width), F32)], axis=0
        )
        t.table[...] = spread_table(table)
        t.keep[...] = column_of(i.keep[...].astype(F32))

        def body(j):
            block = at(j, 64)
            t.stream[block, :] = jnp.where(
                t.keep[block, :] > 0.5, i.tokens[block, :].astype(F32), o.rows[0:1, :]
            )

        loop(0, self.sizes.rows // 64, body)
        self.norm(1)

    def norm(self, gain):
        o, t = self.o, self.t

        def body(j):
            block = at(j, 64)
            x = t.stream[block, :]
            scale = lax.rsqrt(jnp.mean(x * x, axis=-1, keepdims=True) + EPSILON)
            t.normed[block, :] = (x * scale * o.rows[gain : gain + 1, :]).astype(BF16)

        loop(0, self.sizes.rows // 64, body)
        self.turn(t.normed, t.normed_turned)

    def turn(self, source, target):
        def body(j):
            target[at(j, LANES), :] = source[:, at(j, LANES)].T

        loop(0, self.sizes.width // LANES, body)

    def bias(self, low, high):
        i, t = self.i, self.t

        def body(j):
            block = at(j, 16)
            spread = matmul(t.table[...], bucket_rows(i.buckets[block, :]))
            spread = jnp.where(i.live[...] > 0, spread, NEG_FILL).astype(BF16)
            t.bias[:, block, :] = spread.reshape(HEADS, 16, spread.shape[-1])

        loop(low, high, body)

    def project(self, weight, target):
        self.load(1 + weight).wait()
        held, width = self.held(weight), self.sizes.width

        def body(j):
            block = held[:, :, at(j, TILE)].reshape(width, TILE)
            target[:, at(j, TILE)] = matmul(self.t.normed[...], block).astype(BF16)

        loop(0, width // TILE, body)

    def prob_copy(self, slot, pair):
        t = self.t
        return pltpu.make_async_copy(
            t.prob_stage.at[slot], self.o.prob.at[pl.ds(2 * pair, 2)], t.prob_sem.at[slot]
        )

    def attend(self, low, high):
        t = self.t
        lane = lax.broadcasted_iota(I32, (1, LANES), 1)

        def body(pair):
            columns, slot = at(pair, LANES), lax.rem(pair, 2)

            @pl.when(pair >= 2)
            def _():
                self.prob_copy(slot, pair).wait()

            q, k, v = t.q[:, columns], t.k[:, columns], t.v[:, columns]
            mixed = []
            for e in range(2):
                own = jnp.where((lane < HEAD) == (e == 0), q, jnp.zeros_like(q))
                scores = times_trans(own, k) + t.bias[2 * pair + e].astype(F32)
                top = jnp.max(scores, axis=-1, keepdims=True)
                powers = jnp.exp(scores - top)
                total = jnp.sum(powers, axis=-1, keepdims=True)
                prob = (powers * (1.0 / total)).astype(BF16)
                t.prob_stage[slot, e] = prob
                mixed.append(matmul(prob, v))
            t.attended[:, columns] = jnp.where(lane < HEAD, mixed[0], mixed[1]).astype(BF16)
            self.prob_copy(slot, pair).start()

        loop(low, high, body)

    def out_project(self):
        t, width = self.t, self.sizes.width
        self.load(1 + OUT).wait()

        def body(j):
            block = self.held(OUT)[:, :, at(j, TILE)].reshape(width, TILE)
            t.stream[:, at(j, TILE)] += matmul(t.attended[...], block)

        loop(0, width // TILE, body)
        self.turn(t.attended, t.attended_turned)

    def tile_copies(self, slot, j):
        o, t = self.o, self.t
        return [
            pltpu.make_async_copy(t.tile_stage.at[slot, which], ref.at[:, at(j, TILE)], t.tile_sem.at[slot, which])
            for which, ref in enumerate((o.hidden, o.gate_slope, o.up_slope))
        ]

    def feed(self, low, high):
        t, width = self.t, self.sizes.width
        for k, (weight, window) in enumerate(self.order):
            if weight in (GATE, UP) and window[0] == low * TILE:
                self.load(1 + k).wait()

        def body(j):
            slot = lax.rem(j, 2)

            @pl.when(j >= 2)
            def _():
                for copy in self.tile_copies(slot, j):
                    copy.wait()

            second = t.normed[...]
            gate = matmul(second, self.held(GATE)[:, :, at(j, TILE)].reshape(width, TILE))
            up = matmul(second, self.held(UP)[:, :, at(j, TILE)].reshape(width, TILE))
            square = gate * gate
            bend = jnp.tanh(GELU_SCALE * gate * (1.0 + GELU_CUBE * square))
            half = 0.5 * (1.0 + bend)
            act = gate * half
            slope = half + (0.5 * GELU_SCALE) * gate * (1.0 - bend * bend) * (1.0 + (3.0 * GELU_CUBE) * square)
            hidden = (act * up).astype(BF16)
            t.tile_stage[slot, 0] = hidden
            t.tile_stage[slot, 1] = (up * slope).astype(BF16)
            t.tile_stage[slot, 2] = act.astype(BF16)
            for copy in self.tile_copies(slot, j):
                copy.start()
            t.hidden_turned[at(j, TILE), :] = hidden.T

        loop(low, high, body)

    def down_copy(self, slot):
        t = self.t
        return pltpu.make_async_copy(t.down_stage.at[slot % 2], self.o.grad_down.at[slot], t.down_sem.at[slot % 2])

    def down_gradient(self):
        i, t, group = self.i, self.t, self.sizes.down_group
        for slot in range(self.plan.chunks):
            if slot >= 2:
                self.down_copy(slot - 2).wait()

            def body(j, slot=slot):
                near = t.hidden_turned[at(self.place[0] ^ (2 * slot), group), :]
                t.down_stage[slot % 2, :, at(j, TILE)] = (
                    matmul(near, i.cotangent[:, at(j, TILE)])
                    + matmul(t.hidden_far[slot], t.cot_far[:, at(j, TILE)])
                ).astype(BF16)

            loop(0, self.sizes.width // TILE, body)
            self.down_copy(slot).start()
        for slot in range(self.plan.chunks - 2, self.plan.chunks):
            self.down_copy(slot).wait()


class Reduce:
    def __init__(self, plan, rows, window, order):
        self.plan, self.rows = plan, rows
        self.start_column, self.columns = window
        self.padded = round_up(rows, 16)
        self.aligned = self.padded == rows
        self.group = plan.narrow * rows
        self.order = order
        self.chunks = plan.chunks

    def reserve(self):
        count, columns = self.plan.narrow, self.columns
        shapes = [
            sems(2, self.chunks),
            sems(2, count),
            pltpu.VMEM((self.chunks, self.group, columns), BF16),
            pltpu.VMEM((self.chunks - 1, self.group, columns), BF16),
            pltpu.VMEM((count - 1, self.padded, columns), BF16),
        ]
        if not self.aligned:
            shapes.append(pltpu.VMEM((count, self.padded, columns), BF16))
        return shapes

    def bind(self, place, out, refs):
        self.w, self.n = place
        self.out, self.done = out, 0
        self.bsem, self.zsem, self.acc, self.received, self.zreceived = refs[:5]
        if not self.aligned:
            self.stage = refs[5]

    def hops(self, stage):
        bit, masks = self.order[stage], span(self.order[stage + 1 :])
        base = self.chunks - 2 * len(masks)
        return [
            (
                mask >> 1,
                base + k,
                pltpu.make_async_remote_copy(
                    src_ref=self.acc.at[(bit ^ mask) >> 1],
                    dst_ref=self.received.at[base + k],
                    send_sem=self.bsem.at[0, base + k],
                    recv_sem=self.bsem.at[1, base + k],
                    device_id=(self.w ^ bit, self.n),
                    device_id_type=MESH,
                ),
            )
            for k, mask in enumerate(masks)
        ]

    def z_copy(self, d):
        peer = lax.rem(self.n + d, self.plan.narrow)
        source = self.acc.at[0, at(peer, self.rows), :] if self.aligned else self.stage.at[peer]
        return pltpu.make_async_remote_copy(
            src_ref=source,
            dst_ref=self.zreceived.at[d - 1],
            send_sem=self.zsem.at[0, d],
            recv_sem=self.zsem.at[1, d],
            device_id=(self.w, peer),
            device_id_type=MESH,
        )

    def step(self, stage):
        bits = len(self.order)
        if 1 <= stage <= bits:
            for slot, k, copy in self.hops(stage - 1):
                copy.wait_recv()

                def body(j, slot=slot, k=k):
                    block = at(j, 16)
                    self.acc[slot, block, :] += self.received[k, block, :]

                loop(0, self.group // 16, body)
        if stage < bits:
            for _, _, copy in self.hops(stage):
                copy.start()
        elif stage == bits:
            if not self.aligned:
                size, wide = self.group, self.plan.narrow * self.padded
                row = lax.broadcasted_iota(I32, (wide, size), 0)
                column = lax.broadcasted_iota(I32, (wide, size), 1)
                pick = row == (column // self.rows) * self.padded + column % self.rows
                self.stage[...] = (
                    matmul(pick.astype(F32).astype(BF16), self.acc[0]).astype(BF16).reshape(self.stage.shape)
                )
            for d in range(1, self.plan.narrow):
                self.z_copy(d).start()
        else:
            total = self.acc[0, at(self.n, self.rows), :] if self.aligned else self.stage[self.n]
            total = total.astype(F32)
            for d in range(1, self.plan.narrow):
                self.z_copy(d).wait_recv()
                total = total + self.zreceived[d - 1].astype(F32)
            self.out[:, pl.ds(self.start_column, self.columns)] = total[: self.rows]

    def finish(self):
        for stage in range(len(self.order)):
            for _, _, copy in self.hops(stage):
                copy.wait_send()
        for d in range(1, self.plan.narrow):
            self.z_copy(d).wait_send()


class SumAll:
    def __init__(self, plan, shape):
        self.shape = shape
        self.rounds = [(bit, 0) for bit in [1] + plan.bits]
        self.rounds += [(0, 1 << k) for k in range(plan.narrow.bit_length() - 1)]

    def reserve(self):
        count = len(self.rounds)
        return [sems(2, count)] + [pltpu.VMEM((count, *self.shape), F32)] * 2

    def bind(self, place, out, refs):
        self.w, self.n = place
        self.out = out
        self.sem, self.held, self.received = refs

    def copy(self, turn):
        bit, other = self.rounds[turn]
        return pltpu.make_async_remote_copy(
            src_ref=self.held.at[turn],
            dst_ref=self.received.at[turn],
            send_sem=self.sem.at[0, turn],
            recv_sem=self.sem.at[1, turn],
            device_id=(self.w ^ bit, self.n ^ other),
            device_id_type=MESH,
        )

    def start(self, value):
        self.held[0] = value
        self.copy(0).start()

    def step(self, turn):
        self.copy(turn).wait_recv()
        total = self.held[turn] + self.received[turn]
        if turn + 1 < len(self.rounds):
            self.held[turn + 1] = total
            self.copy(turn + 1).start()
        else:
            self.out[...] = total

    def finish(self):
        for turn in range(len(self.rounds)):
            self.copy(turn).wait_send()


class Backward:
    def __init__(self, plan, sizes):
        self.plan, self.sizes = plan, sizes
        ways = [plan.bits, plan.bits[::-1]]
        self.reduces = []
        for weight in range(7):
            windows = sizes.ff_windows if weight in (GATE, UP) else sizes.half_windows
            turn = 1 if weight in (UP, KEY, OUT) else 0
            self.reduces.append(
                [Reduce(plan, sizes.shards[weight], window, ways[k ^ turn]) for k, window in enumerate(windows)]
            )
        self.sums = SumAll(plan, (8, sizes.width))

    def call(self, f, tokens, keep, buckets, cotangent):
        plan, s = self.plan, self.sizes
        rows, width, ff, chunks = s.rows, s.width, s.ff, plan.chunks
        inputs = dict(
            full=f.full,
            queries=f.queries,
            keys=f.keys,
            values=f.values,
            prob=f.prob,
            mid=f.mid,
            hidden=f.hidden,
            gate_slope=f.gate_slope,
            up_slope=f.up_slope,
            turned=f.turned,
            grad_down=f.grad_down,
            rows=f.rows,
            tokens=tokens,
            keep=keep,
            buckets=buckets,
            cotangent=cotangent,
        )
        row_block = struct((rows, width), BF16)
        outputs = dict(
            result=row_block,
            input_grad=struct((rows, width), F32),
            grads=[struct((size, ff if weight in (GATE, UP) else width), F32) for weight, size in enumerate(s.shards)],
            sums=struct((8, width), F32),
            far_ff=[struct((rows, ff), BF16)] * 2,
            far_out=row_block,
            far_attn=[row_block] * 3,
        )
        square = pltpu.VMEM((rows, width), BF16)
        scratch = dict(
            reduces=[[item.reserve() for item in pair] for pair in self.reduces],
            small=self.sums.reserve(),
            keep=pltpu.VMEM((rows, 1), F32),
            stream=pltpu.VMEM((rows, width), F32),
            back=pltpu.VMEM((rows, width), F32),
            totals=pltpu.VMEM((8, width), F32),
            grad_mid=square,
            grad_attended=square,
            grad_qkv=[square] * 3,
            acc_sem=sems(2, chunks),
            load=sems(8),
            ff_sem=sems(2, 2, 2),
            out_sem=sems(2),
            attn_sem=sems(2, 3, 2),
            tile_sem=sems(2, 3),
            result_sem=sems(2),
        )
        return run(
            self.kernel,
            inputs,
            outputs,
            scratch,
            {"rows", "tokens", "keep", "buckets", "cotangent"},
            {"grads", "sums"},
            1,
            "backward_reduce",
        )

    def advance(self, weight, parts=(0, 1)):
        for part in parts:
            item = self.reduces[weight][part]
            item.step(item.done)
            item.done += 1

    def kernel(self, i, o, t):
        self.i, self.o, self.t = i, o, t
        plan, s = self.plan, self.sizes
        self.place = place = enter(plan)
        for pair, out, refs in zip(self.reduces, o.grads, t.reduces):
            for item, own in zip(pair, refs):
                item.bind(place, out, own)
        self.sums.bind(place, o.sums, t.small)
        last = len(plan.bits) + 1

        mid = pltpu.make_async_copy(i.mid, t.stream, t.load.at[0])
        mid.start()
        loads = []
        for part, (start, size) in enumerate(s.half_windows):
            for slot in range(plan.chunks):
                loads.append(
                    pltpu.make_async_copy(
                        i.grad_down.at[slot, :, pl.ds(start, size)],
                        self.reduces[DOWN][part].acc.at[slot],
                        t.acc_sem.at[part, slot],
                    )
                )
                loads[-1].start()
        for copy in loads:
            copy.wait()
        self.advance(DOWN)
        t.keep[...] = column_of(i.keep[...].astype(F32))
        t.totals[...] = jnp.zeros_like(t.totals)

        def feed_phase(near, turned, sem):
            turned_copy = pltpu.make_async_copy(i.turned[2], turned, sem)
            turned_copy.start()
            pl.run_scoped(
                functools.partial(self.feed_back, near, mid),
                pltpu.VMEM((s.ff, s.width), BF16),
                pltpu.VMEM((2, 2, s.rows, TILE), BF16),
                pltpu.VMEM((s.rows, s.ff), BF16),
                pltpu.VMEM((s.rows, s.width), BF16),
                sems(plan.wide),
                sems(2),
            )
            turned_copy.wait()
            pl.run_scoped(
                functools.partial(self.feed_weights, near, turned),
                pltpu.VMEM((2, 2, s.rows, TILE), BF16),
            )
            groups = TILE // s.group
            pl.run_scoped(
                functools.partial(self.feed_input, near),
                pltpu.VMEM((2, 2, groups, s.group, s.ff), BF16),
            )
            for part in range(2):
                for copy in self.ff_copies(near, part):
                    copy.wait_send()

        pl.run_scoped(
            feed_phase,
            [pltpu.VMEM((s.rows, s.ff), BF16)] * 2,
            pltpu.VMEM((2, plan.chunks, s.group, s.rows), BF16),
            pltpu.SemaphoreType.DMA,
        )
        self.norm_back(2)
        out_copy = to_sibling(place, t.grad_mid, o.far_out, t.out_sem)
        out_copy.start()
        pl.run_scoped(
            functools.partial(self.out_back, out_copy),
            pltpu.VMEM((plan.wide, s.group, s.width), BF16),
            pltpu.VMEM((2, plan.chunks, s.group, s.rows), BF16),
            pltpu.VMEM((s.rows, s.width), BF16),
            sems(3),
        )
        self.advance(DOWN)

        def attention_phase(q, k, v, grad_scores, prob, turned, far, sem):
            copies = [
                pltpu.make_async_copy(source, target, sem.at[which])
                for which, (source, target) in enumerate(
                    ((i.queries, q), (i.keys, k), (i.values, v), (i.turned[0], turned))
                )
            ]
            for copy in copies:
                copy.start()
            for copy in copies:
                copy.wait()
            half = HEADS // 4
            self.attend_back(0, half, q, k, v, grad_scores, prob)
            self.send_attention(0)
            self.advance(GATE)
            self.advance(UP)
            self.attention_weights(0, turned, far, sem.at[4])
            self.advance(DOWN)
            self.attend_back(half, 2 * half, q, k, v, grad_scores, prob)
            self.send_attention(1)
            self.advance(OUT)
            self.advance(GATE)
            self.advance(UP)
            self.attention_weights(1, turned, far, sem.at[4])
            self.table_back(grad_scores)

        pl.run_scoped(
            attention_phase,
            *[pltpu.VMEM((s.rows, s.width), BF16)] * 3,
            pltpu.VMEM((HEADS, s.rows, s.rows), BF16),
            pltpu.VMEM((2, 2, s.rows, s.rows), BF16),
            pltpu.VMEM((2, plan.chunks, s.group, s.rows), BF16),
            pltpu.VMEM((3, s.rows, s.width // 2), BF16),
            sems(5),
        )
        self.advance(OUT)
        for weight in (QUERY, KEY, VALUE):
            self.advance(weight)
        groups = TILE // s.group
        pl.run_scoped(self.attention_input, pltpu.VMEM((2, 3, groups, s.group, s.width), BF16))
        self.norm_back(1)
        self.sums.start(t.totals[...])
        store = pltpu.make_async_copy(t.stream, o.input_grad, t.load.at[1])
        store.start()
        turn = 0
        left = [GATE, UP, QUERY, KEY, VALUE, OUT, DOWN]
        while left:
            for weight in list(left):
                if self.reduces[weight][0].done > last:
                    left.remove(weight)
                    continue
                self.advance(weight)
                if turn < len(self.sums.rounds):
                    self.sums.step(turn)
                turn += 1
        store.wait()
        out_copy.wait_send()
        for part in range(2):
            for copy in self.attention_copies(part):
                copy.wait_send()
        for pair in self.reduces:
            for item in pair:
                item.finish()
        self.sums.finish()

    def ff_copies(self, near, part):
        window = pl.ds(*self.sizes.ff_windows[part])
        return [
            to_sibling(
                self.place, near[which].at[:, window], self.o.far_ff[which].at[:, window], self.t.ff_sem.at[part, which]
            )
            for which in range(2)
        ]

    def feed_back(self, near, mid, down, slopes, hidden, result, sem, other):
        i, o, t, s = self.i, self.o, self.t, self.sizes
        group = s.down_group
        copies = [
            pltpu.make_async_copy(i.full[DOWN].at[k], down.at[pl.ds(k * group, group), :], sem.at[k])
            for k in range(self.plan.wide)
        ]
        for copy in copies:
            copy.start()
        hidden_copy = pltpu.make_async_copy(i.hidden, hidden, other.at[0])
        hidden_copy.start()
        for copy in copies:
            copy.wait()

        def slope_copies(slot, j):
            return [
                pltpu.make_async_copy(ref.at[:, at(j, TILE)], slopes.at[slot, which], t.tile_sem.at[slot, which])
                for which, ref in enumerate((i.gate_slope, i.up_slope))
            ]

        def body(j, slot):
            grad_act = times_trans(i.cotangent[...], down[at(j, TILE), :])
            for which in range(2):
                near[which][:, at(j, TILE)] = (grad_act * slopes[slot, which].astype(F32)).astype(BF16)

        edges = [0, s.split // TILE, s.ff // TILE]
        for part in range(2):
            streamed(edges[part], edges[part + 1], slope_copies, body)
            for copy in self.ff_copies(near, part):
                copy.start()
        hidden_copy.wait()
        mid.wait()

        def finish(j):
            block = at(j, TILE)
            result[:, block] = (t.stream[:, block] + matmul(hidden[...], down[:, block])).astype(BF16)

        loop(0, s.width // TILE, finish)
        store = pltpu.make_async_copy(result, o.result, other.at[1])
        store.start()
        store.wait()

    def feed_weights(self, near, turned, far):
        o, t, s = self.o, self.t, self.sizes

        def far_copies(slot, j):
            return [
                pltpu.make_async_copy(o.far_ff[which].at[:, at(j, TILE)], far.at[slot, which], t.tile_sem.at[slot, which])
                for which in range(2)
            ]

        edges = [0, s.split // TILE, s.ff // TILE]
        rows = self.plan.chunks * s.group
        for part in range(2):
            for copy in self.ff_copies(near, part):
                copy.wait_recv()

            def body(j, slot, part=part):
                for which, weight in enumerate((GATE, UP)):
                    own = turned[0].reshape(rows, s.rows)
                    other = turned[1].reshape(rows, s.rows)
                    grad = matmul(own, near[which][:, at(j, TILE)]) + matmul(other, far[slot, which])
                    acc = self.reduces[weight][part].acc
                    acc[:, :, at(j - edges[part], TILE)] = grad.astype(BF16).reshape(self.plan.chunks, s.group, TILE)

            streamed(edges[part], edges[part + 1], far_copies, body)
            self.advance(GATE, (part,))
            self.advance(UP, (part,))
            if part == 0:
                self.advance(DOWN)

    def feed_input(self, near, held):
        i, t, s = self.i, self.t, self.sizes
        groups = TILE // s.group

        def weight_copies(slot, j):
            return [
                pltpu.make_async_copy(i.full[weight].at[pl.ds(j * groups, groups)], held.at[slot, which], t.tile_sem.at[slot, which])
                for which, weight in enumerate((GATE, UP))
            ]

        def body(j, slot):
            t.back[:, at(j, TILE)] = times_trans(near[0][...], held[slot, 0].reshape(TILE, s.ff)) + times_trans(
                near[1][...], held[slot, 1].reshape(TILE, s.ff)
            )

        streamed(0, s.width // TILE, weight_copies, body)

    def norm_back(self, which):
        i, t, s = self.i, self.t, self.sizes

        def body(j):
            block = at(j, 32)
            kept = t.keep[block, :] > 0.5
            back = t.back[block, :]
            if which == 2:
                x = t.stream[block, :]
                before = i.cotangent[block, :].astype(F32)
            else:
                x = jnp.where(kept, i.tokens[block, :].astype(F32), i.rows[0:1, :])
                before = t.stream[block, :]
            scale = lax.rsqrt(jnp.mean(x * x, axis=-1, keepdims=True) + EPSILON)
            scaled = x * scale
            u = back * i.rows[which : which + 1, :]
            inner = jnp.mean(u * scaled, axis=-1, keepdims=True)
            total = before + scale * (u - scaled * inner)
            t.totals[which : which + 1, :] += jnp.sum(back * scaled, axis=0, keepdims=True)
            if which == 2:
                t.stream[block, :] = total
                t.grad_mid[block, :] = total.astype(BF16)
            else:
                t.stream[block, :] = jnp.where(kept, total, 0.0)
                t.totals[0:1, :] += jnp.sum(jnp.where(kept, 0.0, total), axis=0, keepdims=True)

        loop(0, s.rows // 32, body)

    def out_back(self, out_copy, weight, turned, far, sem):
        i, o, t, s = self.i, self.o, self.t, self.sizes
        copies = [
            pltpu.make_async_copy(i.full[OUT], weight, sem.at[0]),
            pltpu.make_async_copy(i.turned[1], turned, sem.at[1]),
        ]
        for copy in copies:
            copy.start()
        for copy in copies:
            copy.wait()
        groups = TILE // s.group

        def attended(j):
            block = weight[pl.ds(j * groups, groups)].reshape(TILE, s.width)
            t.grad_attended[:, at(j, TILE)] = times_trans(t.grad_mid[...], block).astype(BF16)

        loop(0, s.width // TILE, attended)
        out_copy.wait_recv()
        load = pltpu.make_async_copy(o.far_out, far, sem.at[2])
        load.start()
        load.wait()
        rows = self.plan.chunks * s.group
        for part, (start, size) in enumerate(s.half_windows):

            def body(j, part=part, start=start):
                columns = pl.ds(pl.multiple_of(start + j * TILE, TILE), TILE)
                grad = matmul(turned[0].reshape(rows, s.rows), t.grad_mid[:, columns])
                grad += matmul(turned[1].reshape(rows, s.rows), far[:, columns])
                self.reduces[OUT][part].acc[:, :, at(j, TILE)] = grad.astype(BF16).reshape(
                    self.plan.chunks, s.group, TILE
                )

            loop(0, size // TILE, body)
            self.advance(OUT, (part,))

    def attend_back(self, low, high, q, k, v, grad_scores, prob):
        i, t = self.i, self.t
        lane = lax.broadcasted_iota(I32, (1, LANES), 1)

        def prob_copies(slot, pair):
            return [pltpu.make_async_copy(i.prob.at[pl.ds(2 * pair, 2)], prob.at[slot], t.tile_sem.at[slot, 0])]

        def body(pair, slot):
            columns = at(pair, LANES)
            q_pair, k_pair, v_pair, grad = q[:, columns], k[:, columns], v[:, columns], t.grad_attended[:, columns]
            found = [[], [], []]
            for e in range(2):
                own = jnp.where((lane < HEAD) == (e == 0), grad, jnp.zeros_like(grad))
                weights = prob[slot, e]
                wide = weights.astype(F32)
                grad_prob = times_trans(own, v_pair)
                delta = jnp.sum(grad_prob * wide, axis=-1, keepdims=True)
                scores = (wide * (grad_prob - delta)).astype(BF16)
                grad_scores[2 * pair + e] = scores
                found[0].append(matmul(scores, k_pair))
                found[1].append(trans_times(scores, q_pair))
                found[2].append(trans_times(weights, grad))
            for ref, (first, second) in zip(t.grad_qkv, found):
                ref[:, columns] = jnp.where(lane < HEAD, first, second).astype(BF16)

        streamed(low, high, prob_copies, body)

    def attention_copies(self, part):
        window = pl.ds(*self.sizes.half_windows[part])
        return [
            to_sibling(
                self.place,
                self.t.grad_qkv[which].at[:, window],
                self.o.far_attn[which].at[:, window],
                self.t.attn_sem.at[part, which],
            )
            for which in range(3)
        ]

    def send_attention(self, part):
        for copy in self.attention_copies(part):
            copy.start()

    def attention_weights(self, part, turned, far, sem):
        o, t, s = self.o, self.t, self.sizes
        start, size = s.half_windows[part]
        rows = self.plan.chunks * s.group
        for which, copy in enumerate(self.attention_copies(part)):
            copy.wait_recv()
            load = pltpu.make_async_copy(o.far_attn[which].at[:, pl.ds(start, size)], far.at[which], sem)
            load.start()
            load.wait()

            def body(j, which=which):
                columns = pl.ds(pl.multiple_of(start + j * TILE, TILE), TILE)
                grad = matmul(turned[0].reshape(rows, s.rows), t.grad_qkv[which][:, columns])
                grad += matmul(turned[1].reshape(rows, s.rows), far[which, :, at(j, TILE)])
                self.reduces[which][part].acc[:, :, at(j, TILE)] = grad.astype(BF16).reshape(
                    self.plan.chunks, s.group, TILE
                )

            loop(0, size // TILE, body)
            self.advance(which, (part,))

    def attention_input(self, held):
        i, t, s = self.i, self.t, self.sizes
        groups = TILE // s.group

        def weight_copies(slot, j):
            return [
                pltpu.make_async_copy(i.full[which].at[pl.ds(j * groups, groups)], held.at[slot, which], t.tile_sem.at[slot, which])
                for which in range(3)
            ]

        def body(j, slot):
            t.back[:, at(j, TILE)] = sum(
                times_trans(t.grad_qkv[which][...], held[slot, which].reshape(TILE, s.width)) for which in range(3)
            )

        streamed(0, s.width // TILE, weight_copies, body)

    def table_back(self, grad_scores):
        i, t, s = self.i, self.t, self.sizes
        width = BUCKETS * HEADS

        def count(total):
            total[...] = jnp.zeros_like(total)

            def body(j):
                block = at(j, 16)
                scores = grad_scores[:, block, :].reshape(HEADS * 16, s.rows)
                total[...] += times_trans(bucket_rows(i.buckets[block, :]), scores)

            loop(0, s.rows // 16, body)
            found = total[...].T
            row = lax.broadcasted_iota(I32, found.shape, 0)
            lane = lax.broadcasted_iota(I32, found.shape, 1)
            found = jnp.where(row % 16 == lane % 16, found, 0.0)
            by_head = jnp.sum(found.reshape(HEADS, 16, width), axis=1)
            summed = jnp.dot(
                by_head, same_bucket(width), precision=lax.Precision.HIGHEST, preferred_element_type=F32
            )
            head = lax.broadcasted_iota(I32, summed.shape, 0)
            lane = lax.broadcasted_iota(I32, summed.shape, 1)
            t.totals[3:4, :width] = jnp.sum(
                jnp.where(lane % HEADS == head, summed, 0.0), axis=0, keepdims=True
            )

        pl.run_scoped(count, pltpu.VMEM((width, HEADS * 16), F32))


def pack_small(vectors, device):
    rows = []
    for vector in vectors:
        size = vector.shape[0]
        mine = jnp.arange(LANES) // size == lax.rem(device, LANES // size)
        rows.append(jnp.where(mine, jnp.tile(vector, LANES // size), jnp.zeros((), vector.dtype)))
    rows += [jnp.zeros((LANES,), vectors[0].dtype)] * (16 - len(rows))
    return jnp.stack(rows)


def per_device(
    plan,
    tokens,
    patch_keep,
    text_len,
    buckets,
    mask_embed,
    norm_attn,
    w_query,
    w_key,
    w_value,
    w_out,
    bias_table,
    norm_ffn,
    w_gate,
    w_up,
    w_down,
    cotangent,
):
    rows, width = tokens.shape
    page_count, patches = patch_keep.shape
    assert page_count == 1
    device = lax.axis_index("wide") * plan.narrow + lax.axis_index("narrow")
    keep = jnp.concatenate([patch_keep, jnp.ones((1, rows - patches), I32)], axis=1)
    live = (jnp.arange(rows, dtype=I32)[None, :] < (patches + text_len)[:, None]).astype(I32)
    small = pack_small((mask_embed, norm_attn, norm_ffn, bias_table), device)
    weights = (w_query, w_key, w_value, w_out, w_gate, w_up, w_down)
    shards = [jnp.pad(weight, ((0, -weight.shape[0] % 16), (0, 0))) for weight in weights]
    sizes = Sizes(plan, rows, width, w_gate.shape[1], [weight.shape[0] for weight in weights])
    forward = Forward(plan, sizes).call(small, shards, tokens, keep, live, buckets, cotangent)
    back = Backward(plan, sizes).call(forward, tokens, keep, buckets, cotangent)

    def own(row, size):
        return lax.dynamic_slice(back.sums[row], (device * size,), (size,))

    query, key, value, out, gate, up, down = back.grads
    return (
        back.result,
        back.input_grad,
        own(0, mask_embed.shape[0]),
        own(1, norm_attn.shape[0]),
        query,
        key,
        value,
        out,
        own(3, bias_table.shape[0]),
        own(2, norm_ffn.shape[0]),
        gate,
        up,
        down,
    )


def solution(mesh):
    rows, flat = P(("wide", "narrow"), None), P(("wide", "narrow"))
    plan = Plan(mesh.shape["wide"], mesh.shape["narrow"])
    return jax.shard_map(
        functools.partial(per_device, plan),
        mesh=mesh,
        in_specs=(rows, rows, flat, rows, flat, flat, rows, rows, rows, rows, flat, flat, rows, rows, rows, rows),
        out_specs=(rows, rows, flat, flat, rows, rows, rows, rows, flat, flat, rows, rows, rows),
        check_vma=False,
    )
```

time: 567 us -> 316 us (0.56); the launches traced: 558 us -> 315 us
  matrix products: 151 us -> 0 us
  local copies, waits for them, and re-layouts: 98.3 us -> 18.8 us
  other arithmetic: 31.1 us -> 0.61 us
  Pallas kernels: 275 us -> 294 us
    dot_general x29 -> x0, matrix products: 151 us -> none  [the longest x7 31.5 us: matmul(): return jnp.dot(left, right, preferred_element_type=jnp.float32)]
    eq x1 -> x0, local copies, waits for them, and re-layouts: 46.2 us -> none  [bucket_table(): bucket[:, :, None] == jnp.arange(BUCKETS, dtype=jnp.int32)[None, None, :]]
    dot_general x1 -> x0, local copies, waits for them, and re-layouts: 19.4 us -> none  [page_scores(): jnp.einsum('qkb,bh->hqk', one_hot, table_rows, preferred_element_type=jnp...]
    pallas_call x2, Pallas kernels: 275 us -> 294 us  [run(): pl.pallas_call(flat, out_shape=jax.tree.leaves(outputs), in_specs=specs(i...]
    unnamed x106 -> x25, local copies, waits for them, and re-layouts: 19 us -> 8.48 us
    reduce_sum x7 -> x0, other arithmetic: 9.64 us -> none  [the longest x1 8.35 us: attend_forward(): row_total = jnp.sum(exponent, axis=-1, keepdims=True)]
    eq x2 -> x0, other arithmetic: 9.36 us -> none  [the longest x1 8.66 us: bucket_table(): bucket[:, :, None] == jnp.arange(BUCKETS, dtype=jnp.int32)[None, None, :]]
    convert_element_type x3 -> x1, other arithmetic: 9.92 us -> 0.58 us  [per_device(): (jnp.arange(rows, dtype=I32)[None, :] < (patches + text_len)[:, None]).as...]
where the time goes in v2:
time: 316 us; the launch traced here: 315 us
  Pallas kernels  294 us (93%)
  local copies, waits for them, and re-layouts  18.8 us (6%)
    pallas_call x2, Pallas kernels, run(): pl.pallas_call(flat, out_shape=jax.tree.leaves(outputs), in_specs=specs(i...  294 us
    unnamed x25, local copies, waits for them, and re-layouts  8.48 us

profile of v2, /device:TPU:0, one launch (start us, length us, event | category | flops | bytes accessed | tf_op | source)
XLA Modules:
  0.0 315.2 jit_solution(16843647163929415778)
XLA Ops:
  0.6 0.7 tile.42
  1.3 0.1 tile.43
  1.4 0.7 tile.40
  2.1 0.1 tile.41
  2.2 0.7 tile.16
  2.8 0.1 tile.17
  2.9 0.7 tile.18
  3.6 0.1 tile.19
  3.7 1.2 stack.15.refs_11_
  4.9 1.3 concatenate.3.refs_2_.refs_12_
  6.1 1.6 pad.5.refs_10_
  8.4 0.6 compare_convert_fusion.refs_3_
  9.0 140.4 %gather_forward.1 = (bf16[8,128,1024]{2,1,0:T(8,128)(2,1)}, bf16[8,128,1024]{2,1,0:T(8,128)(2,1)}, bf16[8,128,1024]{2,1,0:T(8,128)(2,1)}, bf16[8,128,1024]{2,1,0...) custom-call(s32[512,512]{1,0:T(8,128)} %refs_0_.3, ...), custom_call_target="tpu_custom_call" | custom-call | tf_op jit(solution)/shard_map/gather_forward/pallas_call | solution.py:124
  149.4 154.0 %backward_reduce.1 = (bf16[512,1024]{1,0:T(8,128)(2,1)}, bf16[512,1024]{1,0:T(8,128)(2,1)}, bf16[512,1024]{1,0:T(8,128)(2,1)}, bf16[512,2816]{1,0:T(8,128)(2,1)}...) custom-call(s32[512,512]{1,0:T(8,128)} %refs_0_.3, ...), custom_call_target="tpu_custom_call" | custom-call | tf_op jit(solution)/shard_map/backward_reduce/pallas_call | solution.py:124
  303.4 0.0 copy-start
  303.4 1.0 fusion.5
  304.4 0.6 fusion.1
  305.0 0.6 fusion.2
  305.6 0.6 fusion.3
  306.1 0.6 fusion.4
  306.7 0.0 copy-start.7
  306.7 0.0 copy-start.6
  306.7 2.3 copy.39
  309.0 0.0 copy-done
  309.0 0.0 copy-start.5
  309.0 0.0 copy-start.4
  309.0 0.0 copy-start.3
  309.0 0.0 copy-start.2
  309.0 0.0 copy-start.1
  309.1 1.3 copy.40
  310.4 0.0 copy-done.7
  310.4 0.7 copy.41
  311.0 0.0 copy-done.6
  311.0 0.7 copy.42
  311.7 0.0 copy-done.5
  311.7 0.7 copy.43
  312.4 0.0 copy-done.4
  312.4 0.7 copy.44
  313.0 0.0 copy-done.3
  313.0 0.7 copy.45
  313.8 0.0 copy-done.2
  313.8 0.7 copy.46
  314.5 0.0 copy-done.1
  314.5 0.7 copy.47
  (4 shorter events, 0.0 us)
Async XLA Ops:
  303.4 5.6 %copy-start = (f32[512,1024]{1,0:T(8,128)S(1)}, f32[512,1024]{1,0:T(8,128)}, u32[]{:S(2)}) copy-start(f32[512,1024]{1,0:T(8,128)} %get-tuple-element.95) | copy-start | bytes 6291460
  306.7 3.7 %copy-start.7 = (f32[32,1024]{1,0:T(8,128)S(1)}, f32[32,1024]{1,0:T(8,128)}, u32[]{:S(2)}) copy-start(f32[32,1024]{1,0:T(8,128)} %get-tuple-element.98) | copy-start | bytes 393220
  306.7 4.3 %copy-start.6 = (f32[32,1024]{1,0:T(8,128)S(1)}, f32[32,1024]{1,0:T(8,128)}, u32[]{:S(2)}) copy-start(f32[32,1024]{1,0:T(8,128)} %get-tuple-element.99) | copy-start | bytes 393220
  309.0 2.7 copy-start.5
  309.0 3.3 %copy-start.4 = (f32[32,1024]{1,0:T(8,128)S(1)}, f32[32,1024]{1,0:T(8,128)}, u32[]{:S(2)}) copy-start(f32[32,1024]{1,0:T(8,128)} %get-tuple-element.101) | copy-start | bytes 393220
  309.0 4.0 %copy-start.3 = (f32[32,2816]{1,0:T(8,128)S(1)}, f32[32,2816]{1,0:T(8,128)}, u32[]{:S(2)}) copy-start(f32[32,2816]{1,0:T(8,128)} %get-tuple-element.104) | copy-start | bytes 1081348
  309.0 4.7 %copy-start.2 = (f32[32,2816]{1,0:T(8,128)S(1)}, f32[32,2816]{1,0:T(8,128)}, u32[]{:S(2)}) copy-start(f32[32,2816]{1,0:T(8,128)} %get-tuple-element.105) | copy-start | bytes 1081348
  309.0 5.4 %copy-start.1 = (f32[88,1024]{1,0:T(8,128)S(1)}, f32[88,1024]{1,0:T(8,128)}, u32[]{:S(2)}) copy-start(f32[88,1024]{1,0:T(8,128)} %get-tuple-element.106) | copy-start | bytes 1081348

commit v3 on v2

v3 whole, which is shorter than its diff:
```python
import functools
import types

import jax
import jax.numpy as jnp
from jax import lax
from jax.experimental import pallas as pl
from jax.experimental.pallas import tpu as pltpu
from jax.sharding import PartitionSpec as P

MESH = pl.DeviceIdType.MESH
VMEM_LIMIT = 62 << 20
HEADS = 16
HEAD = 64
BUCKETS = 32
EPSILON = 1e-06
NEG_FILL = -1000000000.0
LANES = 128
TILE = 256
CONTRACT_LAST = (((1,), (1,)), ((), ()))
CONTRACT_FIRST = (((0,), (0,)), ((), ()))
BF16, F32, I32 = jnp.bfloat16, jnp.float32, jnp.int32
GELU_SCALE = 0.7978845608028654
GELU_CUBE = 0.044715


def round_up(value, unit):
    return -(-value // unit) * unit


def matmul(left, right):
    return jnp.dot(left, right, preferred_element_type=F32)


def times_trans(left, right):
    return lax.dot_general(left, right, CONTRACT_LAST, preferred_element_type=F32)


def trans_times(left, right):
    return lax.dot_general(left, right, CONTRACT_FIRST, preferred_element_type=F32)


class Plan:
    def __init__(self, wide, narrow):
        self.wide, self.narrow = wide, narrow
        self.bits = [2 << i for i in range(wide.bit_length() - 2)]
        self.chunks = wide // 2
        assert wide == 2 << len(self.bits)


def span(bits):
    out = [0]
    for bit in bits:
        out = out + [member ^ bit for member in out]
    return out


def halves(start, size):
    half = round_up(size // 2, LANES)
    return [(start, half), (start + half, size - half)] if size > 2 * LANES else [(start, size)]


def enter(plan):
    w, n = lax.axis_index("wide"), lax.axis_index("narrow")
    barrier = pltpu.get_barrier_semaphore()
    partners = [(w ^ bit, n) for bit in [1] + plan.bits]
    partners += [(w, lax.rem(n + d, plan.narrow)) for d in range(1, plan.narrow)]
    for partner in partners:
        pl.semaphore_signal(barrier, inc=1, device_id=partner, device_id_type=MESH)
    pl.semaphore_wait(barrier, len(partners))
    return w, n


def loop(low, high, body):
    def step(i, carry):
        body(i)
        return carry

    lax.fori_loop(low, high, step, 0)


def at(index, size):
    return pl.ds(pl.multiple_of(index * size, size), size)


def streamed(low, high, copies, body):
    for copy in copies(lax.rem(low, 2), low):
        copy.start()

    def step(i):
        slot = lax.rem(i, 2)

        @pl.when(i + 1 < high)
        def _():
            for copy in copies(1 - slot, i + 1):
                copy.start()

        for copy in copies(slot, i):
            copy.wait()
        body(i, slot)

    loop(low, high, step)


def run(kernel, inputs, outputs, scratch, resident, scalars, collective_id, name):
    sizes = [len(jax.tree.leaves(tree)) for tree in (inputs, outputs, scratch)]
    forms = [jax.tree.structure(tree) for tree in (inputs, outputs, scratch)]

    def flat(*refs):
        first, second = sizes[0], sizes[0] + sizes[1]
        parts = (refs[:first], refs[first:second], refs[second:])
        kernel(*(types.SimpleNamespace(**form.unflatten(part)) for form, part in zip(forms, parts)))

    def space(key):
        return pltpu.VMEM if key in resident else pltpu.SMEM if key in scalars else pl.ANY

    def specs(tree):
        return jax.tree.leaves(
            {
                key: jax.tree.map(lambda _, key=key: pl.BlockSpec(memory_space=space(key)), value)
                for key, value in tree.items()
            }
        )

    result = pl.pallas_call(
        flat,
        out_shape=jax.tree.leaves(outputs),
        in_specs=specs(inputs),
        out_specs=specs(outputs),
        scratch_shapes=jax.tree.leaves(scratch),
        compiler_params=pltpu.CompilerParams(
            collective_id=collective_id, has_side_effects=True, vmem_limit_bytes=VMEM_LIMIT
        ),
        name=name,
    )(*jax.tree.leaves(inputs))
    return types.SimpleNamespace(**forms[1].unflatten(result))


def sems(*shape):
    return pltpu.SemaphoreType.DMA(shape)


def struct(shape, dtype):
    return jax.ShapeDtypeStruct(shape, dtype)


class Gather:
    def __init__(self, plan, rows, window):
        self.plan, self.rows = plan, rows
        self.start_column, self.columns = window
        self.padded = round_up(self.rows, 16)
        self.aligned = self.padded == self.rows
        self.group = plan.narrow * self.rows
        self.parts = halves(*window)
        self.orders = [plan.bits, plan.bits[::-1]][: len(self.parts)]
        self.chunks = plan.chunks

    def reserve(self):
        count, parts = self.plan.narrow, len(self.parts)
        return [sems(2, count), sems(2, parts, self.chunks), sems(2, parts, self.chunks), sems(2)]

    def stages_out(self):
        return [] if self.aligned else [struct((self.plan.narrow, self.padded, self.columns), BF16)]

    def bind(self, place, shard, out, stage, refs):
        self.w, self.n = place
        self.shard, self.out = shard, out
        self.zsem, self.bsem, self.csem, self.lsem = refs
        if not self.aligned:
            self.stage = stage[0]

    def window(self):
        return pl.ds(self.start_column, self.columns)

    def own_slot(self):
        if self.aligned:
            rows = pl.ds(pl.multiple_of(self.n * self.rows, self.rows), self.rows)
            return self.out.at[self.w, rows, self.window()]
        return self.stage.at[self.n]

    def z_copy(self, d):
        return pltpu.make_async_remote_copy(
            src_ref=self.shard.at[:, self.window()],
            dst_ref=self.own_slot(),
            send_sem=self.zsem.at[0, d],
            recv_sem=self.zsem.at[1, d],
            device_id=(self.w, lax.rem(self.n + d, self.plan.narrow)),
            device_id_type=MESH,
        )

    def place_copy(self):
        return pltpu.make_async_copy(self.shard.at[:, self.window()], self.own_slot(), self.lsem.at[0])

    def pack_group(self, stage, compact):
        copy = pltpu.make_async_copy(self.stage, stage, self.lsem.at[1])
        copy.start()
        copy.wait()
        size, wide = self.group, self.plan.narrow * self.padded
        row = lax.broadcasted_iota(I32, (size, wide), 0)
        column = lax.broadcasted_iota(I32, (size, wide), 1)
        pick = column == (row // self.rows) * self.padded + row % self.rows
        compact[...] = matmul(pick.astype(F32).astype(BF16), stage[...].reshape(wide, self.columns)).astype(BF16)
        copy = pltpu.make_async_copy(compact, self.out.at[self.w, :, self.window()], self.lsem.at[1])
        copy.start()
        copy.wait()

    def start(self):
        for d in range(1, self.plan.narrow):
            self.z_copy(d).start()
        self.place_copy().start()

    def hop(self, sems, part, mask, bit, slot):
        start, size = self.parts[part]
        target = self.out.at[self.w ^ mask, :, pl.ds(start, size)]
        return pltpu.make_async_remote_copy(
            src_ref=target,
            dst_ref=target,
            send_sem=sems.at[0, part, slot],
            recv_sem=sems.at[1, part, slot],
            device_id=(self.w ^ bit, self.n),
            device_id_type=MESH,
        )

    def hops(self, part, stage):
        order = self.orders[part]
        masks = span(order[:stage])
        return [self.hop(self.bsem, part, mask, order[stage], len(masks) + i - 1) for i, mask in enumerate(masks)]

    def core_hops(self, part, stage):
        masks = span(self.orders[part])
        low, high = (0, 1) if stage == 0 else (1 << (stage - 1), 1 << stage)
        return [self.hop(self.csem, part, masks[i], 1, i) for i in range(low, high)]

    def stages(self):
        return len(self.plan.bits) + 2

    def step(self, stage):
        bits, parts = len(self.plan.bits), range(len(self.parts))
        if stage == 0:
            for d in range(1, self.plan.narrow):
                self.z_copy(d).wait_recv()
            self.place_copy().wait()
            if not self.aligned:
                pl.run_scoped(
                    self.pack_group,
                    pltpu.VMEM((self.plan.narrow, self.padded, self.columns), BF16),
                    pltpu.VMEM((self.group, self.columns), BF16),
                )
        elif stage <= bits:
            for part in parts:
                for copy in self.hops(part, stage - 1):
                    copy.wait_recv()
        else:
            for part in parts:
                for s in range(bits + 1):
                    for copy in self.core_hops(part, s):
                        copy.wait_recv()
        if stage < bits:
            for part in parts:
                for copy in self.hops(part, stage):
                    copy.start()
        if stage <= bits:
            for part in parts:
                for copy in self.core_hops(part, stage):
                    copy.start()

    def finish(self):
        for d in range(1, self.plan.narrow):
            self.z_copy(d).wait_send()
        for part in range(len(self.parts)):
            for s in range(len(self.plan.bits)):
                for copy in self.hops(part, s):
                    copy.wait_send()
            for s in range(len(self.plan.bits) + 1):
                for copy in self.core_hops(part, s):
                    copy.wait_send()


class Swap:
    def __init__(self, plan):
        self.plan = plan

    def reserve(self):
        return sems(3, self.plan.chunks)

    def bind(self, place, source, out, sem):
        self.w, self.n = place
        self.source, self.out, self.sem = source, out, sem
        self.both = len(out.shape) == 4
        self.group = source.shape[0] // self.plan.wide

    def chunk(self, index):
        return self.source.at[pl.ds(pl.multiple_of(index * self.group, self.group), self.group), :]

    def local(self, slot):
        return pltpu.make_async_copy(self.chunk(self.w ^ (2 * slot)), self.out.at[0, slot], self.sem.at[2, slot])

    def landing(self, slot):
        return self.out.at[1, slot] if self.both else self.out.at[slot]

    def remote(self, slot, source):
        return pltpu.make_async_remote_copy(
            src_ref=source,
            dst_ref=self.landing(slot),
            send_sem=self.sem.at[0, slot],
            recv_sem=self.sem.at[1, slot],
            device_id=(self.w ^ 1, self.n),
            device_id_type=MESH,
        )

    def send(self, slot):
        return self.remote(slot, self.chunk(self.w ^ 1 ^ (2 * slot)))

    def start(self):
        for slot in range(self.plan.chunks):
            self.send(slot).start()
            if self.both:
                self.local(slot).start()

    def wait_recv(self):
        for slot in range(self.plan.chunks):
            self.remote(slot, self.landing(slot)).wait_recv()

    def finish(self):
        for slot in range(self.plan.chunks):
            self.send(slot).wait_send()
            if self.both:
                self.local(slot).wait()


def to_sibling(place, source, target, sem):
    return pltpu.make_async_remote_copy(
        src_ref=source,
        dst_ref=target,
        send_sem=sem.at[0],
        recv_sem=sem.at[1],
        device_id=(place[0] ^ 1, place[1]),
        device_id_type=MESH,
    )


def column_of(row):
    eye = lax.broadcasted_iota(I32, (LANES, LANES), 0) == lax.broadcasted_iota(I32, (LANES, LANES), 1)
    pieces = [
        jnp.sum(jnp.where(eye, row[:, start : start + LANES], 0.0), axis=1, keepdims=True)
        for start in range(0, row.shape[1], LANES)
    ]
    return jnp.concatenate(pieces, axis=0)


def unpack_small(plan, packed, sizes):
    summed = jnp.sum(packed.astype(F32).reshape(plan.wide, plan.narrow, 16, LANES), axis=1)
    rows = []
    for i, size in enumerate(sizes):
        each = LANES // (size * plan.narrow)
        blocks = [
            sum(summed[first + j, i : i + 1, :] for j in range(each))
            for first in range(0, plan.wide, each)
        ]
        rows.append(jnp.concatenate(blocks, axis=1))
    return rows


def same_bucket(width):
    row = lax.broadcasted_iota(I32, (width, width), 0) // HEADS
    column = lax.broadcasted_iota(I32, (width, width), 1) // HEADS
    return (row == column).astype(F32)


def spread_table(table_row):
    width = BUCKETS * HEADS
    lane = lax.broadcasted_iota(I32, (HEADS, width), 1)
    head = lax.broadcasted_iota(I32, (HEADS, width), 0)
    same = lane % HEADS == head
    picked = jnp.where(same, table_row, 0.0).astype(BF16)
    spread = matmul(picked, same_bucket(width).astype(BF16))
    return jnp.concatenate(
        [jnp.where(same, spread[h : h + 1, :], 0.0).astype(BF16) for h in range(HEADS)], axis=0
    )


def bucket_rows(bucket):
    small = bucket.astype(F32).astype(BF16)
    one, zero = jnp.ones_like(small), jnp.zeros_like(small)
    return jnp.concatenate(
        [jnp.where(small == jnp.asarray(j, BF16), one, zero) for j in range(BUCKETS)], axis=0
    )


class Reduce:
    def __init__(self, plan, rows, window, order):
        self.plan, self.rows = plan, rows
        self.start_column, self.columns = window
        self.padded = round_up(rows, 16)
        self.aligned = self.padded == rows
        self.group = plan.narrow * rows
        self.order = order
        self.chunks = plan.chunks

    def reserve(self):
        count, columns = self.plan.narrow, self.columns
        shapes = [
            sems(2, self.chunks),
            sems(2, count),
            pltpu.VMEM((self.chunks, self.group, columns), BF16),
            pltpu.VMEM((self.chunks - 1, self.group, columns), BF16),
            pltpu.VMEM((count - 1, self.padded, columns), BF16),
        ]
        if not self.aligned:
            shapes.append(pltpu.VMEM((count, self.padded, columns), BF16))
        return shapes

    def bind(self, place, out, refs):
        self.w, self.n = place
        self.out, self.done = out, 0
        self.bsem, self.zsem, self.acc, self.received, self.zreceived = refs[:5]
        if not self.aligned:
            self.stage = refs[5]

    def hops(self, stage):
        bit, masks = self.order[stage], span(self.order[stage + 1 :])
        base = self.chunks - 2 * len(masks)
        return [
            (
                mask >> 1,
                base + k,
                pltpu.make_async_remote_copy(
                    src_ref=self.acc.at[(bit ^ mask) >> 1],
                    dst_ref=self.received.at[base + k],
                    send_sem=self.bsem.at[0, base + k],
                    recv_sem=self.bsem.at[1, base + k],
                    device_id=(self.w ^ bit, self.n),
                    device_id_type=MESH,
                ),
            )
            for k, mask in enumerate(masks)
        ]

    def z_copy(self, d):
        peer = lax.rem(self.n + d, self.plan.narrow)
        source = self.acc.at[0, at(peer, self.rows), :] if self.aligned else self.stage.at[peer]
        return pltpu.make_async_remote_copy(
            src_ref=source,
            dst_ref=self.zreceived.at[d - 1],
            send_sem=self.zsem.at[0, d],
            recv_sem=self.zsem.at[1, d],
            device_id=(self.w, peer),
            device_id_type=MESH,
        )

    def step(self, stage):
        bits = len(self.order)
        if 1 <= stage <= bits:
            for slot, k, copy in self.hops(stage - 1):
                copy.wait_recv()

                def body(j, slot=slot, k=k):
                    block = at(j, 16)
                    self.acc[slot, block, :] += self.received[k, block, :]

                loop(0, self.group // 16, body)
        if stage < bits:
            for _, _, copy in self.hops(stage):
                copy.start()
        elif stage == bits:
            if not self.aligned:
                size, wide = self.group, self.plan.narrow * self.padded
                row = lax.broadcasted_iota(I32, (wide, size), 0)
                column = lax.broadcasted_iota(I32, (wide, size), 1)
                pick = row == (column // self.rows) * self.padded + column % self.rows
                self.stage[...] = (
                    matmul(pick.astype(F32).astype(BF16), self.acc[0]).astype(BF16).reshape(self.stage.shape)
                )
            for d in range(1, self.plan.narrow):
                self.z_copy(d).start()
        else:
            total = self.acc[0, at(self.n, self.rows), :] if self.aligned else self.stage[self.n]
            total = total.astype(F32)
            for d in range(1, self.plan.narrow):
                self.z_copy(d).wait_recv()
                total = total + self.zreceived[d - 1].astype(F32)
            self.out[:, pl.ds(self.start_column, self.columns)] = total[: self.rows]

    def finish(self):
        for stage in range(len(self.order)):
            for _, _, copy in self.hops(stage):
                copy.wait_send()
        for d in range(1, self.plan.narrow):
            self.z_copy(d).wait_send()


class SumAll:
    def __init__(self, plan, shape):
        self.shape = shape
        self.rounds = [(bit, 0) for bit in [1] + plan.bits]
        self.rounds += [(0, 1 << k) for k in range(plan.narrow.bit_length() - 1)]

    def reserve(self):
        count = len(self.rounds)
        return [sems(2, count)] + [pltpu.VMEM((count, *self.shape), F32)] * 2

    def bind(self, place, out, refs):
        self.w, self.n = place
        self.out = out
        self.sem, self.held, self.received = refs

    def copy(self, turn):
        bit, other = self.rounds[turn]
        return pltpu.make_async_remote_copy(
            src_ref=self.held.at[turn],
            dst_ref=self.received.at[turn],
            send_sem=self.sem.at[0, turn],
            recv_sem=self.sem.at[1, turn],
            device_id=(self.w ^ bit, self.n ^ other),
            device_id_type=MESH,
        )

    def start(self, value):
        self.held[0] = value
        self.copy(0).start()

    def step(self, turn):
        self.copy(turn).wait_recv()
        total = self.held[turn] + self.received[turn]
        if turn + 1 < len(self.rounds):
            self.held[turn + 1] = total
            self.copy(turn + 1).start()
        else:
            self.out[...] = total

    def finish(self):
        for turn in range(len(self.rounds)):
            self.copy(turn).wait_send()


class Sizes:
    def __init__(self, plan, rows, width, ff, shards):
        self.plan, self.rows, self.width, self.ff = plan, rows, width, ff
        self.shards = shards
        self.group = plan.narrow * shards[0]
        self.down_group = plan.narrow * shards[DOWN]
        step = round_up(ff // 3, BLOCK)
        self.ff_windows = [(start, min(step, ff - start)) for start in range(0, ff, step)]
        self.half_windows = [(0, width // 2), (width // 2, width // 2)]
        self.blocks = round_up(ff, BLOCK) // BLOCK

    def full(self):
        wide = self.plan.wide
        return (
            [(wide, self.group, self.width)] * 4
            + [(wide, self.group, self.ff)] * 2
            + [(wide, self.down_group, self.width)]
        )


QUERY, KEY, VALUE, OUT, GATE, UP, DOWN = range(7)
BLOCK = 512


class Layer:
    def __init__(self, plan, sizes):
        self.plan, self.sizes = plan, sizes
        whole = (0, sizes.width)
        wide = [(weight, window) for window in sizes.ff_windows for weight in (GATE, UP)]
        down = [(DOWN, window) for window in sizes.half_windows]
        self.order = [(weight, whole) for weight in (QUERY, KEY, VALUE, OUT)] + down + wide
        self.small = Gather(plan, 16, (0, LANES))
        self.items = [self.small] + [Gather(plan, sizes.shards[weight], window) for weight, window in self.order]
        self.swaps = [Swap(plan) for _ in range(4)]
        self.extra = self.small.stages() - 4
        ways = [plan.bits, plan.bits[::-1]]
        self.reduces = []
        for weight in range(7):
            turn = 1 if weight in (UP, KEY, OUT) else 0
            pairs = enumerate(sizes.half_windows)
            if weight in (GATE, UP):
                pairs = [(0, window) for window in sizes.ff_windows]
            self.reduces.append([Reduce(plan, sizes.shards[weight], window, ways[k ^ turn]) for k, window in pairs])
        self.sums = SumAll(plan, (8, sizes.width))

    def call(self, vectors, counts, shards, tokens, patch_keep, text_len, buckets, cotangent):
        plan, s = self.plan, self.sizes
        self.counts = counts
        rows, width, chunks = s.rows, s.width, plan.chunks
        row_block = struct((rows, width), BF16)
        inputs = dict(
            vectors=vectors,
            shards=shards[:DOWN],
            down_shard=shards[DOWN],
            tokens=tokens,
            patch_keep=patch_keep,
            text_len=text_len,
            buckets=buckets,
            cotangent=cotangent,
        )
        outputs = dict(
            small=struct((plan.wide, plan.narrow * 16, LANES), BF16),
            full=[struct(shape, BF16) for shape in s.full()],
            stages=[item.stages_out() for item in self.items],
            qkv=[row_block] * 3,
            prob=struct((HEADS, rows, rows), BF16),
            turned=[struct((2, chunks, s.group, rows), BF16)] * 3,
            hidden_far=struct((chunks, s.down_group, rows), BF16),
            cot_far=row_block,
            far_ff=struct((2, s.blocks, rows, BLOCK), BF16),
            far_out=row_block,
            far_attn=[row_block] * 3,
            result=row_block,
            input_grad=struct((rows, width), F32),
            grads=[
                struct((size, s.ff if weight in (GATE, UP) else width), F32) for weight, size in enumerate(s.shards)
            ],
            sums=struct((8, width), F32),
        )
        square = pltpu.VMEM((rows, width), BF16)
        down_rows = round_up(s.shards[DOWN], 16)
        scratch = dict(
            items=[item.reserve() for item in self.items],
            swaps=[swap.reserve() for swap in self.swaps],
            reduces=[[item.reserve() for item in pair] for pair in self.reduces],
            exchange=self.sums.reserve(),
            direct=sems(2),
            load=sems(len(self.items)),
            pre=sems(8),
            packed=pltpu.VMEM((16, LANES), BF16),
            small=pltpu.VMEM((plan.wide, plan.narrow * 16, LANES), BF16),
            down_shard=pltpu.VMEM((down_rows, width), BF16),
            rows=pltpu.VMEM((8, width), F32),
            keep=pltpu.VMEM((rows, 1), F32),
            big=pltpu.VMEM((HEADS, rows, rows), BF16),
            stream=pltpu.VMEM((rows, width), F32),
            normed=square,
            totals=pltpu.VMEM((8, width), F32),
            pair_sem=sems(2),
            tile_sem=sems(2, 3),
            ff_sem=sems(len(s.ff_windows), 2, 2, 2),
            out_sem=sems(2),
            attn_sem=sems(2, 3, 2),
            store=sems(6),
        )
        return run(
            self.kernel,
            inputs,
            outputs,
            scratch,
            {"vectors", "down_shard", "patch_keep", "cotangent", "grads", "sums"},
            {"text_len"},
            0,
            "layer",
        )

    def kernel(self, i, o, t):
        self.i, self.o, self.t = i, o, t
        plan, s = self.plan, self.sizes
        square = pltpu.VMEM((s.rows, s.width), BF16)
        planes = pltpu.VMEM((2, plan.chunks, s.group, s.rows), BF16)
        weight_space = pltpu.VMEM((plan.wide, s.group, s.width), BF16)
        self.pack()
        self.place = place = enter(plan)
        self.small.bind(place, t.packed, o.small, o.stages[0], t.items[0])
        for item, (weight, _), stage, refs in zip(self.items[1:], self.order, o.stages[1:], t.items[1:]):
            item.bind(place, t.down_shard if weight == DOWN else i.shards[weight], o.full[weight], stage, refs)
        for pair, out, refs in zip(self.reduces, o.grads, t.reduces):
            for item, own in zip(pair, refs):
                item.bind(place, out, own)
        self.sums.bind(place, o.sums, t.exchange)
        self.direct = to_sibling(place, i.cotangent, o.cot_far, t.direct)

        for item in self.items[:3]:
            item.start()
        self.direct.start()
        for turn in range(-self.extra, 4):
            self.tick(turn)
        self.set_up()
        pl.run_scoped(
            self.attention_phase,
            [weight_space] * 3,
            [square] * 4,
            [pltpu.VMEM((s.width, s.rows), BF16)] * 2,
            pltpu.VMEM((2, 2, s.rows, s.rows), BF16),
            pltpu.VMEM((HEADS * 16, BUCKETS * 16), BF16),
            pltpu.VMEM((s.rows, s.rows), I32),
        )
        pl.run_scoped(
            self.feed_phase,
            [pltpu.VMEM((plan.wide, s.group, s.ff_windows[0][1]), BF16)] * 2,
            pltpu.VMEM((s.ff, s.width), BF16),
            pltpu.VMEM((s.ff, s.rows), BF16),
            pltpu.VMEM((plan.chunks, s.down_group, s.rows), BF16),
            square,
            planes,
            pltpu.VMEM((2, 2, s.rows, TILE), BF16),
            sems(plan.wide),
        )
        pl.run_scoped(
            self.back_phase,
            planes,
            [square] * 3,
            pltpu.VMEM((s.rows, s.width), F32),
            square,
        )


    def tick(self, turn):
        stages, turn = self.small.stages(), turn + self.extra
        for stage in range(stages):
            k = turn - stage
            if 0 <= k < len(self.items):
                self.items[k].step(stage)
        if turn + 3 < len(self.items):
            self.items[turn + 3].start()

    def load(self, weight, window, target):
        k = 1 + self.order.index((weight, window))
        return pltpu.make_async_copy(self.o.full[weight].at[:, :, pl.ds(*window)], target, self.t.load.at[k])

    def pack(self):
        i, t = self.i, self.t
        device = lax.axis_index("wide") * self.plan.narrow + lax.axis_index("narrow")
        source = lax.broadcasted_iota(I32, (LANES, LANES), 0)
        lane = lax.broadcasted_iota(I32, (LANES, LANES), 1)
        row = lax.broadcasted_iota(I32, (16, LANES), 0)
        packed, offset = jnp.zeros((16, LANES), F32), 0
        for k, size in enumerate(self.counts):
            first = lax.rem(device * size, LANES)
            pick = (source == offset + lane - first) & (lane >= first) & (lane < first + size)
            found = matmul(i.vectors[...], pick.astype(F32).astype(BF16))
            packed = jnp.where(row == k, found, packed)
            offset += size
        t.packed[...] = packed.astype(BF16)
        size = i.down_shard.shape[0]
        t.down_shard[...] = jnp.concatenate(
            [i.down_shard[...], jnp.zeros((t.down_shard.shape[0] - size, self.sizes.width), BF16)], axis=0
        )

    def set_up(self):
        i, o, t = self.i, self.o, self.t
        copy = pltpu.make_async_copy(o.small, t.small, t.load.at[0])
        copy.start()
        tokens = pltpu.make_async_copy(i.tokens, t.normed, t.pre.at[7])
        tokens.start()
        patches, rows = i.patch_keep.shape[1], self.sizes.rows
        row = lax.broadcasted_iota(I32, (rows, patches), 0)
        lane = lax.broadcasted_iota(I32, (rows, patches), 1)
        kept = jnp.sum(jnp.where(row == lane, i.patch_keep[...].astype(F32), 0.0), axis=1, keepdims=True)
        t.keep[...] = jnp.where(lax.broadcasted_iota(I32, (rows, 1), 0) >= patches, 1.0, kept)
        t.totals[...] = jnp.zeros_like(t.totals)
        copy.wait()
        embed, gain_one, gain_two, table = unpack_small(self.plan, t.small[...], self.counts)
        t.rows[...] = jnp.concatenate([embed, gain_one, gain_two, jnp.zeros((5, self.sizes.width), F32)], axis=0)
        self.table_row = table
        tokens.wait()

        def body(j):
            block = at(j, 64)
            t.stream[block, :] = jnp.where(
                t.keep[block, :] > 0.5, t.normed[block, :].astype(F32), t.rows[0:1, :]
            )

        loop(0, rows // 64, body)
        self.norm(1)

    def norm(self, gain):
        t = self.t

        def body(j):
            block = at(j, 64)
            x = t.stream[block, :]
            scale = lax.rsqrt(jnp.mean(x * x, axis=-1, keepdims=True) + EPSILON)
            t.normed[block, :] = (x * scale * t.rows[gain : gain + 1, :]).astype(BF16)

        loop(0, self.sizes.rows // 64, body)

    def turn(self, source, target):
        def body(j):
            target[at(j, LANES), :] = source[:, at(j, LANES)].T

        loop(0, self.sizes.width // LANES, body)


    def attention_phase(self, held, qkva, turned, prob, table, buckets):
        o, t, s = self.o, self.t, self.sizes
        bucket_copy = pltpu.make_async_copy(self.i.buckets, buckets, t.pre.at[7])
        bucket_copy.start()
        normed, attended, second, _ = self.swaps
        for swap, source, target, sem in zip(
            self.swaps, (turned[0], turned[1], turned[0]), o.turned, t.swaps
        ):
            swap.bind(self.place, source, target, sem)
        store = [pltpu.make_async_copy(qkva[k], o.qkv[k], t.store.at[k]) for k in range(3)]
        whole = (0, s.width)
        loads = [self.load(weight, whole, held[weight % 3]) for weight in (QUERY, KEY, VALUE, OUT)]
        self.turn(t.normed, turned[0])
        normed.start()
        table[...] = spread_table(self.table_row)
        self.tick(4)
        loads[QUERY].start()
        blocks = s.rows // 16
        bucket_copy.wait()
        self.bias(0, blocks // 2, table, buckets)
        self.tick(5)
        loads[KEY].start()
        loads[QUERY].wait()
        self.project(held[0], qkva[0])
        store[0].start()
        self.bias(blocks // 2, blocks, table, buckets)
        self.tick(6)
        loads[VALUE].start()
        loads[KEY].wait()
        self.project(held[1], qkva[1])
        store[1].start()
        self.tick(7)
        loads[OUT].start()
        loads[VALUE].wait()
        self.project(held[2], qkva[2])
        store[2].start()
        count = HEADS // 2
        self.attend(0, count // 4, qkva, prob)
        self.tick(8)
        self.attend(count // 4, 5 * count // 8, qkva, prob)
        self.tick(9)
        self.attend(5 * count // 8, count, qkva, prob)
        for slot in range(2):
            self.prob_copy(slot, count - 2 + slot, prob).wait()
        loads[OUT].wait()

        def body(j):
            block = held[0][:, :, at(j, TILE)].reshape(s.width, TILE)
            t.stream[:, at(j, TILE)] += matmul(qkva[3][...], block)

        loop(0, s.width // TILE, body)
        self.turn(qkva[3], turned[1])
        attended.start()
        normed.finish()
        self.norm(2)
        self.turn(t.normed, turned[0])
        second.start()
        for copy in store:
            copy.wait()
        attended.finish()
        second.finish()

    def bias(self, low, high, table, buckets):
        i, t = self.i, self.t
        live = lax.broadcasted_iota(I32, (1, self.sizes.rows), 1) < i.patch_keep.shape[1] + i.text_len[0]

        def body(j):
            block = at(j, 16)
            spread = matmul(table[...], bucket_rows(buckets[block, :]))
            spread = jnp.where(live, spread, NEG_FILL).astype(BF16)
            t.big[:, block, :] = spread.reshape(HEADS, 16, spread.shape[-1])

        loop(low, high, body)

    def project(self, weight, target):
        def body(j):
            block = weight[:, :, at(j, TILE)].reshape(self.sizes.width, TILE)
            target[:, at(j, TILE)] = matmul(self.t.normed[...], block).astype(BF16)

        loop(0, self.sizes.width // TILE, body)

    def prob_copy(self, slot, pair, prob):
        return pltpu.make_async_copy(prob.at[slot], self.o.prob.at[pl.ds(2 * pair, 2)], self.t.pair_sem.at[slot])

    def attend(self, low, high, qkva, prob):
        t = self.t
        lane = lax.broadcasted_iota(I32, (1, LANES), 1)

        def body(pair):
            columns, slot = at(pair, LANES), lax.rem(pair, 2)

            @pl.when(pair >= 2)
            def _():
                self.prob_copy(slot, pair, prob).wait()

            q, k, v = (ref[:, columns] for ref in qkva[:3])
            mixed = []
            for e in range(2):
                own = jnp.where((lane < HEAD) == (e == 0), q, jnp.zeros_like(q))
                scores = times_trans(own, k) + t.big[2 * pair + e].astype(F32)
                top = jnp.max(scores, axis=-1, keepdims=True)
                powers = jnp.exp(scores - top)
                total = jnp.sum(powers, axis=-1, keepdims=True)
                weights = (powers * (1.0 / total)).astype(BF16)
                prob[slot, e] = weights
                mixed.append(matmul(weights, v))
            qkva[3][:, columns] = jnp.where(lane < HEAD, mixed[0], mixed[1]).astype(BF16)
            self.prob_copy(slot, pair, prob).start()

        loop(low, high, body)


    def feed_phase(self, held, down, hidden, hidden_far, cot_far, planes, far, sem):
        i, o, t, s = self.i, self.o, self.t, self.sizes
        group, windows = s.down_group, s.ff_windows
        copies = [
            pltpu.make_async_copy(o.full[DOWN].at[k], down.at[pl.ds(k * group, group), :], sem.at[k])
            for k in range(self.plan.wide)
        ]
        for copy in copies:
            copy.start()
        swap = self.swaps[3]
        swap.bind(self.place, hidden, o.hidden_far, t.swaps[3])
        planes_copy = pltpu.make_async_copy(o.turned[2], planes, t.pre.at[0])
        self.tick(10)
        for part, window in enumerate(windows):
            loads = [
                self.load(weight, window, held[k].at[:, :, pl.ds(0, window[1])]) for k, weight in enumerate((GATE, UP))
            ]
            loads[0].start()
            self.tick(11 + 2 * part)
            loads[1].start()
            if part == 0:
                for copy in copies:
                    copy.wait()
            if part > 0:
                self.feed_weights(part - 1, planes, far)
            for copy in loads:
                copy.wait()
            self.feed(part, held, down, hidden)
            for copy in self.ff_copies(part):
                copy.start()
            if part == 0:
                self.swaps[2].wait_recv()
                planes_copy.start()
                planes_copy.wait()
            self.tick(12 + 2 * part)
        swap.start()
        for item in self.items:
            item.finish()
        self.direct.wait()
        cot_copy = pltpu.make_async_copy(o.cot_far, cot_far, t.pre.at[1])
        cot_copy.start()
        self.feed_weights(len(windows) - 1, planes, far)
        swap.wait_recv()
        far_copy = pltpu.make_async_copy(o.hidden_far, hidden_far, t.pre.at[2])
        far_copy.start()
        cot_copy.wait()
        far_copy.wait()
        self.down_gradient(hidden, hidden_far, cot_far)
        self.advance(DOWN)
        self.advance(GATE, (0,))
        self.advance(UP, (0,))
        store = pltpu.make_async_copy(cot_far, o.result, t.pre.at[1])

        def finish(j):
            block = at(j, TILE)
            cot_far[:, block] = (t.stream[:, block] + trans_times(hidden[...], down[:, block])).astype(BF16)

        loop(0, s.width // TILE, finish)
        store.start()
        store.wait()
        swap.finish()

    def near(self, which, j):
        return which * self.sizes.blocks + lax.div(j, 2), at(lax.rem(j, 2), TILE)

    def ff_copies(self, part):
        s, t = self.sizes, self.t
        start, size = s.ff_windows[part]
        copies = []
        for which in range(2):
            for k, first in enumerate(range(start, start + size, BLOCK)):
                block, columns = first // BLOCK, pl.ds(0, min(BLOCK, start + size - first))
                copies.append(
                    to_sibling(
                        self.place,
                        t.big.at[which * s.blocks + block, :, columns],
                        self.o.far_ff.at[which, block, :, columns],
                        t.ff_sem.at[part, which, k],
                    )
                )
        return copies

    def feed(self, part, held, down, hidden):
        i, t, s = self.i, self.t, self.sizes
        start, size = s.ff_windows[part]
        first = start // TILE

        def body(j):
            tile, columns = first + j, at(j, TILE)
            gate = matmul(t.normed[...], held[0][:, :, columns].reshape(s.width, TILE))
            up = matmul(t.normed[...], held[1][:, :, columns].reshape(s.width, TILE))
            grad = times_trans(i.cotangent[...], down[at(tile, TILE), :])
            square = gate * gate
            bend = jnp.tanh(GELU_SCALE * gate * (1.0 + GELU_CUBE * square))
            half = 0.5 * (1.0 + bend)
            act = gate * half
            slope = half + (0.5 * GELU_SCALE) * gate * (1.0 - bend * bend) * (1.0 + (3.0 * GELU_CUBE) * square)
            hidden[at(tile, TILE), :] = (act * up).astype(BF16).T
            for which, value in enumerate((grad * up * slope, grad * act)):
                block, lanes = self.near(which, tile)
                t.big[block, :, lanes] = value.astype(BF16)

        loop(0, size // TILE, body)

    def feed_weights(self, part, planes, far):
        o, t, s = self.o, self.t, self.sizes
        start, size = s.ff_windows[part]
        first, rows = start // TILE, self.plan.chunks * s.group
        for copy in self.ff_copies(part):
            copy.wait_recv()

        def far_copies(slot, j):
            return [
                pltpu.make_async_copy(
                    o.far_ff.at[which, lax.div(first + j, 2), :, self.near(which, first + j)[1]],
                    far.at[slot, which],
                    t.tile_sem.at[slot, which],
                )
                for which in range(2)
            ]

        def body(j, slot):
            left = jnp.concatenate([planes[0].reshape(rows, s.rows), planes[1].reshape(rows, s.rows)], axis=1)
            for which, weight in enumerate((GATE, UP)):
                block, lanes = self.near(which, first + j)
                right = jnp.concatenate([t.big[block, :, lanes], far[slot, which]], axis=0)
                acc = self.reduces[weight][part].acc
                acc[:, :, at(j, TILE)] = matmul(left, right).astype(BF16).reshape(self.plan.chunks, s.group, TILE)

        streamed(0, size // TILE, far_copies, body)
        self.advance(GATE, (part,))
        self.advance(UP, (part,))

    def down_gradient(self, hidden, hidden_far, cot_far):
        i, s = self.i, self.sizes
        for part, (start, size) in enumerate(s.half_windows):
            acc = self.reduces[DOWN][part].acc

            def body(slot, acc=acc, start=start, size=size):
                columns = pl.ds(start, size)
                near = hidden[at(self.place[0] ^ (2 * slot), s.down_group), :]
                left = jnp.concatenate([near, hidden_far[slot]], axis=1)
                right = jnp.concatenate([i.cotangent[:, columns], cot_far[:, columns]], axis=0)
                acc[slot] = matmul(left, right).astype(BF16)

            loop(0, self.plan.chunks, body)


    def advance(self, weight, parts=None):
        for part in range(len(self.reduces[weight])) if parts is None else parts:
            item = self.reduces[weight][part]
            item.step(item.done)
            item.done += 1

    def back_phase(self, planes, qkv, back, grad_attended):
        o, t, s = self.o, self.t, self.sizes
        square = pltpu.VMEM((s.rows, s.width), BF16)
        self.swaps[0].wait_recv()
        loads = [
            pltpu.make_async_copy(source, target, t.pre.at[k])
            for k, (source, target) in enumerate(zip([o.turned[0]] + o.qkv, [planes] + qkv))
        ]
        for copy in loads:
            copy.start()
        pl.run_scoped(
            functools.partial(self.middle, back, grad_attended),
            pltpu.VMEM((self.plan.wide, s.group, s.width), BF16),
            pltpu.VMEM((2, self.plan.chunks, s.group, s.rows), BF16),
            square,
        )
        for copy in loads:
            copy.wait()
        pl.run_scoped(
            functools.partial(self.attention_back, planes, qkv, back, grad_attended),
            [square] * 3,
            pltpu.VMEM((3, s.rows, s.width // 2), BF16),
        )

    def middle(self, back, grad_attended, weight, planes, grad_mid):
        o, t, s = self.o, self.t, self.sizes
        self.swaps[1].wait_recv()
        loads = [
            pltpu.make_async_copy(o.full[OUT], weight, t.pre.at[4]),
            pltpu.make_async_copy(o.turned[1], planes, t.pre.at[5]),
        ]
        for copy in loads:
            copy.start()
        groups = TILE // s.group
        pl.run_scoped(
            functools.partial(self.feed_input, back), pltpu.VMEM((2, 2, groups, s.group, s.ff), BF16)
        )
        for part in range(len(s.ff_windows)):
            for copy in self.ff_copies(part):
                copy.wait_send()
        self.norm_back(2, back, grad_mid)
        out_copy = to_sibling(self.place, grad_mid, o.far_out, t.out_sem)
        out_copy.start()
        self.advance(GATE, (1,))
        self.advance(UP, (1,))
        for copy in loads:
            copy.wait()
        pl.run_scoped(
            functools.partial(self.out_back, out_copy, weight, planes, grad_mid, grad_attended),
            pltpu.VMEM((s.rows, s.width), BF16),
        )
        self.advance(GATE, (0,))
        self.advance(UP, (0,))
        out_copy.wait_send()

    def attention_back(self, planes, qkv, back, grad_attended, grad_qkv, far):
        i, o, t, s, plan = self.i, self.o, self.t, self.sizes, self.plan
        self.grad_qkv = grad_qkv
        prob_space = pltpu.VMEM((2, 2, s.rows, s.rows), BF16)
        half = HEADS // 4
        tokens = pltpu.make_async_copy(i.tokens, t.normed, t.pre.at[7])
        tokens.start()
        pl.run_scoped(functools.partial(self.attend_back, 0, half, qkv, grad_attended), prob_space)
        self.send_attention(0)
        self.advance(GATE, (2,))
        self.advance(UP, (2,))
        self.advance(DOWN)
        self.attention_weights(0, planes, far)
        self.advance(GATE, (0, 1))
        self.advance(UP, (0, 1))
        pl.run_scoped(functools.partial(self.attend_back, half, 2 * half, qkv, grad_attended), prob_space)
        self.send_attention(1)
        self.advance(OUT)
        self.advance(GATE, (2,))
        self.advance(UP, (2,))
        self.advance(DOWN)
        self.attention_weights(1, planes, far)
        for weight in (QUERY, KEY, VALUE):
            self.advance(weight, (0,))
        groups = TILE // s.group
        pl.run_scoped(
            functools.partial(self.attention_input, back), pltpu.VMEM((2, 3, groups, s.group, s.width), BF16)
        )
        self.advance(OUT)
        for weight in (QUERY, KEY, VALUE):
            self.advance(weight, (1,))
        tokens.wait()
        self.norm_back(1, back, None)
        store = pltpu.make_async_copy(t.stream, o.input_grad, t.pre.at[0])
        store.start()
        for weight in (QUERY, KEY, VALUE):
            self.advance(weight, (0,))
        self.table_back()
        self.sums.start(t.totals[...])
        for weight in (QUERY, KEY, VALUE):
            self.advance(weight, (1,))
        turn, last = 0, len(plan.bits) + 1
        left = [(weight, part) for weight in (GATE, UP, DOWN, OUT) for part in range(len(self.reduces[weight]))]
        left += [(weight, part) for part in range(2) for weight in (QUERY, KEY, VALUE)]
        while left:
            for weight, part in list(left):
                if self.reduces[weight][part].done > last:
                    left.remove((weight, part))
                    continue
                self.advance(weight, (part,))
                if turn % 2 == 1 and turn // 2 < len(self.sums.rounds):
                    self.sums.step(turn // 2)
                turn += 1
        for k in range(turn // 2, len(self.sums.rounds)):
            self.sums.step(k)
        store.wait()
        for part in range(2):
            for copy in self.attention_copies(part):
                copy.wait_send()
        for pair in self.reduces:
            for item in pair:
                item.finish()
        self.sums.finish()

    def feed_input(self, back, held):
        o, t, s = self.o, self.t, self.sizes
        groups = TILE // s.group
        last = s.ff - BLOCK * (s.blocks - 1)

        def weight_copies(slot, j):
            return [
                pltpu.make_async_copy(
                    o.full[weight].at[pl.ds(j * groups, groups)], held.at[slot, which], t.tile_sem.at[slot, which]
                )
                for which, weight in enumerate((GATE, UP))
            ]

        def body(j, slot):
            total = None
            for which in range(2):
                first = which * s.blocks
                near = [t.big[first + k] for k in range(s.blocks - 1)]
                near.append(t.big[first + s.blocks - 1, :, pl.ds(0, last)])
                found = times_trans(jnp.concatenate(near, axis=1), held[slot, which].reshape(TILE, s.ff))
                total = found if total is None else total + found
            back[:, at(j, TILE)] = total

        streamed(0, s.width // TILE, weight_copies, body)

    def norm_back(self, which, back, grad_mid):
        i, t, s = self.i, self.t, self.sizes

        def body(j):
            block = at(j, 64)
            kept = t.keep[block, :] > 0.5
            grad = back[block, :]
            if which == 2:
                x = t.stream[block, :]
                before = i.cotangent[block, :].astype(F32)
            else:
                x = jnp.where(kept, t.normed[block, :].astype(F32), t.rows[0:1, :])
                before = t.stream[block, :]
            scale = lax.rsqrt(jnp.mean(x * x, axis=-1, keepdims=True) + EPSILON)
            scaled = x * scale
            u = grad * t.rows[which : which + 1, :]
            inner = jnp.mean(u * scaled, axis=-1, keepdims=True)
            total = before + scale * (u - scaled * inner)
            t.totals[which : which + 1, :] += jnp.sum(grad * scaled, axis=0, keepdims=True)
            if which == 2:
                t.stream[block, :] = total
                grad_mid[block, :] = total.astype(BF16)
            else:
                t.stream[block, :] = jnp.where(kept, total, 0.0)
                t.totals[0:1, :] += jnp.sum(jnp.where(kept, 0.0, total), axis=0, keepdims=True)

        loop(0, s.rows // 64, body)

    def out_back(self, out_copy, weight, planes, grad_mid, grad_attended, far):
        o, t, s = self.o, self.t, self.sizes
        groups = TILE // s.group

        def attended(j):
            block = weight[pl.ds(j * groups, groups)].reshape(TILE, s.width)
            grad_attended[:, at(j, TILE)] = times_trans(grad_mid[...], block).astype(BF16)

        loop(0, s.width // TILE, attended)
        out_copy.wait_recv()
        load = pltpu.make_async_copy(o.far_out, far, t.pre.at[6])
        load.start()
        load.wait()
        rows = self.plan.chunks * s.group
        for part, (start, size) in enumerate(s.half_windows):
            columns = pl.ds(start, size)
            left = jnp.concatenate([planes[0].reshape(rows, s.rows), planes[1].reshape(rows, s.rows)], axis=1)
            right = jnp.concatenate([grad_mid[:, columns], far[:, columns]], axis=0)
            acc = self.reduces[OUT][part].acc
            acc[...] = matmul(left, right).astype(BF16).reshape(acc.shape)
            self.advance(OUT, (part,))

    def attend_back(self, low, high, qkv, grad_attended, prob):
        o, t = self.o, self.t
        lane = lax.broadcasted_iota(I32, (1, LANES), 1)

        def prob_copies(slot, pair):
            return [pltpu.make_async_copy(o.prob.at[pl.ds(2 * pair, 2)], prob.at[slot], t.tile_sem.at[slot, 0])]

        def body(pair, slot):
            columns = at(pair, LANES)
            q, k, v = (ref[:, columns] for ref in qkv)
            grad = grad_attended[:, columns]
            found = [[], [], []]
            for e in range(2):
                own = jnp.where((lane < HEAD) == (e == 0), grad, jnp.zeros_like(grad))
                weights = prob[slot, e]
                wide = weights.astype(F32)
                grad_prob = times_trans(own, v)
                delta = jnp.sum(grad_prob * wide, axis=-1, keepdims=True)
                scores = (wide * (grad_prob - delta)).astype(BF16)
                t.big[2 * pair + e] = scores
                found[0].append(matmul(scores, k))
                found[1].append(trans_times(scores, q))
                found[2].append(trans_times(weights, grad))
            for ref, (first, second) in zip(self.grad_qkv, found):
                ref[:, columns] = jnp.where(lane < HEAD, first, second).astype(BF16)

        streamed(low, high, prob_copies, body)

    def attention_copies(self, part):
        window = pl.ds(*self.sizes.half_windows[part])
        return [
            to_sibling(
                self.place,
                self.grad_qkv[which].at[:, window],
                self.o.far_attn[which].at[:, window],
                self.t.attn_sem.at[part, which],
            )
            for which in range(3)
        ]

    def send_attention(self, part):
        for copy in self.attention_copies(part):
            copy.start()

    def attention_weights(self, part, planes, far):
        o, t, s = self.o, self.t, self.sizes
        columns = pl.ds(*s.half_windows[part])
        rows = self.plan.chunks * s.group
        loads = []
        for which, copy in enumerate(self.attention_copies(part)):
            copy.wait_recv()
            loads.append(pltpu.make_async_copy(o.far_attn[which].at[:, columns], far.at[which], t.pre.at[which]))
            loads[-1].start()
        for which in range(3):
            loads[which].wait()
            left = jnp.concatenate([planes[0].reshape(rows, s.rows), planes[1].reshape(rows, s.rows)], axis=1)
            right = jnp.concatenate([self.grad_qkv[which][:, columns], far[which]], axis=0)
            acc = self.reduces[which][part].acc
            acc[...] = matmul(left, right).astype(BF16).reshape(acc.shape)
            self.advance(which, (part,))

    def attention_input(self, back, held):
        o, t, s = self.o, self.t, self.sizes
        groups = TILE // s.group

        def weight_copies(slot, j):
            return [
                pltpu.make_async_copy(
                    o.full[which].at[pl.ds(j * groups, groups)], held.at[slot, which], t.tile_sem.at[slot, which]
                )
                for which in range(3)
            ]

        def body(j, slot):
            back[:, at(j, TILE)] = sum(
                times_trans(self.grad_qkv[which][...], held[slot, which].reshape(TILE, s.width)) for which in range(3)
            )

        streamed(0, s.width // TILE, weight_copies, body)

    def table_back(self):
        i, t, s = self.i, self.t, self.sizes
        width, step = BUCKETS * HEADS, 4

        def count(total, buckets):
            copy = pltpu.make_async_copy(i.buckets, buckets, t.pre.at[7])
            copy.start()
            total[...] = jnp.zeros_like(total)
            copy.wait()

            def body(j):
                left, right = [], []
                for k in range(step):
                    block = at(j * step + k, 16)
                    left.append(bucket_rows(buckets[block, :]))
                    right.append(t.big[:, block, :].reshape(HEADS * 16, s.rows))
                total[...] += times_trans(jnp.concatenate(left, axis=1), jnp.concatenate(right, axis=1))

            loop(0, s.rows // (16 * step), body)
            found = total[...].T
            row = lax.broadcasted_iota(I32, found.shape, 0)
            lane = lax.broadcasted_iota(I32, found.shape, 1)
            found = jnp.where(row % 16 == lane % 16, found, 0.0)
            by_head = jnp.sum(found.reshape(HEADS, 16, width), axis=1)
            summed = jnp.dot(
                by_head, same_bucket(width), precision=lax.Precision.HIGHEST, preferred_element_type=F32
            )
            head = lax.broadcasted_iota(I32, summed.shape, 0)
            lane = lax.broadcasted_iota(I32, summed.shape, 1)
            t.totals[3:4, :width] = jnp.sum(jnp.where(lane % HEADS == head, summed, 0.0), axis=0, keepdims=True)

        pl.run_scoped(count, pltpu.VMEM((width, HEADS * 16), F32), pltpu.VMEM((s.rows, s.rows), I32))


def per_device(
    plan,
    tokens,
    patch_keep,
    text_len,
    buckets,
    mask_embed,
    norm_attn,
    w_query,
    w_key,
    w_value,
    w_out,
    bias_table,
    norm_ffn,
    w_gate,
    w_up,
    w_down,
    cotangent,
):
    rows, width = tokens.shape
    assert patch_keep.shape[0] == 1
    device = lax.axis_index("wide") * plan.narrow + lax.axis_index("narrow")
    small = (mask_embed, norm_attn, norm_ffn, bias_table)
    counts = [member.shape[0] for member in small]
    vectors = jnp.concatenate(list(small) + [jnp.zeros((LANES - sum(counts),), BF16)]).reshape(1, LANES)
    weights = (w_query, w_key, w_value, w_out, w_gate, w_up, w_down)
    shards = [jnp.pad(weight, ((0, -weight.shape[0] % 16), (0, 0))) for weight in weights[:DOWN]] + [w_down]
    sizes = Sizes(plan, rows, width, w_gate.shape[1], [weight.shape[0] for weight in weights])
    f = Layer(plan, sizes).call(vectors, counts, shards, tokens, patch_keep, text_len, buckets, cotangent)

    def own(row, size):
        return lax.dynamic_slice(f.sums[row], (device * size,), (size,))

    query, key, value, out, gate, up, down = f.grads
    return (
        f.result,
        f.input_grad,
        own(0, mask_embed.shape[0]),
        own(1, norm_attn.shape[0]),
        query,
        key,
        value,
        out,
        own(3, bias_table.shape[0]),
        own(2, norm_ffn.shape[0]),
        gate,
        up,
        down,
    )


def solution(mesh):
    rows, flat = P(("wide", "narrow"), None), P(("wide", "narrow"))
    plan = Plan(mesh.shape["wide"], mesh.shape["narrow"])
    return jax.shard_map(
        functools.partial(per_device, plan),
        mesh=mesh,
        in_specs=(rows, rows, flat, rows, flat, flat, rows, rows, rows, rows, flat, flat, rows, rows, rows, rows),
        out_specs=(rows, rows, flat, flat, rows, rows, rows, rows, flat, flat, rows, rows, rows),
        check_vma=False,
    )
```

time: 316 us -> 288 us (0.911)
  Pallas kernels: 294 us -> 270 us
  local copies, waits for them, and re-layouts: 18.8 us -> 14.4 us
    pallas_call x2 -> x1, Pallas kernels: 294 us -> 270 us  [run(): pl.pallas_call(flat, out_shape=jax.tree.leaves(outputs), in_specs=specs(i...]
    another operation x11 -> x1, local copies, waits for them, and re-layouts: 4.18 us -> 0.01 us  [the longest x8 2.99 us: pack_small(): jnp.tile(vector, LANES // size)]
where the time goes in v3:
time: 288 us; the launch traced here: 286 us
  Pallas kernels  270 us (94%)
  local copies, waits for them, and re-layouts  14.4 us (5%)
    pallas_call x1, Pallas kernels, run(): pl.pallas_call(flat, out_shape=jax.tree.leaves(outputs), in_specs=specs(i...  270 us
    unnamed x25, local copies, waits for them, and re-layouts  8.44 us

profile of v3, /device:TPU:0, one launch (start us, length us, event | category | flops | bytes accessed | tf_op | source)
XLA Modules:
  0.0 286.1 jit_solution(12744666825032307235)
XLA Ops:
  1.3 3.3 %concatenate.3 = bf16[128]{0:T(256)(128)(2,1)} concatenate(bf16[32]{0:T(256)(128)(2,1)} %param.20, bf16[32]{0:T(256)(128)(2,1)} %param.21, bf16[32]{0:T(256)(128)(2,1)} %param.27, bf16[16]{0:T(256)(128)(2,1)} %param.26, bf16[16]{0:T(256)(128)(2,1)S(1)} %broadcast.3), dimensions={0} | concatenate | bytes 512 | tf_op jit(solution)/shard_map/concatenate | solution.py:1379
  4.6 270.3 %layer.1 = (bf16[512,1024]{1,0:T(8,128)(2,1)}, bf16[512,1024]{1,0:T(8,128)(2,1)}, bf16[512,1024]{1,0:T(8,128)(2,1)}, bf16[512,1024]{1,0:T(8,128)(2,1)}, bf16[2,6...) custom-call(s32[512,512]{1,0:T(8,128)} %refs_0_.1, ...), custom_call_target="tpu_custom_call" | custom-call | tf_op jit(solution)/shard_map/layer/pallas_call | solution.py:125
  274.9 0.0 copy-start
  274.9 1.0 fusion.4
  275.9 0.6 fusion
  276.5 0.6 fusion.2
  277.1 0.6 fusion.3
  277.6 2.3 copy.39
  279.9 0.0 copy-done
  279.9 0.0 copy-start.7
  279.9 0.0 copy-start.6
  279.9 0.0 copy-start.5
  279.9 0.0 copy-start.4
  279.9 0.0 copy-start.3
  279.9 0.0 copy-start.2
  279.9 1.3 copy.40
  281.3 0.0 copy-done.7
  281.3 0.0 copy-start.1
  281.3 0.7 copy.41
  281.9 0.0 copy-done.6
  281.9 0.7 copy.42
  282.6 0.0 copy-done.5
  282.6 0.7 copy.43
  283.2 0.0 copy-done.4
  283.2 0.7 copy.44
  283.9 0.0 copy-done.3
  283.9 0.7 copy.45
  284.6 0.0 copy-done.2
  284.6 0.7 copy.46
  285.4 0.0 copy-done.1
  285.4 0.7 copy.47
  (1 shorter events, 0.0 us)
Async XLA Ops:
  274.9 5.0 %copy-start = (f32[512,1024]{1,0:T(8,128)S(1)}, f32[512,1024]{1,0:T(8,128)}, u32[]{:S(2)}) copy-start(f32[512,1024]{1,0:T(8,128)} %get-tuple-element.53) | copy-start | bytes 6291460
  279.9 1.4 copy-start.7
  279.9 2.0 copy-start.6
  279.9 2.7 copy-start.5
  279.9 3.3 %copy-start.4 = (f32[32,1024]{1,0:T(8,128)S(1)}, f32[32,1024]{1,0:T(8,128)}, u32[]{:S(2)}) copy-start(f32[32,1024]{1,0:T(8,128)} %get-tuple-element.59) | copy-start | bytes 393220
  279.9 4.0 %copy-start.3 = (f32[32,2816]{1,0:T(8,128)S(1)}, f32[32,2816]{1,0:T(8,128)}, u32[]{:S(2)}) copy-start(f32[32,2816]{1,0:T(8,128)} %get-tuple-element.62) | copy-start | bytes 1081348
  279.9 4.7 %copy-start.2 = (f32[32,2816]{1,0:T(8,128)S(1)}, f32[32,2816]{1,0:T(8,128)}, u32[]{:S(2)}) copy-start(f32[32,2816]{1,0:T(8,128)} %get-tuple-element.63) | copy-start | bytes 1081348
  281.3 4.1 %copy-start.1 = (f32[88,1024]{1,0:T(8,128)S(1)}, f32[88,1024]{1,0:T(8,128)}, u32[]{:S(2)}) copy-start(f32[88,1024]{1,0:T(8,128)} %get-tuple-element.64) | copy-start | bytes 1081348

commit v4 on v3

--- a/solution.py
+++ b/solution.py
@@ -129,7 +129,7 @@
         out_specs=specs(outputs),
         scratch_shapes=jax.tree.leaves(scratch),
         compiler_params=pltpu.CompilerParams(
-            collective_id=collective_id, has_side_effects=True, vmem_limit_bytes=VMEM_LIMIT
+            collective_id=collective_id, has_side_effects=collective_id is not None, vmem_limit_bytes=VMEM_LIMIT
         ),
         name=name,
     )(*jax.tree.leaves(inputs))
@@ -815,11 +815,11 @@
         self.project(held[2], qkva[2])
         store[2].start()
         count = HEADS // 2
-        self.attend(0, count // 4, qkva, prob)
+        self.attend(0, 3 * count // 8, qkva, prob)
         self.tick(8)
-        self.attend(count // 4, 5 * count // 8, qkva, prob)
+        self.attend(3 * count // 8, 6 * count // 8, qkva, prob)
         self.tick(9)
-        self.attend(5 * count // 8, count, qkva, prob)
+        self.attend(6 * count // 8, count, qkva, prob)
         for slot in range(2):
             self.prob_copy(slot, count - 2 + slot, prob).wait()
         loads[OUT].wait()
@@ -1352,6 +1352,41 @@
         pl.run_scoped(count, pltpu.VMEM((width, HEADS * 16), F32), pltpu.VMEM((s.rows, s.rows), I32))
 
 
+def hand_out(plan, large, sums, counts):
+    def kernel(i, o, t):
+        takes = [pltpu.make_async_copy(*pair, t.take.at[k]) for k, pair in enumerate(zip(i.large, t.held))]
+        gives = [pltpu.make_async_copy(*pair, t.give.at[k]) for k, pair in enumerate(zip(t.held, o.large))]
+        for copy in takes:
+            copy.start()
+        device = lax.axis_index("wide") * plan.narrow + lax.axis_index("narrow")
+        width = i.sums.shape[1]
+        source = lax.broadcasted_iota(I32, (width, LANES), 0)
+        lane = lax.broadcasted_iota(I32, (width, LANES), 1)
+        for row, (size, target) in enumerate(zip(counts, o.owned)):
+            pick = (source == device * size + lane).astype(F32)
+            found = jnp.dot(
+                i.sums[...], pick, precision=lax.Precision.HIGHEST, preferred_element_type=F32
+            )
+            target[...] = found[row : row + 1, :size]
+        for take, give in zip(takes, gives):
+            take.wait()
+            give.start()
+        for copy in gives:
+            copy.wait()
+
+    done = run(
+        kernel,
+        dict(large=large, sums=sums),
+        dict(large=[struct(x.shape, x.dtype) for x in large], owned=[struct((1, size), F32) for size in counts]),
+        dict(take=sems(len(large)), give=sems(len(large)), held=[pltpu.VMEM(x.shape, x.dtype) for x in large]),
+        {"sums", "owned"},
+        set(),
+        None,
+        "hand_out",
+    )
+    return done.large, done.owned
+
+
 def per_device(
     plan,
     tokens,
@@ -1376,27 +1411,30 @@
     device = lax.axis_index("wide") * plan.narrow + lax.axis_index("narrow")
     small = (mask_embed, norm_attn, norm_ffn, bias_table)
     counts = [member.shape[0] for member in small]
-    vectors = jnp.concatenate(list(small) + [jnp.zeros((LANES - sum(counts),), BF16)]).reshape(1, LANES)
+    starts = [sum(counts[:k]) for k in range(len(counts))]
+    vectors = sum(
+        jnp.pad(member.reshape(1, -1), ((0, 0), (start, LANES - start - member.shape[0])))
+        for start, member in zip(starts, small)
+    )
     weights = (w_query, w_key, w_value, w_out, w_gate, w_up, w_down)
     shards = [jnp.pad(weight, ((0, -weight.shape[0] % 16), (0, 0))) for weight in weights[:DOWN]] + [w_down]
     sizes = Sizes(plan, rows, width, w_gate.shape[1], [weight.shape[0] for weight in weights])
     f = Layer(plan, sizes).call(vectors, counts, shards, tokens, patch_keep, text_len, buckets, cotangent)
 
-    def own(row, size):
-        return lax.dynamic_slice(f.sums[row], (device * size,), (size,))
-
-    query, key, value, out, gate, up, down = f.grads
+    large = [f.result, f.input_grad] + f.grads
+    (result, input_grad, query, key, value, out, gate, up, down), owned = hand_out(plan, large, f.sums, counts)
+    embed, gain_one, gain_two, table = (part.reshape(-1) for part in owned)
     return (
-        f.result,
-        f.input_grad,
-        own(0, mask_embed.shape[0]),
-        own(1, norm_attn.shape[0]),
+        result,
+        input_grad,
+        embed,
+        gain_one,
         query,
         key,
         value,
         out,
-        own(3, bias_table.shape[0]),
-        own(2, norm_ffn.shape[0]),
+        table,
+        gain_two,
         gate,
         up,
         down,

time: 288 us -> 279 us (0.969)
  local copies, waits for them, and re-layouts: 14.4 us -> 0 us
  Pallas kernels: 270 us -> 274 us
    unnamed x25 -> x0, local copies, waits for them, and re-layouts: 8.44 us -> none
    pallas_call x1 -> x2, Pallas kernels: 270 us -> 274 us  [run(): pl.pallas_call(flat, out_shape=jax.tree.leaves(outputs), in_specs=specs(i...]
    concatenate x1 -> x0, local copies, waits for them, and re-layouts: 3.28 us -> none  [per_device(): jnp.concatenate(list(small) + [jnp.zeros((LANES - sum(counts),), BF16)])]
where the time goes in v4:
time: 279 us; the launch traced here: 277 us
  Pallas kernels  274 us (98%)
    pallas_call x2, Pallas kernels, run(): pl.pallas_call(flat, out_shape=jax.tree.leaves(outputs), in_specs=specs(i...  274 us

profile of v4, /device:TPU:0, one launch (start us, length us, event | category | flops | bytes accessed | tf_op | source)
XLA Modules:
  0.0 277.0 jit_solution(10079322551019466872)
XLA Ops:
  1.3 1.3 pad_add_fusion.refs_12_
  2.6 269.1 %layer.1 = (bf16[512,1024]{1,0:T(8,128)(2,1)}, bf16[512,1024]{1,0:T(8,128)(2,1)}, bf16[512,1024]{1,0:T(8,128)(2,1)}, bf16[512,1024]{1,0:T(8,128)(2,1)}, bf16[2,6...) custom-call(s32[512,512]{1,0:T(8,128)} %refs_0_.1, ...), custom_call_target="tpu_custom_call" | custom-call | tf_op jit(solution)/shard_map/layer/pallas_call | solution.py:125
  271.7 5.2 %hand_out.1 = (bf16[512,1024]{1,0:T(8,128)(2,1)}, f32[512,1024]{1,0:T(8,128)}, f32[32,1024]{1,0:T(8,128)}, f32[32,1024]{1,0:T(8,128)}, f32[32,1024]{1,0:T(8,128)...) custom-call(bf16[512,1024]{1,0:T(8,128)(2,1)} %get-tuple-element.36., ...), custom_call_target="tpu_custom_call" | custom-call | tf_op jit(solution)/shard_map/hand_out/pallas_call | solution.py:125

commit v5 on v4

--- a/solution.py
+++ b/solution.py
@@ -83,14 +83,16 @@
     return pl.ds(pl.multiple_of(index * size, size), size)
 
 
-def streamed(low, high, copies, body):
-    for copy in copies(lax.rem(low, 2), low):
-        copy.start()
+def streamed(low, high, copies, body, first=None, last=None):
+    first, last = low if first is None else first, high if last is None else last
+    if low == first:
+        for copy in copies(lax.rem(low, 2), low):
+            copy.start()
 
     def step(i):
         slot = lax.rem(i, 2)
 
-        @pl.when(i + 1 < high)
+        @pl.when(i + 1 < last)
         def _():
             for copy in copies(1 - slot, i + 1):
                 copy.start()
@@ -666,7 +668,7 @@
         self.sums.bind(place, o.sums, t.exchange)
         self.direct = to_sibling(place, i.cotangent, o.cot_far, t.direct)
 
-        for item in self.items[:3]:
+        for item in self.items[:2]:
             item.start()
         self.direct.start()
         for turn in range(-self.extra, 4):
@@ -707,8 +709,8 @@
             k = turn - stage
             if 0 <= k < len(self.items):
                 self.items[k].step(stage)
-        if turn + 3 < len(self.items):
-            self.items[turn + 3].start()
+        if turn + 2 < len(self.items):
+            self.items[turn + 2].start()
 
     def load(self, weight, window, target):
         k = 1 + self.order.index((weight, window))
@@ -829,6 +831,7 @@
             t.stream[:, at(j, TILE)] += matmul(qkva[3][...], block)
 
         loop(0, s.width // TILE, body)
+        self.tick(10)
         self.turn(qkva[3], turned[1])
         attended.start()
         normed.finish()
@@ -902,7 +905,6 @@
         swap = self.swaps[3]
         swap.bind(self.place, hidden, o.hidden_far, t.swaps[3])
         planes_copy = pltpu.make_async_copy(o.turned[2], planes, t.pre.at[0])
-        self.tick(10)
         for part, window in enumerate(windows):
             loads = [
                 self.load(weight, window, held[k].at[:, :, pl.ds(0, window[1])]) for k, weight in enumerate((GATE, UP))
@@ -1052,10 +1054,8 @@
             pltpu.make_async_copy(source, target, t.pre.at[k])
             for k, (source, target) in enumerate(zip([o.turned[0]] + o.qkv, [planes] + qkv))
         ]
-        for copy in loads:
-            copy.start()
         pl.run_scoped(
-            functools.partial(self.middle, back, grad_attended),
+            functools.partial(self.middle, loads, back, grad_attended),
             pltpu.VMEM((self.plan.wide, s.group, s.width), BF16),
             pltpu.VMEM((2, self.plan.chunks, s.group, s.rows), BF16),
             square,
@@ -1068,18 +1068,16 @@
             pltpu.VMEM((3, s.rows, s.width // 2), BF16),
         )
 
-    def middle(self, back, grad_attended, weight, planes, grad_mid):
+    def middle(self, later, back, grad_attended, weight, planes, grad_mid):
         o, t, s = self.o, self.t, self.sizes
         self.swaps[1].wait_recv()
         loads = [
             pltpu.make_async_copy(o.full[OUT], weight, t.pre.at[4]),
             pltpu.make_async_copy(o.turned[1], planes, t.pre.at[5]),
         ]
-        for copy in loads:
-            copy.start()
         groups = TILE // s.group
         pl.run_scoped(
-            functools.partial(self.feed_input, back), pltpu.VMEM((2, 2, groups, s.group, s.ff), BF16)
+            functools.partial(self.feed_input, loads + later, back), pltpu.VMEM((2, 2, groups, s.group, s.ff), BF16)
         )
         for part in range(len(s.ff_windows)):
             for copy in self.ff_copies(part):
@@ -1163,7 +1161,7 @@
                 item.finish()
         self.sums.finish()
 
-    def feed_input(self, back, held):
+    def feed_input(self, loads, back, held):
         o, t, s = self.o, self.t, self.sizes
         groups = TILE // s.group
         last = s.ff - BLOCK * (s.blocks - 1)
@@ -1186,7 +1184,9 @@
                 total = found if total is None else total + found
             back[:, at(j, TILE)] = total
 
-        streamed(0, s.width // TILE, weight_copies, body)
+        for copy in weight_copies(0, 0) + loads:
+            copy.start()
+        streamed(0, s.width // TILE, weight_copies, body, first=-1)
 
     def norm_back(self, which, back, grad_mid):
         i, t, s = self.i, self.t, self.sizes

time: 279 us -> 276 us (0.989)
  no operation moved by 1% of the time
where the time goes in v5:
time: 276 us
  Pallas kernels  273 us (99%)
    pallas_call x2, Pallas kernels, run(): pl.pallas_call(flat, out_shape=jax.tree.leaves(outputs), in_specs=specs(i...  273 us

profile of v5, /device:TPU:0, one launch (start us, length us, event | category | flops | bytes accessed | tf_op | source)
XLA Modules:
  0.0 275.6 jit_solution(2100935607768664773)
XLA Ops:
  1.3 1.3 pad_add_fusion.refs_12_
  2.6 267.6 %layer.1 = (bf16[512,1024]{1,0:T(8,128)(2,1)}, bf16[512,1024]{1,0:T(8,128)(2,1)}, bf16[512,1024]{1,0:T(8,128)(2,1)}, bf16[512,1024]{1,0:T(8,128)(2,1)}, bf16[2,6...) custom-call(s32[512,512]{1,0:T(8,128)} %refs_0_.1, ...), custom_call_target="tpu_custom_call" | custom-call | tf_op jit(solution)/shard_map/layer/pallas_call | solution.py:127
  270.2 5.2 %hand_out.1 = (bf16[512,1024]{1,0:T(8,128)(2,1)}, f32[512,1024]{1,0:T(8,128)}, f32[32,1024]{1,0:T(8,128)}, f32[32,1024]{1,0:T(8,128)}, f32[32,1024]{1,0:T(8,128)...) custom-call(bf16[512,1024]{1,0:T(8,128)(2,1)} %get-tuple-element.36., ...), custom_call_target="tpu_custom_call" | custom-call | tf_op jit(solution)/shard_map/hand_out/pallas_call | solution.py:127

commit v6 on v5

--- a/solution.py
+++ b/solution.py
@@ -1358,19 +1358,21 @@
         gives = [pltpu.make_async_copy(*pair, t.give.at[k]) for k, pair in enumerate(zip(t.held, o.large))]
         for copy in takes:
             copy.start()
+        for take, give in zip(takes, gives):
+            take.wait()
+            give.start()
         device = lax.axis_index("wide") * plan.narrow + lax.axis_index("narrow")
         width = i.sums.shape[1]
         source = lax.broadcasted_iota(I32, (width, LANES), 0)
         lane = lax.broadcasted_iota(I32, (width, LANES), 1)
-        for row, (size, target) in enumerate(zip(counts, o.owned)):
+        found = {}
+        for size in sorted(set(counts)):
             pick = (source == device * size + lane).astype(F32)
-            found = jnp.dot(
+            found[size] = jnp.dot(
                 i.sums[...], pick, precision=lax.Precision.HIGHEST, preferred_element_type=F32
             )
-            target[...] = found[row : row + 1, :size]
-        for take, give in zip(takes, gives):
-            take.wait()
-            give.start()
+        for row, (size, target) in enumerate(zip(counts, o.owned)):
+            target[...] = found[size][row : row + 1, :size]
         for copy in gives:
             copy.wait()
 

time: 276 us -> 276 us (level)
  no operation moved by 1% of the time
where the time goes in v6:
time: 276 us
  Pallas kernels  273 us (99%)
    pallas_call x2, Pallas kernels, run(): pl.pallas_call(flat, out_shape=jax.tree.leaves(outputs), in_specs=specs(i...  273 us

profile of v6, /device:TPU:0, one launch (start us, length us, event | category | flops | bytes accessed | tf_op | source)
XLA Modules:
  0.0 275.6 jit_solution(17431517537527563095)
XLA Ops:
  1.3 1.3 pad_add_fusion.refs_12_
  2.6 267.6 %layer.1 = (bf16[512,1024]{1,0:T(8,128)(2,1)}, bf16[512,1024]{1,0:T(8,128)(2,1)}, bf16[512,1024]{1,0:T(8,128)(2,1)}, bf16[512,1024]{1,0:T(8,128)(2,1)}, bf16[2,6...) custom-call(s32[512,512]{1,0:T(8,128)} %refs_0_.1, ...), custom_call_target="tpu_custom_call" | custom-call | tf_op jit(solution)/shard_map/layer/pallas_call | solution.py:127
  270.2 5.2 %hand_out.1 = (bf16[512,1024]{1,0:T(8,128)(2,1)}, f32[512,1024]{1,0:T(8,128)}, f32[32,1024]{1,0:T(8,128)}, f32[32,1024]{1,0:T(8,128)}, f32[32,1024]{1,0:T(8,128)...) custom-call(bf16[512,1024]{1,0:T(8,128)(2,1)} %get-tuple-element.36., ...), custom_call_target="tpu_custom_call" | custom-call | tf_op jit(solution)/shard_map/hand_out/pallas_call | solution.py:127
